TPU v7x, 256 devices: a whole 4x4x8 slice. The times are simulated.
256 devices in a mesh: blk: 32 (over x_hi, z, core), head: 8 (over y, x_lo).
Axes of the slice: x: 4 (x_hi: 2, x_lo: 2; x = x_hi * 2 + x_lo), y: 4, z: 8, core: 2. Of those that a mesh axis runs over, the one named last changes fastest.
Arguments:
- query: bfloat16 [32768, 4096], P(('blk', 'head')), may hold values from -128 to 128
- key: bfloat16 [4096, 4096], P('blk', 'head'), may hold values from -8 to 8
- value: bfloat16 [4096, 4096], P('blk', 'head'), may hold values from -6 to 6
- d_out: bfloat16 [32768, 4096], P(('blk', 'head')), may hold values from -6 to 6
- seg_map: int32 [256], replicated, may hold values from 0 to 63, never falling along the last dimension, each value on 1 to 8 neighbouring positions
- spans: int32 [64, 8], replicated, may hold values from 0 to 31, all different within a row
Outputs:
- attn_out: bfloat16 [32768, 4096], P(('blk', 'head'))
- d_query: bfloat16 [32768, 4096], P(('blk', 'head'))
- d_key: bfloat16 [4096, 4096], P('blk', 'head')
- d_value: bfloat16 [4096, 4096], P('blk', 'head')
Inputs may be any that keep to these rules, and one draw needn't show every extreme that they name: `seg_map`: segment numbers never fall from one CAD block to the next; each segment covers 1 to 8 blocks, one exactly 8. `spans`: each row names 8 different document blocks; every document block is named by some row.
All inputs are finite; a program needn't handle non-finite values.
Results may differ from a plain program's by a relative error of at most 0.024.
Values may be sent and summed in bfloat16 or wider, within the bound.
No kernel may reach another device: no remote copies, remote signals or barrier semaphores. Data moves between devices by JAX's collectives and lax.ppermute only.
A program may use at most 128 MiB of HBM per device.

v0:
```python
import math

import jax
import jax.numpy as jnp
from jax import lax
from jax.sharding import PartitionSpec as P

HEADS = 32
HEAD_DIM = 128
BLOCK = 128
SPANS = 8


def head_pass(q_head, dout_head, key_head, value_head, id_groups):
    factor = 1.0 / math.sqrt(HEAD_DIM)
    group_width = q_head.shape[1]
    doc_blocks = key_head.shape[0]

    def one_group(sums, inputs):
        q_group, dout_group, group_ids = inputs
        flat_ids = group_ids.reshape(group_width * SPANS)
        key_tiles = jnp.take(key_head, flat_ids, axis=0).reshape(
            group_width, SPANS * BLOCK, HEAD_DIM
        )
        value_tiles = jnp.take(value_head, flat_ids, axis=0).reshape(
            group_width, SPANS * BLOCK, HEAD_DIM
        )
        scores = (
            jnp.einsum("cqd,ckd->cqk", q_group, key_tiles, preferred_element_type=jnp.float32)
            * factor
        )
        top_score = jnp.max(scores, axis=-1, keepdims=True)
        expo = jnp.exp(scores - top_score)
        prob = expo / jnp.sum(expo, axis=-1, keepdims=True)
        prob_b = prob.astype(jnp.bfloat16)
        attn = jnp.einsum("cqk,ckd->cqd", prob_b, value_tiles, preferred_element_type=jnp.float32)
        delta = jnp.sum(dout_group.astype(jnp.float32) * attn, axis=-1, keepdims=True)
        dprob = jnp.einsum(
            "cqd,ckd->cqk", dout_group, value_tiles, preferred_element_type=jnp.float32
        )
        dscore_b = (prob * (dprob - delta)).astype(jnp.bfloat16)
        grad_query = (
            jnp.einsum("cqk,ckd->cqd", dscore_b, key_tiles, preferred_element_type=jnp.float32)
            * factor
        ).astype(jnp.bfloat16)
        key_slots = (
            jnp.einsum("cqk,cqd->ckd", dscore_b, q_group, preferred_element_type=jnp.float32)
            * factor
        )
        value_slots = jnp.einsum(
            "cqk,cqd->ckd", prob_b, dout_group, preferred_element_type=jnp.float32
        )
        one_hot = (jnp.arange(doc_blocks, dtype=jnp.int32)[:, None] == flat_ids[None, :]).astype(
            jnp.float32
        )
        key_sums = sums[0] + jnp.dot(
            one_hot,
            key_slots.reshape(group_width * SPANS, BLOCK * HEAD_DIM),
            precision=lax.Precision.HIGHEST,
            preferred_element_type=jnp.float32,
        )
        value_sums = sums[1] + jnp.dot(
            one_hot,
            value_slots.reshape(group_width * SPANS, BLOCK * HEAD_DIM),
            precision=lax.Precision.HIGHEST,
            preferred_element_type=jnp.float32,
        )
        return ((key_sums, value_sums), (attn.astype(jnp.bfloat16), grad_query))

    zero_sums = jnp.zeros((doc_blocks, BLOCK * HEAD_DIM), jnp.float32)
    (key_sums, value_sums), (attn_head, grad_head) = lax.scan(
        one_group, (zero_sums, zero_sums), (q_head, dout_head, id_groups)
    )
    return (attn_head, grad_head, key_sums, value_sums)


def block_table(global_blocks, seg_map, spans):
    block_count = global_blocks.shape[0]
    seg_match = (
        global_blocks[:, None] == jnp.arange(seg_map.shape[0], dtype=jnp.int32)[None, :]
    ).astype(jnp.int32)
    seg_here = jnp.sum(seg_match * seg_map[None, :], axis=1)
    span_match = (seg_here[:, None] == jnp.arange(spans.shape[0], dtype=jnp.int32)[None, :]).astype(
        jnp.int32
    )
    block_ids = jnp.sum(span_match[:, :, None] * spans[None, :, :], axis=1)
    group_width = math.gcd(block_count, max(1, 512 // BLOCK))
    group_count = block_count // group_width
    return (block_ids.reshape(group_count, group_width, SPANS), group_count, group_width)


def by_heads(array, heads_count, group_count, group_width):
    block_count = group_count * group_width
    shaped = array.reshape(block_count, BLOCK, heads_count, HEAD_DIM).transpose(2, 0, 1, 3)
    return shaped.reshape(heads_count, group_count, group_width, BLOCK, HEAD_DIM)


def from_heads(array, heads_count):
    row_count = array.shape[1] * array.shape[2] * BLOCK
    shaped = array.reshape(heads_count, row_count, HEAD_DIM).transpose(1, 0, 2)
    return shaped.reshape(row_count, heads_count * HEAD_DIM)


def from_head_sums(array, heads_count):
    doc_rows = array.shape[1] // HEAD_DIM * BLOCK // BLOCK * array.shape[0] // array.shape[0]
    doc_rows = array.shape[1] * array.shape[2] // (BLOCK * HEAD_DIM) * BLOCK
    shaped = array.reshape(heads_count, doc_rows, HEAD_DIM).transpose(1, 0, 2)
    return shaped.reshape(doc_rows, heads_count * HEAD_DIM)


def body(query, key, value, d_out, seg_map, spans):
    dummy_carry = jnp.zeros((), jnp.int32)
    doc_local = key.shape[0]
    heads_local = HEADS // lax.axis_size("head")
    q_rows, dout_rows = (
        lax.all_to_all(query, "head", split_axis=1, concat_axis=0, tiled=True),
        lax.all_to_all(d_out, "head", split_axis=1, concat_axis=0, tiled=True),
    )
    block_count = q_rows.shape[0] // BLOCK
    doc_blocks = doc_local * lax.axis_size("blk") // BLOCK
    global_blocks = lax.axis_index("blk") * block_count + jnp.arange(block_count, dtype=jnp.int32)
    id_groups, group_count, group_width = block_table(global_blocks, seg_map, spans)
    q_heads = by_heads(q_rows, heads_local, group_count, group_width)
    dout_heads = by_heads(dout_rows, heads_local, group_count, group_width)
    key_all, value_all = (
        lax.all_gather(key, "blk", axis=0, tiled=True),
        lax.all_gather(value, "blk", axis=0, tiled=True),
    )

    def to_blocks(array):
        return array.reshape(doc_blocks, BLOCK, heads_local, HEAD_DIM).transpose(2, 0, 1, 3)

    def scan_head(carry, inputs):
        q_head, dout_head, key_head, value_head = inputs
        return (carry, head_pass(q_head, dout_head, key_head, value_head, id_groups))

    _, (attn_heads, grad_heads, key_parts, value_parts) = lax.scan(
        scan_head, dummy_carry, (q_heads, dout_heads, to_blocks(key_all), to_blocks(value_all))
    )
    key_total, value_total = (
        lax.psum_scatter(
            from_head_sums(key_parts, heads_local).astype(jnp.bfloat16),
            "blk",
            scatter_dimension=0,
            tiled=True,
        ).astype(jnp.float32),
        lax.psum_scatter(
            from_head_sums(value_parts, heads_local).astype(jnp.bfloat16),
            "blk",
            scatter_dimension=0,
            tiled=True,
        ).astype(jnp.float32),
    )
    attn_out, d_query = (
        lax.all_to_all(
            from_heads(attn_heads, heads_local), "head", split_axis=0, concat_axis=1, tiled=True
        ),
        lax.all_to_all(
            from_heads(grad_heads, heads_local), "head", split_axis=0, concat_axis=1, tiled=True
        ),
    )
    return (attn_out, d_query, key_total.astype(jnp.bfloat16), value_total.astype(jnp.bfloat16))


def solution(mesh):
    placed = (
        P(("blk", "head"), None),
        P("blk", "head"),
        P("blk", "head"),
        P(("blk", "head"), None),
        P(),
        P(),
    )
    return jax.shard_map(
        body,
        mesh=mesh,
        in_specs=placed,
        out_specs=(
            P(("blk", "head"), None),
            P(("blk", "head"), None),
            P("blk", "head"),
            P("blk", "head"),
        ),
        check_vma=False,
    )
```

profile of v0, /device:TPU:1, one launch (start us, length us, event | category | flops | bytes accessed | tf_op | source)
XLA Modules:
  0.0 792.2 jit_solution(7581235901659764690)
XLA Ops:
  11.0 5.9 all-to-all-start
  18.3 13.2 %all-to-all-done = bf16[128,8,512]{0,2,1:T(8,128)(2,1)S(1)} async-done(((bf16[128,8,512]{0,2,1:T(8,128)(2,1)}), bf16[128,8,512]{0,2,1:T(8,128)(2,1)S(1)}, u32[]{:S(2)}, u32[]{:S(2)}) %all-to-all-start) | async-done | bytes 1048608 | tf_op jit(solution)/shard_map/all_to_all | solution.py:116
  31.5 4.1 all-to-all-start.1
  36.2 65.8 %all-gather.3.cloned.1.call-done = bf16[4096,512]{1,0:T(8,128)(2,1)} async-done(((bf16[128,512]{1,0:T(8,128)(2,1)}), bf16[4096,512]{1,0:T(8,128)(2,1)}) %all-gather.3.cloned.1.call-update) | async-done | bytes 4194320 | tf_op jit(solution)/shard_map/all_gather | solution.py:126
  102.0 6.9 reshape.149
  108.9 5.2 copy.132
  114.1 74.2 %all-gather.5.cloned.1.call-done = bf16[4096,512]{1,0:T(8,128)(2,1)} async-done(((bf16[128,512]{1,0:T(8,128)(2,1)}), bf16[4096,512]{1,0:T(8,128)(2,1)}) %all-gather.5.cloned.1.call-update) | async-done | bytes 4194320 | tf_op jit(solution)/shard_map/all_gather | solution.py:127
  188.3 6.9 reshape.150
  195.2 5.3 copy.131
  200.5 315.4 %while.34 = (s32[]{:T(128)}, bf16[4,2,4,128,128]{4,3,2,1,0:T(8,128)(2,1)}, bf16[4,2,4,128,128]{4,3,2,1,0:T(8,128)(2,1)}, bf16[4,32,16384]{2,1,0:T(8,128)(2,1)}, ...) while((s32[]{:T(128)}, ...), condition=%wide.region_8.10_spmd, body=%wide.region_2.9_spmd.sunk | while | flops 1216745216 | bytes 96878912 | solution.py:137
  206.5 66.0 %while.35 = (s32[]{:T(128)}, f32[32,16384]{1,0:T(8,128)}, f32[32,16384]{1,0:T(8,128)}, bf16[2,4,128,128]{2,3,1,0:T(8,128)(2,1)}, bf16[2,4,128,128]{3,2,1,0:T(8,1...) while((s32[]{:T(128)}, f32[32,16384]{1,0:T(8,128)}, ...), condition=%wide.region_7.8_spmd.clone, body=%wide.region_3.7_spmd.clone.sunk | while | flops 1216745216 | bytes 63848388 | solution.py:71
  225.3 2.8 reshape.161
  228.1 4.1 convolution_add_fusion.4
  257.3 2.8 reshape.161
  260.0 4.8 convolution_add_fusion.4
  268.4 4.1 convolution_add_fusion.5
  275.4 4.0 bitcast_dynamic-update-slice_fusion.8
  285.4 66.0 %while.35 = (s32[]{:T(128)}, f32[32,16384]{1,0:T(8,128)}, f32[32,16384]{1,0:T(8,128)}, bf16[2,4,128,128]{2,3,1,0:T(8,128)(2,1)}, bf16[2,4,128,128]{3,2,1,0:T(8,1...) while((s32[]{:T(128)}, f32[32,16384]{1,0:T(8,128)}, ...), condition=%wide.region_7.8_spmd.clone, body=%wide.region_3.7_spmd.clone.sunk | while | flops 1216745216 | bytes 63848388 | solution.py:71
  304.2 2.8 reshape.161
  307.0 4.1 convolution_add_fusion.4
  336.1 2.8 reshape.161
  338.9 4.8 convolution_add_fusion.4
  347.3 4.1 convolution_add_fusion.5
  354.3 3.9 bitcast_dynamic-update-slice_fusion.8
  364.2 66.0 %while.35 = (s32[]{:T(128)}, f32[32,16384]{1,0:T(8,128)}, f32[32,16384]{1,0:T(8,128)}, bf16[2,4,128,128]{2,3,1,0:T(8,128)(2,1)}, bf16[2,4,128,128]{3,2,1,0:T(8,1...) while((s32[]{:T(128)}, f32[32,16384]{1,0:T(8,128)}, ...), condition=%wide.region_7.8_spmd.clone, body=%wide.region_3.7_spmd.clone.sunk | while | flops 1216745216 | bytes 63848388 | solution.py:71
  383.1 2.8 reshape.161
  385.8 4.1 convolution_add_fusion.4
  415.0 2.8 reshape.161
  417.7 4.8 convolution_add_fusion.4
  426.1 4.1 convolution_add_fusion.5
  433.1 3.9 bitcast_dynamic-update-slice_fusion.8
  443.0 66.0 %while.35 = (s32[]{:T(128)}, f32[32,16384]{1,0:T(8,128)}, f32[32,16384]{1,0:T(8,128)}, bf16[2,4,128,128]{2,3,1,0:T(8,128)(2,1)}, bf16[2,4,128,128]{3,2,1,0:T(8,1...) while((s32[]{:T(128)}, f32[32,16384]{1,0:T(8,128)}, ...), condition=%wide.region_7.8_spmd.clone, body=%wide.region_3.7_spmd.clone.sunk | while | flops 1216745216 | bytes 63848388 | solution.py:71
  461.9 2.8 reshape.161
  464.6 4.1 convolution_add_fusion.4
  493.8 2.8 reshape.161
  496.5 4.8 convolution_add_fusion.4
  504.9 4.1 convolution_add_fusion.5
  511.9 3.9 bitcast_dynamic-update-slice_fusion.8
  515.9 7.4 convert_element_type.58
  523.3 6.0 copy.107
  531.9 7.4 convert_element_type.54
  539.4 5.8 copy.106
  551.1 4.1 all-to-all-start.2
  557.3 13.3 %all-to-all-done.2 = bf16[8,128,512]{1,2,0:T(8,128)(2,1)S(1)} async-done(((bf16[8,128,512]{1,2,0:T(8,128)(2,1)}), bf16[8,128,512]{1,2,0:T(8,128)(2,1)S(1)}, u32[]{:S(2)}, u32[]{:S(2)}) %all-to-all-start.2) | async-done | bytes 1048608 | tf_op jit(solution)/shard_map/all_to_all | solution.py:155
  570.6 3.6 all-to-all-start.3
  575.5 17.4 %all-to-all-done.3 = bf16[8,128,512]{1,2,0:T(8,128)(2,1)S(1)} async-done(((bf16[8,128,512]{1,2,0:T(8,128)(2,1)}), bf16[8,128,512]{1,2,0:T(8,128)(2,1)S(1)}, u32[]{:S(2)}, u32[]{:S(2)}) %all-to-all-start.3) | async-done | bytes 1048608 | tf_op jit(solution)/shard_map/all_to_all | solution.py:158
  594.2 60.1 %reduce-scatter.5.cloned.1.call-done = bf16[128,512]{1,0:T(8,128)(2,1)} async-done(((bf16[4096,512]{1,0:T(8,128)(2,1)}), bf16[128,512]{1,0:T(8,128)(2,1)}) %reduce-scatter.5.cloned.1.call-update) | async-done | bytes 131088 | tf_op jit(solution)/shard_map/reduce_scatter | solution.py:147
  654.3 131.4 %reduce-scatter.3.cloned.1.call-done = bf16[128,512]{1,0:T(8,128)(2,1)} async-done(((bf16[4096,512]{1,0:T(8,128)(2,1)}), bf16[128,512]{1,0:T(8,128)(2,1)}) %reduce-scatter.3.cloned.1.call-update) | async-done | bytes 131088 | tf_op jit(solution)/shard_map/reduce_scatter | solution.py:141
  (395 shorter events, 243.5 us)
Async XLA Ops:
  7.2 94.8 %all-gather.3.cloned.1.call-start = ((), (), s32[]{:S(2)}) async-start(), calls=%async_computation.6 | async-start | bytes 4325376 | tf_op jit(solution)/shard_map/all_gather | solution.py:126
  7.9 180.4 %all-gather.5.cloned.1.call-start = ((), (), s32[]{:S(2)}) async-start(), calls=%async_computation.7 | async-start | bytes 4325376 | tf_op jit(solution)/shard_map/all_gather | solution.py:127
  8.6 8.3 %copy-start.12 = (bf16[128,4096]{1,0:T(8,128)(2,1)S(1)}, bf16[128,4096]{1,0:T(8,128)(2,1)}, u32[]{:S(2)}) copy-start(bf16[128,4096]{1,0:T(8,128)(2,1)} %param.15) | copy-start | bytes 3145732
  11.0 20.4 %all-to-all-start = ((bf16[128,8,512]{0,2,1:T(8,128)(2,1)}), bf16[128,8,512]{0,2,1:T(8,128)(2,1)S(1)}, u32[]{:S(2)}, u32[]{:S(2)}) async-start(bf16[128,8,512]{0,2,1:T(8,128)(2,1)} %bitcast.8), calls=%async_computation | async-start | bytes 2097152 | tf_op jit(solution)/shard_map/all_to_all | solution.py:116
  17.0 18.7 %copy-start.16 = (s32[256]{0:T(256)S(1)}, s32[256]{0:T(256)}, u32[]{:S(2)}) copy-start(s32[256]{0:T(256)} %param.16) | copy-start | bytes 3076
  17.0 19.0 %copy-start.15 = (s32[64,8]{0,1:T(8,128)S(1)}, s32[64,8]{0,1:T(8,128)}, u32[]{:S(2)}) copy-start(s32[64,8]{0,1:T(8,128)} %param.17) | copy-start | bytes 6148
  31.5 169.0 %all-to-all-start.1 = ((bf16[128,8,512]{0,2,1:T(8,128)(2,1)}), bf16[128,8,512]{0,2,1:T(8,128)(2,1)S(1)}, u32[]{:S(2)}, u32[]{:S(2)}) async-start(bf16[128,8,512]{0,2,1:T(8,128)(2,1)} %bitcast.13), calls=%async_computation.1 | async-start | bytes 2097152 | tf_op jit(solution)/shard_map/all_to_all | solution.py:117
  35.6 618.7 %reduce-scatter.5.cloned.1.call-start = ((), (), s32[]{:S(2)}) async-start(), calls=%async_computation.9 | async-start | bytes 4325376 | tf_op jit(solution)/shard_map/reduce_scatter | solution.py:147
  200.5 3.6 copy-start.8
  200.5 3.6 copy-start.10
  206.5 5.3 copy-start.1
  220.0 2.2 copy-start.6
  228.1 4.1 copy-start.3
  238.4 5.3 copy-start.1
  260.0 4.8 copy-start.3
  275.4 4.0 copy-start.9
  275.4 4.0 copy-start.11
  279.4 3.7 copy-start.8
  279.4 3.7 copy-start.10
  285.4 5.3 copy-start.1
  307.0 4.1 copy-start.3
  317.3 5.3 copy-start.1
  330.8 2.2 copy-start.6
  338.9 4.8 copy-start.3
  354.3 3.9 copy-start.9
  354.3 3.9 copy-start.11
  358.2 3.7 copy-start.8
  358.2 3.7 copy-start.10
  364.2 5.3 copy-start.1
  385.8 4.1 copy-start.3
  396.1 5.3 copy-start.1
  409.6 2.2 copy-start.6
  417.7 4.8 copy-start.3
  433.1 3.9 copy-start.9
  433.1 3.9 copy-start.11
  437.0 3.7 copy-start.8
  437.0 3.7 copy-start.10
  443.0 5.3 copy-start.1
  464.6 4.1 copy-start.3
  474.9 5.3 copy-start.1
  488.4 2.2 copy-start.6
  496.5 4.8 copy-start.3
  511.9 3.9 copy-start.9
  511.9 3.9 copy-start.11
  531.9 253.8 %reduce-scatter.3.cloned.1.call-start = ((), (), s32[]{:S(2)}) async-start(), calls=%async_computation.8 | async-start | bytes 4325376 | tf_op jit(solution)/shard_map/reduce_scatter | solution.py:141
  550.0 5.3 copy-start.13
  551.1 19.5 %all-to-all-start.2 = ((bf16[8,128,512]{1,2,0:T(8,128)(2,1)}), bf16[8,128,512]{1,2,0:T(8,128)(2,1)S(1)}, u32[]{:S(2)}, u32[]{:S(2)}) async-start(bf16[8,128,512]{1,2,0:T(8,128)(2,1)} %copy.103), calls=%async_computation.2 | async-start | bytes 2097152 | tf_op jit(solution)/shard_map/all_to_all | solution.py:155
  570.6 22.3 %all-to-all-start.3 = ((bf16[8,128,512]{1,2,0:T(8,128)(2,1)}), bf16[8,128,512]{1,2,0:T(8,128)(2,1)S(1)}, u32[]{:S(2)}, u32[]{:S(2)}) async-start(bf16[8,128,512]{1,2,0:T(8,128)(2,1)} %copy.105), calls=%async_computation.3 | async-start | bytes 2097152 | tf_op jit(solution)/shard_map/all_to_all | solution.py:158
  (45 other events, 63.2 us)
Sparse Core Ops, SparseCore 0:
  10.8 91.1 all-gather.2
  104.8 83.4 all-gather.4
  532.0 122.2 reduce-scatter.4
  659.5 126.0 reduce-scatter.2
where the time goes:
time: 800 us; the launch traced here: 792 us
  waiting for transfers between devices  377 us (47%)
  local copies, waits for them, and re-layouts  207 us (26%)
  matrix products  140 us (18%)
  other arithmetic  34.7 us (4%)
  starting transfers between devices  17.9 us (2%)
  between operations  13.9 us (2%)
    reduce_scatter x1, waiting for transfers between devices, body(): lax.psum_scatter(from_head_sums(key_parts, heads_local).astype(jnp.bfloat...  131 us
    all_gather x1, waiting for transfers between devices, body(): lax.all_gather(value, 'blk', axis=0, tiled=True)  74.2 us
    all_gather x1, waiting for transfers between devices, body(): lax.all_gather(key, 'blk', axis=0, tiled=True)  65.8 us
    reduce_scatter x1, waiting for transfers between devices, body(): lax.psum_scatter(from_head_sums(value_parts, heads_local).astype(jnp.bflo...  60.1 us
    dot_general x8, matrix products, one_group(): jnp.dot(one_hot, key_slots.reshape(group_width * SPANS, BLOCK * HEAD_DIM)...  35.5 us
    dynamic_update_slice x12, local copies, waits for them, and re-layouts, body(): lax.scan(scan_head, dummy_carry, (q_heads, dout_heads, to_blocks(key_all)...  27.2 us
    dot_general x8, matrix products, one_group(): jnp.dot(one_hot, value_slots.reshape(group_width * SPANS, BLOCK * HEAD_DI...  26.5 us
    reshape x8, local copies, waits for them, and re-layouts, one_group(): key_slots.reshape(group_width * SPANS, BLOCK * HEAD_DIM)  22 us
  transfers between devices with their start and end apart: 8, of which 7 were waited for; matrix products, arithmetic and copies ran while one was open for 6% of the time, Pallas kernels for 0%

commit v1 on v0

v1 whole, which is shorter than its diff:
```python
import functools
import math

import jax
import jax.numpy as jnp
from jax import lax
from jax.experimental import pallas as pl
from jax.experimental.pallas import tpu as pltpu
from jax.sharding import Mesh, PartitionSpec as P

HEAD_DIM = 128
BLOCK = 128
SPANS = 8
PLANE = ("head", "xhi", "core")
FACTOR = 1.0 / math.sqrt(HEAD_DIM)
LOG2E = math.log2(math.e)
UNROLL = 2


def nt(a, b):
    return lax.dot_general(a, b, (((1,), (1,)), ((), ())), preferred_element_type=jnp.float32)


def nn(a, b):
    return lax.dot_general(a, b, (((1,), (0,)), ((), ())), preferred_element_type=jnp.float32)


def attention_kernel(
    zi_ref, seg_ref, spans_ref, q_ref, do_ref, kv_ref, o_ref, dq_ref, dkv_ref, kvt_ref, acc_ref
):
    z = zi_ref[0]
    doc_blocks = kv_ref.shape[0]
    cad_blocks = q_ref.shape[0]

    @pl.loop(0, doc_blocks)
    def _(d):
        tile = kv_ref[d]
        kvt_ref[d, :HEAD_DIM, :] = tile[:, :HEAD_DIM].T
        kvt_ref[d, HEAD_DIM:, :] = tile[:, HEAD_DIM:].T
        acc_ref[d] = jnp.zeros(acc_ref.shape[1:], jnp.float32)

    zero = jnp.zeros((BLOCK, HEAD_DIM), jnp.bfloat16)

    def one_block(s):
        head, xhi, core = s // 4, (s // 2) % 2, s % 2
        seg = seg_ref[(xhi * 16 + z * 2 + core) * 8 + head]
        locs = []
        for j in range(SPANS):
            d = spans_ref[j, seg]
            locs.append(((d // 2) % 8) * 4 + (d // 16) * 2 + d % 2)
        q, do = q_ref[s], do_ref[s]
        diag = jnp.concatenate(
            [jnp.concatenate([q, zero], axis=1), jnp.concatenate([zero, do], axis=1)], axis=0
        )
        kv = jnp.concatenate([kv_ref[loc] for loc in locs], axis=0)
        both = nt(kv, diag)
        scores, dprob = both[:, :BLOCK], both[:, BLOCK:]
        top = jnp.max(scores, axis=0, keepdims=True)
        expo = jnp.exp2((scores - top) * (FACTOR * LOG2E))
        prob = expo * (1.0 / jnp.sum(expo, axis=0, keepdims=True))
        prob_b = prob.astype(jnp.bfloat16)
        value_t = jnp.concatenate([kvt_ref[loc, HEAD_DIM:, :] for loc in locs], axis=1)
        attn_t = nn(value_t, prob_b)
        attn = attn_t.T
        o_ref[s] = attn.astype(jnp.bfloat16)
        delta = jnp.sum(do.astype(jnp.float32).T * attn_t, axis=0, keepdims=True)
        dscore_b = (prob * (dprob - delta)).astype(jnp.bfloat16)
        key_t = jnp.concatenate([kvt_ref[loc, :HEAD_DIM, :] for loc in locs], axis=1)
        dq_t = nn(key_t, dscore_b) * FACTOR
        dq_ref[s] = dq_t.T.astype(jnp.bfloat16)
        slots = nn(jnp.concatenate([dscore_b, prob_b], axis=1), diag)
        for j in range(SPANS):
            acc_ref[locs[j]] += slots[j * BLOCK : (j + 1) * BLOCK]

    @pl.loop(0, cad_blocks // UNROLL)
    def _(i):
        for u in range(UNROLL):
            one_block(i * UNROLL + u)

    @pl.loop(0, doc_blocks)
    def _(d):
        dkv_ref[d, :, :HEAD_DIM] = (acc_ref[d, :, :HEAD_DIM] * FACTOR).astype(jnp.bfloat16)
        dkv_ref[d, :, HEAD_DIM:] = acc_ref[d, :, HEAD_DIM:].astype(jnp.bfloat16)


def attention(zi, seg_map, spans_t, q, do, kv):
    cad_blocks, doc_blocks = q.shape[0], kv.shape[0]
    smem = pl.BlockSpec(memory_space=pltpu.SMEM)
    vmem = pl.BlockSpec(memory_space=pltpu.VMEM)
    return pl.pallas_call(
        attention_kernel,
        out_shape=(
            jax.ShapeDtypeStruct(q.shape, jnp.bfloat16),
            jax.ShapeDtypeStruct(q.shape, jnp.bfloat16),
            jax.ShapeDtypeStruct(kv.shape, jnp.bfloat16),
        ),
        in_specs=[smem, smem, smem, vmem, vmem, vmem],
        out_specs=(vmem, vmem, vmem),
        scratch_shapes=[
            pltpu.VMEM((doc_blocks, 2 * HEAD_DIM, BLOCK), jnp.bfloat16),
            pltpu.VMEM((doc_blocks, BLOCK, 2 * HEAD_DIM), jnp.float32),
        ],
        compiler_params=pltpu.CompilerParams(vmem_limit_bytes=48 * 2**20),
        cost_estimate=pl.CostEstimate(
            flops=cad_blocks * SPANS * 12 * BLOCK * BLOCK * HEAD_DIM,
            bytes_accessed=2 * (4 * q.size + 2 * kv.size),
            transcendentals=cad_blocks * SPANS * BLOCK * BLOCK,
        ),
        name="attention",
    )(zi, seg_map, spans_t, q, do, kv)


def swap(array, axes):
    return lax.all_to_all(array, axes, split_axis=0, concat_axis=0, tiled=True)


def body(query, key, value, d_out, seg_map, spans):
    rows = query.shape[0]

    def by_head(array):
        return array.reshape(rows, -1, HEAD_DIM).transpose(1, 0, 2)

    kv = swap(jnp.concatenate([by_head(key), by_head(value)], axis=2), ("xhi", "core"))
    kv = lax.all_gather(kv, "z", axis=0, tiled=True)
    q = swap(by_head(query), PLANE)
    do = swap(by_head(d_out), PLANE)
    zi = lax.axis_index("z").astype(jnp.int32).reshape(1)
    o, dq, dkv = attention(zi, seg_map, spans.T, q, do, kv)
    dkv = lax.psum_scatter(dkv, "z", scatter_dimension=0, tiled=True)
    o, dq = swap(o, PLANE), swap(dq, PLANE)
    dkv = swap(dkv, ("xhi", "core"))

    def by_rows(array):
        return array.transpose(1, 0, 2).reshape(rows, -1)

    return (
        by_rows(o),
        by_rows(dq),
        by_rows(dkv[:, :, :HEAD_DIM]),
        by_rows(dkv[:, :, HEAD_DIM:]),
    )


def solution(mesh):
    fine = Mesh(mesh.devices.reshape(2, 8, 2, 8), ("xhi", "z", "core", "head"))
    blk = ("xhi", "z", "core")
    rows, tiles = P((*blk, "head"), None), P(blk, "head")
    return jax.shard_map(
        body,
        mesh=fine,
        in_specs=(rows, tiles, tiles, rows, P(), P()),
        out_specs=(rows, rows, tiles, tiles),
        check_vma=False,
    )
```

time: 800 us -> 179 us (0.22)
  waiting for transfers between devices: 377 us -> 34.7 us
  local copies, waits for them, and re-layouts: 207 us -> 14.9 us
  matrix products: 140 us -> 0 us
  blocking collectives: 0 us -> 53.9 us
  Pallas kernels: 0 us -> 46.9 us
  other arithmetic: 34.7 us -> 0.02 us
    reduce_scatter x2 -> x1, waiting for transfers between devices: 191 us -> 0.01 us  [body(): dkv = lax.psum_scatter(dkv, 'z', scatter_dimension=0, tiled=True)]
    all_gather x2 -> x1, waiting for transfers between devices: 140 us -> 0.01 us  [body(): kv = lax.all_gather(kv, 'z', axis=0, tiled=True)]
    dot_general x56 -> x0, matrix products: 124 us -> none  [the longest x8 35.5 us: one_group(): jnp.dot(one_hot, key_slots.reshape(group_width * SPANS, BLOCK * HEAD_DIM)...]
    all_to_all x0 -> x3, blocking collectives: none -> 53.9 us  [swap(): return lax.all_to_all(array, axes, split_axis=0, concat_axis=0, tiled=True)]
    reshape x19 -> x2, local copies, waits for them, and re-layouts: 50.3 us -> 2.63 us  [by_head(): return array.reshape(rows, -1, HEAD_DIM).transpose(1, 0, 2)]
    pallas_call x0 -> x1, Pallas kernels: none -> 46.9 us  [attention(): pl.pallas_call(attention_kernel, out_shape=(jax.ShapeDtypeStruct(q.shape,...]
    gather x16 -> x0, local copies, waits for them, and re-layouts: 31.6 us -> none  [the longest x8 15.8 us: one_group(): jnp.take(key_head, flat_ids, axis=0)]
    dynamic_update_slice x12 -> x0, local copies, waits for them, and re-layouts: 27.2 us -> none  [body(): lax.scan(scan_head, dummy_carry, (q_heads, dout_heads, to_blocks(key_all)...]
  transfers between devices with their start and end apart: 8 -> 5, of which waited for: 7 -> 3; matrix products, arithmetic and copies ran while one was open for 6% -> 4% of each run, Pallas kernels for 0% -> 0%
where the time goes in v1:
time: 179 us; the launch traced here: 178 us
  blocking collectives  53.9 us (30%)
  Pallas kernels  46.9 us (26%)
  waiting for transfers between devices  34.7 us (19%)
  local copies, waits for them, and re-layouts  14.9 us (8%)
  between operations  14.2 us (8%)
  starting transfers between devices  13.4 us (7%)
    all_to_all x3, blocking collectives, swap(): return lax.all_to_all(array, axes, split_axis=0, concat_axis=0, tiled=True)  53.9 us
    pallas_call x1, Pallas kernels, attention(): pl.pallas_call(attention_kernel, out_shape=(jax.ShapeDtypeStruct(q.shape,...  46.9 us
    all_to_all x3, waiting for transfers between devices, swap(): return lax.all_to_all(array, axes, split_axis=0, concat_axis=0, tiled=True)  34.7 us
    all_to_all x3, starting transfers between devices, swap(): return lax.all_to_all(array, axes, split_axis=0, concat_axis=0, tiled=True)  13.4 us
    unnamed x20, local copies, waits for them, and re-layouts  9.81 us
  transfers between devices with their start and end apart: 5, of which 3 were waited for; matrix products, arithmetic and copies ran while one was open for 4% of the time, Pallas kernels for 0%

profile of v1, /device:TPU:1, one launch (start us, length us, event | category | flops | bytes accessed | tf_op | source)
XLA Modules:
  0.0 178.1 jit_solution(903597923574047107)
XLA Ops:
  7.2 0.0 copy-start.4
  7.2 0.0 all-gather.2.cloned.1.call-start
  7.2 1.1 copy.30
  8.3 1.0 copy.31
  9.4 12.1 %all_to_all.30 = bf16[4,128,256]{1,2,0:T(8,128)(2,1)S(1)} all-to-all(bf16[4,128,256]{1,2,0:T(8,128)(2,1)S(1)} %pad_maximum_fusion), channel_id=1, replica_groups=mesh['xhi'=2,'z'=8,'core'=2,'head'=8] {'xhi','core'}, dimensions={0} | all-to-all | bytes 524288 | tf_op jit(solution)/shard_map/all_to_all | solution.py:114
  21.5 0.9 copy.32
  22.4 0.0 all-gather.2.cloned.1.call-update
  22.4 0.0 copy-done.4
  22.4 0.7 copy.26
  23.1 0.0 copy-start.5
  23.1 1.3 copy.27
  24.4 5.7 %all-to-all-start = ((bf16[32,128,128]{2,1,0:T(8,128)(2,1)}), bf16[32,128,128]{2,1,0:T(8,128)(2,1)S(1)}, u32[]{:S(2)}, u32[]{:S(2)}) async-start(bf16[32,128,128]{2,1,0:T(8,128)(2,1)} %bitcast.3), calls=%async_computation | async-start | bytes 2097152 | tf_op jit(solution)/shard_map/all_to_all | solution.py:114
  30.1 0.0 copy-done.5
  30.1 0.7 copy.28
  30.7 0.0 copy-start.2
  30.8 0.0 copy-start.3
  30.8 1.3 copy.29
  32.1 15.1 %all-to-all-done.q_ref = bf16[32,128,128]{2,1,0:T(8,128)(2,1)S(1)} async-done(((bf16[32,128,128]{2,1,0:T(8,128)(2,1)}), bf16[32,128,128]{2,1,0:T(8,128)(2,1)S(1)}, u32[]{:S(2)}, u32[]{:S(2)}) %all-to-all-start) | async-done | bytes 1048608 | tf_op jit(solution)/shard_map/all_to_all | solution.py:114
  47.1 4.3 %all-to-all-start.1 = ((bf16[32,128,128]{2,1,0:T(8,128)(2,1)}), bf16[32,128,128]{2,1,0:T(8,128)(2,1)S(1)}, u32[]{:S(2)}, u32[]{:S(2)}) async-start(bf16[32,128,128]{2,1,0:T(8,128)(2,1)} %bitcast.5), calls=%async_computation.1 | async-start | bytes 2097152 | tf_op jit(solution)/shard_map/all_to_all | solution.py:114
  51.5 0.0 reduce-scatter.2.cloned.1.call-start
  51.5 17.0 %all-to-all-done.1.do_ref = bf16[32,128,128]{2,1,0:T(8,128)(2,1)S(1)} async-done(((bf16[32,128,128]{2,1,0:T(8,128)(2,1)}), bf16[32,128,128]{2,1,0:T(8,128)(2,1)S(1)}, u32[]{:S(2)}, u32[]{:S(2)}) %all-to-all-start.1) | async-done | bytes 1048608 | tf_op jit(solution)/shard_map/all_to_all | solution.py:114
  68.5 0.0 all-gather.2.cloned.1.call-done.kv_ref
  68.5 0.0 copy-done.2
  68.5 0.0 copy-done.3
  68.5 46.9 %attention.1 = (bf16[32,128,128]{2,1,0:T(8,128)(2,1)S(1)}, bf16[32,128,128]{2,1,0:T(8,128)(2,1)S(1)}, bf16[32,128,256]{2,1,0:T(8,128)(2,1)}) custom-call(s32[1]{0:T(128)} %bitcast.zi_ref, s32[256]{0:T(256)S(1)} %copy-done.3, s32[8,64]{1,0:T(8,128)S(1)} %bitcast.22, bf16[32,128,128]{2,1,0:T(8,128)(2,1)S(1)} %all-to-all-done.q_ref, ...), custom_call_target="tpu_custom_call" | custom-call | flops 6442450944 | bytes 8388608 | tf_op jit(solution)/shard_map/attention/pallas_call | solution.py:90
  115.5 0.0 copy-start
  115.5 1.0 copy-done
  116.4 0.0 copy-start.1
  116.4 0.0 reduce-scatter.2.cloned.1.call-update
  116.5 1.2 copy-done.1
  117.7 20.8 %all_to_all.31 = bf16[32,128,128]{2,1,0:T(8,128)(2,1)S(1)} all-to-all(bf16[32,128,128]{2,1,0:T(8,128)(2,1)S(1)} %copy-done.1), channel_id=1, replica_groups=mesh['xhi'=2,'z'=8,'core'=2,'head'=8] {'head','xhi','core'}, dimensions={0} | all-to-all | bytes 2097152 | tf_op jit(solution)/shard_map/all_to_all | solution.py:114
  138.4 21.0 %all_to_all.32 = bf16[32,128,128]{2,1,0:T(8,128)(2,1)S(1)} all-to-all(bf16[32,128,128]{2,1,0:T(8,128)(2,1)S(1)} %get-tuple-element.8), channel_id=1, replica_groups=mesh['xhi'=2,'z'=8,'core'=2,'head'=8] {'head','xhi','core'}, dimensions={0} | all-to-all | bytes 2097152 | tf_op jit(solution)/shard_map/all_to_all | solution.py:114
  159.4 0.0 reduce-scatter.2.cloned.1.call-done
  159.4 3.4 %all-to-all-start.5 = ((bf16[4,128,256]{2,1,0:T(8,128)(2,1)}), bf16[4,128,256]{2,1,0:T(8,128)(2,1)S(1)}, u32[]{:S(2)}, u32[]{:S(2)}) async-start(bf16[4,128,256]{2,1,0:T(8,128)(2,1)} %reduce-scatter.2.cloned.1.call-done), calls=%async_computation.6 | async-start | bytes 524288 | tf_op jit(solution)/shard_map/all_to_all | solution.py:114
  162.8 0.7 copy.33
  163.5 1.3 copy.37
  164.8 0.7 copy.34
  165.5 1.3 copy.38
  166.8 2.6 %all-to-all-done.5 = bf16[4,128,256]{2,1,0:T(8,128)(2,1)S(1)} async-done(((bf16[4,128,256]{2,1,0:T(8,128)(2,1)}), bf16[4,128,256]{2,1,0:T(8,128)(2,1)S(1)}, u32[]{:S(2)}, u32[]{:S(2)}) %all-to-all-start.5) | async-done | bytes 262176 | tf_op jit(solution)/shard_map/all_to_all | solution.py:114
  169.4 0.1 copy.36
  169.5 0.8 copy.40
  170.3 0.1 copy.35
  170.5 0.8 copy.39
  (2 shorter events, 0.1 us)
Async XLA Ops:
  7.2 15.2 %copy-start.4 = (bf16[128,4096]{1,0:T(8,128)(2,1)S(1)}, bf16[128,4096]{1,0:T(8,128)(2,1)}, u32[]{:S(2)}) copy-start(bf16[128,4096]{1,0:T(8,128)(2,1)} %param.6) | copy-start | bytes 3145732
  7.2 61.4 %all-gather.2.cloned.1.call-start = ((), (), s32[]{:S(2)}) async-start(), calls=%async_computation.7 | async-start | bytes 2359296 | tf_op jit(solution)/shard_map/all_gather | solution.py:124
  23.1 7.0 %copy-start.5 = (bf16[128,4096]{1,0:T(8,128)(2,1)S(1)}, bf16[128,4096]{1,0:T(8,128)(2,1)}, u32[]{:S(2)}) copy-start(bf16[128,4096]{1,0:T(8,128)(2,1)} %param.9) | copy-start | bytes 3145732
  24.4 22.7 %all-to-all-start = ((bf16[32,128,128]{2,1,0:T(8,128)(2,1)}), bf16[32,128,128]{2,1,0:T(8,128)(2,1)S(1)}, u32[]{:S(2)}, u32[]{:S(2)}) async-start(bf16[32,128,128]{2,1,0:T(8,128)(2,1)} %bitcast.3), calls=%async_computation | async-start | bytes 2097152 | tf_op jit(solution)/shard_map/all_to_all | solution.py:114
  30.7 37.8 %copy-start.2 = (s32[64,8]{0,1:T(8,128)S(1)}, s32[64,8]{0,1:T(8,128)}, u32[]{:S(2)}) copy-start(s32[64,8]{0,1:T(8,128)} %param.11) | copy-start | bytes 6148
  30.8 37.8 %copy-start.3 = (s32[256]{0:T(256)S(1)}, s32[256]{0:T(256)}, u32[]{:S(2)}) copy-start(s32[256]{0:T(256)} %seg_ref.1) | copy-start | bytes 3076
  47.1 21.4 %all-to-all-start.1 = ((bf16[32,128,128]{2,1,0:T(8,128)(2,1)}), bf16[32,128,128]{2,1,0:T(8,128)(2,1)S(1)}, u32[]{:S(2)}, u32[]{:S(2)}) async-start(bf16[32,128,128]{2,1,0:T(8,128)(2,1)} %bitcast.5), calls=%async_computation.1 | async-start | bytes 2097152 | tf_op jit(solution)/shard_map/all_to_all | solution.py:114
  51.5 108.0 %reduce-scatter.2.cloned.1.call-start = ((), (), s32[]{:S(2)}) async-start(), calls=%async_computation.8 | async-start | bytes 2359296 | tf_op jit(solution)/shard_map/reduce_scatter | solution.py:129
  115.5 1.0 copy-start
  116.4 1.2 copy-start.1
  159.4 9.9 %all-to-all-start.5 = ((bf16[4,128,256]{2,1,0:T(8,128)(2,1)}), bf16[4,128,256]{2,1,0:T(8,128)(2,1)S(1)}, u32[]{:S(2)}, u32[]{:S(2)}) async-start(bf16[4,128,256]{2,1,0:T(8,128)(2,1)} %reduce-scatter.2.cloned.1.call-done), calls=%async_computation.6 | async-start | bytes 524288 | tf_op jit(solution)/shard_map/all_to_all | solution.py:114
Sparse Core Ops, SparseCore 0:
  22.5 38.2 all-gather.1
  116.6 36.9 reduce-scatter.1

commit v2 on v1

v2 whole, which is shorter than its diff:
```python
import math

import jax
import jax.numpy as jnp
from jax import lax
from jax.experimental import pallas as pl
from jax.experimental.pallas import tpu as pltpu
from jax.sharding import Mesh, PartitionSpec as P

HEAD_DIM = 128
BLOCK = 128
SPANS = 8
PLANES = 8
PLANE = ("head", "xhi", "core")
QUAD = ("xhi", "core")
FACTOR = 1.0 / math.sqrt(HEAD_DIM)
LOG2E = math.log2(math.e)
UNROLL = 4
VMEM_MIB = 8
BIG_MIB = 60
WIDE = 2 * HEAD_DIM
BF16, F32 = jnp.bfloat16, jnp.float32
SMEM = pl.BlockSpec(memory_space=pltpu.SMEM)
VMEM = pl.BlockSpec(memory_space=pltpu.VMEM)


def nt(a, b):
    return lax.dot_general(a, b, (((1,), (1,)), ((), ())), preferred_element_type=F32)


def nn(a, b):
    return lax.dot_general(a, b, (((1,), (0,)), ((), ())), preferred_element_type=F32)


def columns(block):
    return pl.ds(pl.multiple_of(block * HEAD_DIM, HEAD_DIM), HEAD_DIM)


def call(kernel, name, in_specs, shapes, scratch=(), **params):
    return pl.pallas_call(
        kernel,
        out_shape=tuple(jax.ShapeDtypeStruct(shape, BF16) for shape in shapes),
        in_specs=in_specs,
        out_specs=tuple(VMEM for _ in shapes),
        scratch_shapes=scratch,
        name=name,
        compiler_params=pltpu.CompilerParams(vmem_limit_bytes=(BIG_MIB if name == 'attention' else VMEM_MIB) * 2**20),
        **params,
    )


def split_kv(me, key, value):
    def kernel(me_ref, key_ref, value_ref, *tiles):
        for t, tile in enumerate(tiles):
            tile[:, :HEAD_DIM] = key_ref[:, columns(me_ref[0] ^ t)]
            tile[:, HEAD_DIM:] = value_ref[:, columns(me_ref[0] ^ t)]

    return call(kernel, "split_kv", [SMEM, VMEM, VMEM], [(BLOCK, WIDE)] * 4)(me, key, value)


def join_kv(me, tiles):
    def kernel(me_ref, *refs):
        *tiles, key_ref, value_ref = refs
        for t, tile in enumerate(tiles):
            key_ref[:, columns(me_ref[0] ^ t)] = tile[:, :HEAD_DIM]
            value_ref[:, columns(me_ref[0] ^ t)] = tile[:, HEAD_DIM:]

    return call(kernel, "join_kv", [SMEM] + [VMEM] * 4, [(BLOCK, 4 * HEAD_DIM)] * 2)(me, *tiles)


def split_heads(query, d_out):
    heads = query.shape[1] // HEAD_DIM

    def kernel(query_ref, d_out_ref, tiles):
        for h in range(heads):
            tiles[h, :, :HEAD_DIM] = query_ref[:, columns(h)]
            tiles[h, :, HEAD_DIM:] = d_out_ref[:, columns(h)]

    return call(kernel, "split_heads", [VMEM] * 2, [(heads, BLOCK, WIDE)])(query, d_out)[0]


def join_heads(tiles):
    heads = tiles.shape[0]

    def kernel(tiles, attn_ref, grad_ref):
        for h in range(heads):
            attn_ref[:, columns(h)] = tiles[h, :, :HEAD_DIM]
            grad_ref[:, columns(h)] = tiles[h, :, HEAD_DIM:]

    return call(kernel, "join_heads", [VMEM], [(BLOCK, heads * HEAD_DIM)] * 2)(tiles)


def plus(*terms):
    return sum(term.astype(F32) for term in terms).astype(BF16)


def attention_kernel(me_ref, seg_ref, spans_ref, qd_ref, *refs):
    pieces, (od_ref, *parts), (kv_ref, kvt_ref, acc_ref) = refs[:9], refs[9:19], refs[19:]
    quad, z = me_ref[0], me_ref[1]
    cad_blocks = qd_ref.shape[0]

    def places(first):
        own, up1, down1, up2, down2, up3, down3, up4, down4 = first
        return (
            (own, 0), (down1, 1), (down2, 2), (down3, 3), (up3, 5), (up2, 6), (up1, 7)
        ), (up4, down4)

    whole, halves = places(pieces)
    for piece, at in (*((p, 4 * o) for p, o in whole), (halves[0], 16), (halves[1], 18)):

        @pl.loop(0, piece.shape[0])
        def _(t):
            tile = piece[t]
            kv_ref[at + t] = tile
            kvt_ref[at + t, :HEAD_DIM, :] = tile[:, :HEAD_DIM].T
            kvt_ref[at + t, HEAD_DIM:, :] = tile[:, HEAD_DIM:].T
            acc_ref[at + t] = jnp.zeros((BLOCK, WIDE), F32)

    def one_block(s):
        head, xhi, core = s // 4, (s // 2) % 2, s % 2
        seg = seg_ref[(xhi * 16 + z * 2 + core) * 8 + head]
        locs = []
        for j in range(SPANS):
            d = spans_ref[j, seg]
            away = ((d // 2) % 8 - z) & 7
            locs.append(away * 4 + (((d // 16) * 2 + d % 2) ^ quad))
        q, do = qd_ref[s, :, :HEAD_DIM], qd_ref[s, :, HEAD_DIM:]
        keys = jnp.concatenate([kv_ref[loc, :, :HEAD_DIM] for loc in locs], axis=0)
        scores = nt(keys, q)
        top = jnp.max(scores, axis=0, keepdims=True)
        expo = jnp.exp2((scores - top) * (FACTOR * LOG2E))
        prob = expo * (1.0 / jnp.sum(expo, axis=0, keepdims=True))
        prob_b = prob.astype(BF16)
        value_t = jnp.concatenate([kvt_ref[loc, HEAD_DIM:, :] for loc in locs], axis=1)
        attn_t = nn(value_t, prob_b)
        od_ref[s, :, :HEAD_DIM] = attn_t.T.astype(BF16)
        values = jnp.concatenate([kv_ref[loc, :, HEAD_DIM:] for loc in locs], axis=0)
        dprob = nt(values, do)
        delta = jnp.sum(do.astype(F32).T * attn_t, axis=0, keepdims=True)
        dscore_b = (prob * (dprob - delta)).astype(BF16)
        key_t = jnp.concatenate([kvt_ref[loc, :HEAD_DIM, :] for loc in locs], axis=1)
        dq_t = nn(key_t, dscore_b) * FACTOR
        od_ref[s, :, HEAD_DIM:] = dq_t.T.astype(BF16)
        key_slots, value_slots = nn(dscore_b, q), nn(prob_b, do)
        for j in range(SPANS):
            rows = slice(j * BLOCK, (j + 1) * BLOCK)
            acc_ref[locs[j], :, :HEAD_DIM] += key_slots[rows]
            acc_ref[locs[j], :, HEAD_DIM:] += value_slots[rows]

    @pl.loop(0, cad_blocks // UNROLL)
    def _(i):
        for u in range(UNROLL):
            one_block(i * UNROLL + u)

    own, up1, up2, up3, up4, down1, down2, down3, down4 = parts
    for part, at in (
        (own, 0), (up1, 4), (up2, 8), (up3, 12), (up4, 16),
        (down4, 18), (down3, 20), (down2, 24), (down1, 28),
    ):

        @pl.loop(0, part.shape[0])
        def _(t):
            part[t, :, :HEAD_DIM] = (acc_ref[at + t, :, :HEAD_DIM] * FACTOR).astype(BF16)
            part[t, :, HEAD_DIM:] = acc_ref[at + t, :, HEAD_DIM:].astype(BF16)


def attention(me, seg_map, spans_t, qd, pieces):
    cad_blocks, doc_blocks = qd.shape[0], 4 * PLANES
    whole, half = (4, BLOCK, WIDE), (2, BLOCK, WIDE)
    return call(
        attention_kernel,
        "attention",
        [SMEM] * 3 + [VMEM] * 10,
        [qd.shape] + ([whole] * 4 + [half] + [whole] * 3 + [half]),
        [
            pltpu.VMEM((doc_blocks, BLOCK, WIDE), BF16),
            pltpu.VMEM((doc_blocks, WIDE, BLOCK), BF16),
            pltpu.VMEM((doc_blocks, BLOCK, WIDE), F32),
        ],
        cost_estimate=pl.CostEstimate(
            flops=cad_blocks * SPANS * 12 * BLOCK * BLOCK * HEAD_DIM,
            bytes_accessed=2 * (2 * qd.size + 2 * doc_blocks * BLOCK * WIDE),
            transcendentals=cad_blocks * SPANS * BLOCK * BLOCK,
        ),
    )(me, seg_map, spans_t, qd, *pieces)


def up(array):
    return lax.ppermute(array, "z", [(i, (i + 1) % PLANES) for i in range(PLANES)])


def down(array):
    return lax.ppermute(array, "z", [(i, (i - 1) % PLANES) for i in range(PLANES)])


def exchange(tiles):
    return [tiles[0]] + [
        lax.ppermute(tiles[t], QUAD, [(i, i ^ t) for i in range(4)]) for t in (1, 2, 3)
    ]


def gather_z(own):
    up1, down1 = up(own), down(own)
    up2, down2 = up(up1), down(down1)
    up3, down3 = up(up2), down(down2)
    up4, down4 = up(up3[:2]), down(down3[2:])
    return own, up1, down1, up2, down2, up3, down3, up4, down4


def scatter_z(parts, beside):
    own, up1, up2, up3, up4, down1, down2, down3, down4 = parts
    ups, downs = up(up4), down(down4)
    beside, ups, downs = lax.optimization_barrier((beside, ups, downs))
    beside = swap(beside)
    ups = up(jnp.concatenate([plus(up3[:2], ups), up3[2:]]))
    downs = down(jnp.concatenate([down3[:2], plus(down3[2:], downs)]))
    ups, downs = up(plus(up2, ups)), down(plus(down2, downs))
    ups, downs = up(plus(up1, ups)), down(plus(down1, downs))
    beside, ups, downs = lax.optimization_barrier((beside, ups, downs))
    return [plus(own[t], ups[t], downs[t]) for t in range(4)], beside


def swap(array):
    return lax.all_to_all(array, PLANE, split_axis=0, concat_axis=0, tiled=True)


def body(query, key, value, d_out, seg_map, spans):
    me = jnp.stack([lax.axis_index(QUAD), lax.axis_index("z")]).astype(jnp.int32)
    tiles = exchange(split_kv(me, key, value))
    qd, tiles = lax.optimization_barrier((split_heads(query, d_out), tiles))
    qd, pieces = swap(qd), gather_z(jnp.stack(tiles))
    od, *parts = attention(me, seg_map, spans.T, qd, pieces)
    tiles, od = scatter_z(parts, od)
    attn_out, d_query = join_heads(od)
    d_key, d_value = join_kv(me, exchange(tiles))
    return attn_out, d_query, d_key, d_value


def solution(mesh):
    fine = Mesh(mesh.devices.reshape(2, PLANES, 2, 8), ("xhi", "z", "core", "head"))
    blk = ("xhi", "z", "core")
    rows, tiles = P((*blk, "head"), None), P(blk, "head")
    return jax.shard_map(
        body,
        mesh=fine,
        in_specs=(rows, tiles, tiles, rows, P(), P()),
        out_specs=(rows, rows, tiles, tiles),
        check_vma=False,
    )
```

time: 179 us -> 148 us (0.83)
  blocking collectives: 53.9 us -> 0 us
  starting transfers between devices: 13.4 us -> 55.8 us
  between operations: 14.2 us -> 0.99 us
  local copies, waits for them, and re-layouts: 14.9 us -> 6.31 us
  waiting for transfers between devices: 34.7 us -> 41.2 us
  Pallas kernels: 46.9 us -> 42.9 us
    all_to_all x3 -> x0, blocking collectives: 53.9 us -> none  [swap(): return lax.all_to_all(array, axes, split_axis=0, concat_axis=0, tiled=True)]
    ppermute x0 -> x22, waiting for transfers between devices: none -> 38.6 us  [the longest x8 21.8 us: up(): lax.ppermute(array, 'z', [(i, (i + 1) % PLANES) for i in range(PLANES)])]
    ppermute x0 -> x22, starting transfers between devices: none -> 38 us  [the longest x8 27.1 us: down(): lax.ppermute(array, 'z', [(i, (i - 1) % PLANES) for i in range(PLANES)])]
    all_to_all x3 -> x2, waiting for transfers between devices: 34.7 us -> 2.6 us  [swap(): return lax.all_to_all(array, PLANE, split_axis=0, concat_axis=0, tiled=True)]
    all_to_all x3 -> x2, starting transfers between devices: 13.4 us -> 17.9 us  [swap(): return lax.all_to_all(array, PLANE, split_axis=0, concat_axis=0, tiled=True)]
    pallas_call x1 -> x5, Pallas kernels: 46.9 us -> 42.9 us  [the longest x1 37.5 us: attention(): call(attention_kernel, 'attention', [SMEM] * 3 + [VMEM] * 10, [qd.shape]...]
    unnamed x20 -> x44, local copies, waits for them, and re-layouts: 9.81 us -> 6.27 us
    reshape x2 -> x0, local copies, waits for them, and re-layouts: 2.63 us -> none  [by_head(): return array.reshape(rows, -1, HEAD_DIM).transpose(1, 0, 2)]
  transfers between devices with their start and end apart: 5 -> 24, of which waited for: 3 -> 11; matrix products, arithmetic and copies ran while one was open for 4% -> 0% of each run, Pallas kernels for 0% -> 2%
where the time goes in v2:
time: 148 us
  starting transfers between devices  55.8 us (38%)
  Pallas kernels  42.9 us (29%)
  waiting for transfers between devices  41.2 us (28%)
  local copies, waits for them, and re-layouts  6.31 us (4%)
    pallas_call x1, Pallas kernels, attention(): call(attention_kernel, 'attention', [SMEM] * 3 + [VMEM] * 10, [qd.shape]...  37.5 us
    ppermute x8, starting transfers between devices, down(): lax.ppermute(array, 'z', [(i, (i - 1) % PLANES) for i in range(PLANES)])  27.1 us
    ppermute x8, waiting for transfers between devices, up(): lax.ppermute(array, 'z', [(i, (i + 1) % PLANES) for i in range(PLANES)])  21.8 us
    all_to_all x2, starting transfers between devices, swap(): return lax.all_to_all(array, PLANE, split_axis=0, concat_axis=0, tiled=True)  17.9 us
    ppermute x8, waiting for transfers between devices, down(): lax.ppermute(array, 'z', [(i, (i - 1) % PLANES) for i in range(PLANES)])  15.3 us
    ppermute x6, starting transfers between devices, exchange(): lax.ppermute(tiles[t], QUAD, [(i, i ^ t) for i in range(4)])  10.3 us
    unnamed x44, local copies, waits for them, and re-layouts  6.27 us
  transfers between devices with their start and end apart: 24, of which 11 were waited for; matrix products, arithmetic and copies ran while one was open for 0% of the time, Pallas kernels for 2%

profile of v2, /device:TPU:1, one launch (start us, length us, event | category | flops | bytes accessed | tf_op | source)
XLA Modules:
  0.0 147.8 jit_solution(12887598866431906059)
XLA Ops:
  0.6 0.1 pad_add_fusion.me_ref
  0.7 0.9 copy-done.2
  1.6 0.9 copy-done.3
  2.5 0.6 split_kv.1
  3.1 3.3 %collective-permute-start = (bf16[128,256]{1,0:T(8,128)(2,1)S(1)}, bf16[128,256]{1,0:T(8,128)(2,1)S(1)}, u32[]{:S(2)}, u32[]{:S(2)}) collective-permute-start(bf16[128,256]{1,0:T(8,128)(2,1)S(1)} %get-tuple-element.34), channel_id=1, source_target_pairs={{0,8},{8,0},{128,136},{136,128},{1,9},{9,1},{129,137},{137,129},{2... | collective-permute-start | bytes 196616 | tf_op jit(solution)/shard_map/ppermute | solution.py:198
  6.5 1.0 collective-permute-start.1
  7.5 2.2 %collective-permute-start.2 = (bf16[128,256]{1,0:T(8,128)(2,1)S(1)}, bf16[128,256]{1,0:T(8,128)(2,1)S(1)}, u32[]{:S(2)}, u32[]{:S(2)}) collective-permute-start(bf16[128,256]{1,0:T(8,128)(2,1)S(1)} %get-tuple-element.36), channel_id=1, source_target_pairs={{0,136},{8,128},{128,8},{136,0},{1,137},{9,129},{129,9},{137,1},{2... | collective-permute-start | bytes 196616 | tf_op jit(solution)/shard_map/ppermute | solution.py:198
  9.7 1.2 copy-done
  10.9 1.2 copy-done.1
  12.1 1.7 %split_heads.1 = bf16[32,128,256]{2,1,0:T(8,128)(2,1)} custom-call(bf16[128,4096]{1,0:T(8,128)(2,1)S(1)} %copy-done, bf16[128,4096]{1,0:T(8,128)(2,1)S(1)} %copy-done.1), custom_call_target="tpu_custom_call" | custom-call | tf_op jit(solution)/shard_map/split_heads/pallas_call | solution.py:79
  13.9 5.5 %all-to-all-start = ((bf16[32,128,256]{2,1,0:T(8,128)(2,1)}), bf16[32,128,256]{2,1,0:T(8,128)(2,1)S(1)}, u32[]{:S(2)}, u32[]{:S(2)}) async-start(bf16[32,128,256]{2,1,0:T(8,128)(2,1)} %split_heads.1), calls=%async_computation | async-start | bytes 4194304 | tf_op jit(solution)/shard_map/all_to_all | solution.py:224
  19.4 5.7 %collective-permute-start.4 = (bf16[4,128,256]{2,1,0:T(8,128)(2,1)S(1)}, bf16[4,128,256]{2,1,0:T(8,128)(2,1)S(1)}, u32[]{:S(2)}, u32[]{:S(2)}) collective-permute-start(bf16[4,128,256]{2,1,0:T(8,128)(2,1)S(1)} %pad_maximum_fusion.refs_0_), channel_id=1, source_target_pairs={{0,112},{16,0},{32,16},{48,32},{64,48},{80,64},{96,80},{112,96},{1... | collective-permute-start | bytes 786440 | tf_op jit(solution)/shard_map/ppermute | solution.py:193
  25.1 5.5 %collective-permute-done.4.refs_2_ = bf16[4,128,256]{2,1,0:T(8,128)(2,1)S(1)} collective-permute-done((bf16[4,128,256]{2,1,0:T(8,128)(2,1)S(1)}, bf16[4,128,256]{2,1,0:T(8,128)(2,1)S(1)}, u32[]{:S(2)}, u32[]{:S(2)}) %collective-permute-start.4) | collective-permute-done | bytes 262176 | tf_op jit(solution)/shard_map/ppermute | solution.py:193
  30.6 3.4 %collective-permute-start.6 = (bf16[4,128,256]{2,1,0:T(8,128)(2,1)S(1)}, bf16[4,128,256]{2,1,0:T(8,128)(2,1)S(1)}, u32[]{:S(2)}, u32[]{:S(2)}) collective-permute-start(bf16[4,128,256]{2,1,0:T(8,128)(2,1)S(1)} %collective-permute-done.4.refs_2_), channel_id=1, source_target_pairs={{0,112},{16,0},{32,16},{48,32},{64,48},{80,64},{96,80},{112,96},{1... | collective-permute-start | bytes 786440 | tf_op jit(solution)/shard_map/ppermute | solution.py:193
  34.0 4.5 %collective-permute-done.6.refs_4_ = bf16[4,128,256]{2,1,0:T(8,128)(2,1)S(1)} collective-permute-done((bf16[4,128,256]{2,1,0:T(8,128)(2,1)S(1)}, bf16[4,128,256]{2,1,0:T(8,128)(2,1)S(1)}, u32[]{:S(2)}, u32[]{:S(2)}) %collective-permute-start.6) | collective-permute-done | bytes 262176 | tf_op jit(solution)/shard_map/ppermute | solution.py:193
  38.5 3.4 %collective-permute-start.8 = (bf16[4,128,256]{2,1,0:T(8,128)(2,1)S(1)}, bf16[4,128,256]{2,1,0:T(8,128)(2,1)S(1)}, u32[]{:S(2)}, u32[]{:S(2)}) collective-permute-start(bf16[4,128,256]{2,1,0:T(8,128)(2,1)S(1)} %collective-permute-done.6.refs_4_), channel_id=1, source_target_pairs={{0,112},{16,0},{32,16},{48,32},{64,48},{80,64},{96,80},{112,96},{1... | collective-permute-start | bytes 786440 | tf_op jit(solution)/shard_map/ppermute | solution.py:193
  42.0 3.6 %collective-permute-done.8.refs_6_ = bf16[4,128,256]{2,1,0:T(8,128)(2,1)S(1)} collective-permute-done((bf16[4,128,256]{2,1,0:T(8,128)(2,1)S(1)}, bf16[4,128,256]{2,1,0:T(8,128)(2,1)S(1)}, u32[]{:S(2)}, u32[]{:S(2)}) %collective-permute-start.8) | collective-permute-done | bytes 262176 | tf_op jit(solution)/shard_map/ppermute | solution.py:193
  45.6 3.5 %collective-permute-start.10 = (bf16[2,128,256]{2,1,0:T(8,128)(2,1)S(1)}, bf16[2,128,256]{2,1,0:T(8,128)(2,1)S(1)}, u32[]{:S(2)}, u32[]{:S(2)}) collective-permute-start(bf16[2,128,256]{2,1,0:T(8,128)(2,1)S(1)} %slice.73), channel_id=1, source_target_pairs={{0,112},{16,0},{32,16},{48,32},{64,48},{80,64},{96,80},{112,96},{1... | collective-permute-start | bytes 393224 | tf_op jit(solution)/shard_map/ppermute | solution.py:193
  49.1 0.3 collective-permute-start.9
  49.4 1.7 %collective-permute-done.10.refs_8_ = bf16[2,128,256]{2,1,0:T(8,128)(2,1)S(1)} collective-permute-done((bf16[2,128,256]{2,1,0:T(8,128)(2,1)S(1)}, bf16[2,128,256]{2,1,0:T(8,128)(2,1)S(1)}, u32[]{:S(2)}, u32[]{:S(2)}) %collective-permute-start.10) | collective-permute-done | bytes 131104 | tf_op jit(solution)/shard_map/ppermute | solution.py:193
  51.0 0.7 copy-done.21
  51.7 2.8 %collective-permute-done.9.refs_7_ = bf16[2,128,256]{2,1,0:T(8,128)(2,1)} collective-permute-done((bf16[2,128,256]{2,1,0:T(8,128)(2,1)S(1)}, bf16[2,128,256]{2,1,0:T(8,128)(2,1)}, u32[]{:S(2)}, u32[]{:S(2)}) %collective-permute-start.9) | collective-permute-done | bytes 131104 | tf_op jit(solution)/shard_map/ppermute | solution.py:189
  54.6 1.3 copy-done.6
  55.8 37.5 %attention.1 = (bf16[32,128,256]{2,1,0:T(8,128)(2,1)}, bf16[4,128,256]{2,1,0:T(8,128)(2,1)}, bf16[4,128,256]{2,1,0:T(8,128)(2,1)}, bf16[4,128,256]{2,1,0:T(8,128...) custom-call(s32[2]{0:T(128)} %copy-done.4, ...), custom_call_target="tpu_custom_call" | custom-call | flops 6442450944 | bytes 8388608 | tf_op jit(solution)/shard_map/attention/pallas_call | solution.py:170
  93.4 2.7 %collective-permute-start.12 = (bf16[2,128,256]{2,1,0:T(8,128)(2,1)}, bf16[2,128,256]{2,1,0:T(8,128)(2,1)S(1)}, u32[]{:S(2)}, u32[]{:S(2)}) collective-permute-start(bf16[2,128,256]{2,1,0:T(8,128)(2,1)} %get-tuple-element.44), channel_id=1, source_target_pairs={{0,112},{16,0},{32,16},{48,32},{64,48},{80,64},{96,80},{112,96},{1... | collective-permute-start | bytes 393224 | tf_op jit(solution)/shard_map/ppermute | solution.py:193
  96.0 2.6 %collective-permute-done.11 = bf16[2,128,256]{2,1,0:T(8,128)(2,1)S(1)} collective-permute-done((bf16[2,128,256]{2,1,0:T(8,128)(2,1)}, bf16[2,128,256]{2,1,0:T(8,128)(2,1)S(1)}, u32[]{:S(2)}, u32[]{:S(2)}) %collective-permute-start.11) | collective-permute-done | bytes 131104 | tf_op jit(solution)/shard_map/ppermute | solution.py:189
  98.6 12.3 %all-to-all-start.1 = ((bf16[32,128,256]{2,1,0:T(8,128)(2,1)}), bf16[32,128,256]{2,1,0:T(8,128)(2,1)S(1)}, u32[]{:S(2)}, u32[]{:S(2)}) async-start(bf16[32,128,256]{2,1,0:T(8,128)(2,1)} %get-tuple-element.45), calls=%async_computation.1 | async-start | bytes 4194304 | tf_op jit(solution)/shard_map/all_to_all | solution.py:224
  111.1 0.1 collective-permute-start.13
  111.3 3.0 %collective-permute-start.16 = (bf16[4,128,256]{2,1,0:T(8,128)(2,1)S(1)}, bf16[4,128,256]{2,1,0:T(8,128)(2,1)S(1)}, u32[]{:S(2)}, u32[]{:S(2)}) collective-permute-start(bf16[4,128,256]{2,1,0:T(8,128)(2,1)S(1)} %pad_maximum_fusion.2), channel_id=1, source_target_pairs={{0,112},{16,0},{32,16},{48,32},{64,48},{80,64},{96,80},{112,96},{1... | collective-permute-start | bytes 786440 | tf_op jit(solution)/shard_map/ppermute | solution.py:193
  114.3 6.4 %collective-permute-done.13 = bf16[4,128,256]{2,1,0:T(8,128)(2,1)S(1)} collective-permute-done((bf16[4,128,256]{2,1,0:T(8,128)(2,1)S(1)}, bf16[4,128,256]{2,1,0:T(8,128)(2,1)S(1)}, u32[]{:S(2)}, u32[]{:S(2)}) %collective-permute-start.13) | collective-permute-done | bytes 262176 | tf_op jit(solution)/shard_map/ppermute | solution.py:189
  120.7 0.1 add_convert_fusion.3
  120.7 0.1 collective-permute-start.14
  120.8 0.1 add_convert_fusion.1
  120.9 2.7 %collective-permute-start.17 = (bf16[4,128,256]{2,1,0:T(8,128)(2,1)S(1)}, bf16[4,128,256]{2,1,0:T(8,128)(2,1)S(1)}, u32[]{:S(2)}, u32[]{:S(2)}) collective-permute-start(bf16[4,128,256]{2,1,0:T(8,128)(2,1)S(1)} %add_convert_fusion.1), channel_id=1, source_target_pairs={{0,112},{16,0},{32,16},{48,32},{64,48},{80,64},{96,80},{112,96},{1... | collective-permute-start | bytes 786440 | tf_op jit(solution)/shard_map/ppermute | solution.py:193
  123.6 5.5 %collective-permute-done.14 = bf16[4,128,256]{2,1,0:T(8,128)(2,1)S(1)} collective-permute-done((bf16[4,128,256]{2,1,0:T(8,128)(2,1)S(1)}, bf16[4,128,256]{2,1,0:T(8,128)(2,1)S(1)}, u32[]{:S(2)}, u32[]{:S(2)}) %collective-permute-start.14) | collective-permute-done | bytes 262176 | tf_op jit(solution)/shard_map/ppermute | solution.py:189
  129.1 0.1 add_convert_fusion.2
  129.2 0.1 collective-permute-start.15
  129.3 0.1 add_convert_fusion
  129.4 2.7 %collective-permute-start.18 = (bf16[4,128,256]{2,1,0:T(8,128)(2,1)S(1)}, bf16[4,128,256]{2,1,0:T(8,128)(2,1)S(1)}, u32[]{:S(2)}, u32[]{:S(2)}) collective-permute-start(bf16[4,128,256]{2,1,0:T(8,128)(2,1)S(1)} %add_convert_fusion), channel_id=1, source_target_pairs={{0,112},{16,0},{32,16},{48,32},{64,48},{80,64},{96,80},{112,96},{1... | collective-permute-start | bytes 786440 | tf_op jit(solution)/shard_map/ppermute | solution.py:193
  132.1 4.6 %collective-permute-done.15 = bf16[4,128,256]{2,1,0:T(8,128)(2,1)S(1)} collective-permute-done((bf16[4,128,256]{2,1,0:T(8,128)(2,1)S(1)}, bf16[4,128,256]{2,1,0:T(8,128)(2,1)S(1)}, u32[]{:S(2)}, u32[]{:S(2)}) %collective-permute-start.15) | collective-permute-done | bytes 262176 | tf_op jit(solution)/shard_map/ppermute | solution.py:189
  136.7 2.6 %all-to-all-done.1.tiles = bf16[32,128,256]{2,1,0:T(8,128)(2,1)S(1)} async-done(((bf16[32,128,256]{2,1,0:T(8,128)(2,1)}), bf16[32,128,256]{2,1,0:T(8,128)(2,1)S(1)}, u32[]{:S(2)}, u32[]{:S(2)}) %all-to-all-start.1) | async-done | bytes 2097184 | tf_op jit(solution)/shard_map/all_to_all | solution.py:224
  139.3 0.1 fusion.3
  139.4 2.5 %collective-permute-start.21 = (bf16[128,256]{1,0:T(8,128)(2,1)S(1)}, bf16[128,256]{1,0:T(8,128)(2,1)S(1)}, u32[]{:S(2)}, u32[]{:S(2)}) collective-permute-start(bf16[128,256]{1,0:T(8,128)(2,1)S(1)} %get-tuple-element.62), channel_id=1, source_target_pairs={{0,136},{8,128},{128,8},{136,0},{1,137},{9,129},{129,9},{137,1},{2... | collective-permute-start | bytes 196616 | tf_op jit(solution)/shard_map/ppermute | solution.py:198
  141.9 0.4 collective-permute-start.20
  142.3 0.8 collective-permute-start.19
  143.1 1.9 %join_heads.1 = (bf16[128,4096]{1,0:T(8,128)(2,1)}, bf16[128,4096]{1,0:T(8,128)(2,1)}) custom-call(bf16[32,128,256]{2,1,0:T(8,128)(2,1)S(1)} %all-to-all-done.1.tiles), custom_call_target="tpu_custom_call" | custom-call | tf_op jit(solution)/shard_map/join_heads/pallas_call | solution.py:90
  145.0 1.5 %collective-permute-done.20.refs_2_ = bf16[128,256]{1,0:T(8,128)(2,1)S(1)} collective-permute-done((bf16[128,256]{1,0:T(8,128)(2,1)S(1)}, bf16[128,256]{1,0:T(8,128)(2,1)S(1)}, u32[]{:S(2)}, u32[]{:S(2)}) %collective-permute-start.20) | collective-permute-done | bytes 65568 | tf_op jit(solution)/shard_map/ppermute | solution.py:198
  146.5 1.3 join_kv.1
  (64 shorter events, 0.4 us)
Async XLA Ops:
  0.7 0.9 copy-start.2
  1.6 0.9 copy-start.3
  2.5 11.3 %copy-start.4 = (s32[2]{0:T(128)}, s32[2]{0:T(128)S(1)}, u32[]{:S(2)}) copy-start(s32[2]{0:T(128)S(1)} %pad_add_fusion.me_ref) | copy-start | bytes 28
  3.1 10.7 %collective-permute-start = (bf16[128,256]{1,0:T(8,128)(2,1)S(1)}, bf16[128,256]{1,0:T(8,128)(2,1)S(1)}, u32[]{:S(2)}, u32[]{:S(2)}) collective-permute-start(bf16[128,256]{1,0:T(8,128)(2,1)S(1)} %get-tuple-element.34), channel_id=1, source_target_pairs={{0,8},{8,0},{128,136},{136,128},{1,9},{9,1},{129,137},{137,129},{2... | collective-permute-start | bytes 196616 | tf_op jit(solution)/shard_map/ppermute | solution.py:198
  6.5 7.4 %collective-permute-start.1 = (bf16[128,256]{1,0:T(8,128)(2,1)S(1)}, bf16[128,256]{1,0:T(8,128)(2,1)S(1)}, u32[]{:S(2)}, u32[]{:S(2)}) collective-permute-start(bf16[128,256]{1,0:T(8,128)(2,1)S(1)} %get-tuple-element.35), channel_id=1, source_target_pairs={{0,128},{8,136},{128,0},{136,8},{1,129},{9,137},{129,1},{137,9},{2... | collective-permute-start | bytes 196616 | tf_op jit(solution)/shard_map/ppermute | solution.py:198
  7.5 6.4 %collective-permute-start.2 = (bf16[128,256]{1,0:T(8,128)(2,1)S(1)}, bf16[128,256]{1,0:T(8,128)(2,1)S(1)}, u32[]{:S(2)}, u32[]{:S(2)}) collective-permute-start(bf16[128,256]{1,0:T(8,128)(2,1)S(1)} %get-tuple-element.36), channel_id=1, source_target_pairs={{0,136},{8,128},{128,8},{136,0},{1,137},{9,129},{129,9},{137,1},{2... | collective-permute-start | bytes 196616 | tf_op jit(solution)/shard_map/ppermute | solution.py:198
  9.7 1.2 copy-start
  10.9 1.2 copy-start.1
  13.9 40.6 %all-to-all-start = ((bf16[32,128,256]{2,1,0:T(8,128)(2,1)}), bf16[32,128,256]{2,1,0:T(8,128)(2,1)S(1)}, u32[]{:S(2)}, u32[]{:S(2)}) async-start(bf16[32,128,256]{2,1,0:T(8,128)(2,1)} %split_heads.1), calls=%async_computation | async-start | bytes 4194304 | tf_op jit(solution)/shard_map/all_to_all | solution.py:224
  19.4 35.1 %copy-start.13 = (bf16[4,128,256]{2,1,0:T(8,128)(2,1)}, bf16[4,128,256]{2,1,0:T(8,128)(2,1)S(1)}, u32[]{:S(2)}) copy-start(bf16[4,128,256]{2,1,0:T(8,128)(2,1)S(1)} %pad_maximum_fusion.refs_0_) | copy-start | bytes 786436
  19.4 11.1 %collective-permute-start.4 = (bf16[4,128,256]{2,1,0:T(8,128)(2,1)S(1)}, bf16[4,128,256]{2,1,0:T(8,128)(2,1)S(1)}, u32[]{:S(2)}, u32[]{:S(2)}) collective-permute-start(bf16[4,128,256]{2,1,0:T(8,128)(2,1)S(1)} %pad_maximum_fusion.refs_0_), channel_id=1, source_target_pairs={{0,112},{16,0},{32,16},{48,32},{64,48},{80,64},{96,80},{112,96},{1... | collective-permute-start | bytes 786440 | tf_op jit(solution)/shard_map/ppermute | solution.py:193
  25.1 8.9 %collective-permute-start.3 = (bf16[4,128,256]{2,1,0:T(8,128)(2,1)S(1)}, bf16[4,128,256]{2,1,0:T(8,128)(2,1)S(1)}, u32[]{:S(2)}, u32[]{:S(2)}) collective-permute-start(bf16[4,128,256]{2,1,0:T(8,128)(2,1)S(1)} %pad_maximum_fusion.refs_0_), channel_id=1, source_target_pairs={{0,16},{16,32},{32,48},{48,64},{64,80},{80,96},{96,112},{112,0},{1... | collective-permute-start | bytes 786440 | tf_op jit(solution)/shard_map/ppermute | solution.py:189
  30.6 23.9 %copy-start.17 = (bf16[4,128,256]{2,1,0:T(8,128)(2,1)}, bf16[4,128,256]{2,1,0:T(8,128)(2,1)S(1)}, u32[]{:S(2)}) copy-start(bf16[4,128,256]{2,1,0:T(8,128)(2,1)S(1)} %collective-permute-done.4.refs_2_) | copy-start | bytes 786436
  30.6 8.0 %collective-permute-start.6 = (bf16[4,128,256]{2,1,0:T(8,128)(2,1)S(1)}, bf16[4,128,256]{2,1,0:T(8,128)(2,1)S(1)}, u32[]{:S(2)}, u32[]{:S(2)}) collective-permute-start(bf16[4,128,256]{2,1,0:T(8,128)(2,1)S(1)} %collective-permute-done.4.refs_2_), channel_id=1, source_target_pairs={{0,112},{16,0},{32,16},{48,32},{64,48},{80,64},{96,80},{112,96},{1... | collective-permute-start | bytes 786440 | tf_op jit(solution)/shard_map/ppermute | solution.py:193
  34.0 20.5 %copy-start.18 = (bf16[4,128,256]{2,1,0:T(8,128)(2,1)}, bf16[4,128,256]{2,1,0:T(8,128)(2,1)S(1)}, u32[]{:S(2)}) copy-start(bf16[4,128,256]{2,1,0:T(8,128)(2,1)S(1)} %collective-permute-done.3.refs_1_) | copy-start | bytes 786436
  34.0 8.0 %collective-permute-start.5 = (bf16[4,128,256]{2,1,0:T(8,128)(2,1)S(1)}, bf16[4,128,256]{2,1,0:T(8,128)(2,1)S(1)}, u32[]{:S(2)}, u32[]{:S(2)}) collective-permute-start(bf16[4,128,256]{2,1,0:T(8,128)(2,1)S(1)} %collective-permute-done.3.refs_1_), channel_id=1, source_target_pairs={{0,16},{16,32},{32,48},{48,64},{64,80},{80,96},{96,112},{112,0},{1... | collective-permute-start | bytes 786440 | tf_op jit(solution)/shard_map/ppermute | solution.py:189
  38.5 3.4 %copy-start.19 = (bf16[4,128,256]{2,1,0:T(8,128)(2,1)}, bf16[4,128,256]{2,1,0:T(8,128)(2,1)S(1)}, u32[]{:S(2)}) copy-start(bf16[4,128,256]{2,1,0:T(8,128)(2,1)S(1)} %collective-permute-done.6.refs_4_) | copy-start | bytes 786436
  38.5 7.0 %collective-permute-start.8 = (bf16[4,128,256]{2,1,0:T(8,128)(2,1)S(1)}, bf16[4,128,256]{2,1,0:T(8,128)(2,1)S(1)}, u32[]{:S(2)}, u32[]{:S(2)}) collective-permute-start(bf16[4,128,256]{2,1,0:T(8,128)(2,1)S(1)} %collective-permute-done.6.refs_4_), channel_id=1, source_target_pairs={{0,112},{16,0},{32,16},{48,32},{64,48},{80,64},{96,80},{112,96},{1... | collective-permute-start | bytes 786440 | tf_op jit(solution)/shard_map/ppermute | solution.py:193
  42.0 7.1 %copy-start.20 = (bf16[4,128,256]{2,1,0:T(8,128)(2,1)}, bf16[4,128,256]{2,1,0:T(8,128)(2,1)S(1)}, u32[]{:S(2)}) copy-start(bf16[4,128,256]{2,1,0:T(8,128)(2,1)S(1)} %collective-permute-done.5.refs_3_) | copy-start | bytes 786436
  42.0 7.1 %collective-permute-start.7 = (bf16[4,128,256]{2,1,0:T(8,128)(2,1)S(1)}, bf16[4,128,256]{2,1,0:T(8,128)(2,1)S(1)}, u32[]{:S(2)}, u32[]{:S(2)}) collective-permute-start(bf16[4,128,256]{2,1,0:T(8,128)(2,1)S(1)} %collective-permute-done.5.refs_3_), channel_id=1, source_target_pairs={{0,16},{16,32},{32,48},{48,64},{64,80},{80,96},{96,112},{112,0},{1... | collective-permute-start | bytes 786440 | tf_op jit(solution)/shard_map/ppermute | solution.py:189
  45.6 9.0 %copy-start.15 = (bf16[4,128,256]{2,1,0:T(8,128)(2,1)}, bf16[4,128,256]{2,1,0:T(8,128)(2,1)S(1)}, u32[]{:S(2)}) copy-start(bf16[4,128,256]{2,1,0:T(8,128)(2,1)S(1)} %collective-permute-done.8.refs_6_) | copy-start | bytes 786436
  45.6 5.4 %collective-permute-start.10 = (bf16[2,128,256]{2,1,0:T(8,128)(2,1)S(1)}, bf16[2,128,256]{2,1,0:T(8,128)(2,1)S(1)}, u32[]{:S(2)}, u32[]{:S(2)}) collective-permute-start(bf16[2,128,256]{2,1,0:T(8,128)(2,1)S(1)} %slice.73), channel_id=1, source_target_pairs={{0,112},{16,0},{32,16},{48,32},{64,48},{80,64},{96,80},{112,96},{1... | collective-permute-start | bytes 393224 | tf_op jit(solution)/shard_map/ppermute | solution.py:193
  49.1 5.5 %copy-start.16 = (bf16[4,128,256]{2,1,0:T(8,128)(2,1)}, bf16[4,128,256]{2,1,0:T(8,128)(2,1)S(1)}, u32[]{:S(2)}) copy-start(bf16[4,128,256]{2,1,0:T(8,128)(2,1)S(1)} %collective-permute-done.7.refs_5_) | copy-start | bytes 786436
  49.1 5.4 %collective-permute-start.9 = (bf16[2,128,256]{2,1,0:T(8,128)(2,1)S(1)}, bf16[2,128,256]{2,1,0:T(8,128)(2,1)}, u32[]{:S(2)}, u32[]{:S(2)}) collective-permute-start(bf16[2,128,256]{2,1,0:T(8,128)(2,1)S(1)} %slice.72), channel_id=1, source_target_pairs={{0,16},{16,32},{32,48},{48,64},{64,80},{80,96},{96,112},{112,0},{1... | collective-permute-start | bytes 393224 | tf_op jit(solution)/shard_map/ppermute | solution.py:189
  51.0 0.7 copy-start.21
  54.5 1.3 copy-start.6
  93.3 5.3 %collective-permute-start.11 = (bf16[2,128,256]{2,1,0:T(8,128)(2,1)}, bf16[2,128,256]{2,1,0:T(8,128)(2,1)S(1)}, u32[]{:S(2)}, u32[]{:S(2)}) collective-permute-start(bf16[2,128,256]{2,1,0:T(8,128)(2,1)} %get-tuple-element.43), channel_id=1, source_target_pairs={{0,16},{16,32},{32,48},{48,64},{64,80},{80,96},{96,112},{112,0},{1... | collective-permute-start | bytes 393224 | tf_op jit(solution)/shard_map/ppermute | solution.py:189
  93.4 5.2 %collective-permute-start.12 = (bf16[2,128,256]{2,1,0:T(8,128)(2,1)}, bf16[2,128,256]{2,1,0:T(8,128)(2,1)S(1)}, u32[]{:S(2)}, u32[]{:S(2)}) collective-permute-start(bf16[2,128,256]{2,1,0:T(8,128)(2,1)} %get-tuple-element.44), channel_id=1, source_target_pairs={{0,112},{16,0},{32,16},{48,32},{64,48},{80,64},{96,80},{112,96},{1... | collective-permute-start | bytes 393224 | tf_op jit(solution)/shard_map/ppermute | solution.py:193
  98.6 12.4 %copy-start.12 = (bf16[4,128,256]{2,1,0:T(8,128)(2,1)S(1)}, bf16[4,128,256]{2,1,0:T(8,128)(2,1)}, u32[]{:S(2)}) copy-start(bf16[4,128,256]{2,1,0:T(8,128)(2,1)} %get-tuple-element.48) | copy-start | bytes 786436
  98.6 12.4 %copy-start.11 = (bf16[4,128,256]{2,1,0:T(8,128)(2,1)S(1)}, bf16[4,128,256]{2,1,0:T(8,128)(2,1)}, u32[]{:S(2)}) copy-start(bf16[4,128,256]{2,1,0:T(8,128)(2,1)} %get-tuple-element.52) | copy-start | bytes 786436
  98.6 40.7 %all-to-all-start.1 = ((bf16[32,128,256]{2,1,0:T(8,128)(2,1)}), bf16[32,128,256]{2,1,0:T(8,128)(2,1)S(1)}, u32[]{:S(2)}, u32[]{:S(2)}) async-start(bf16[32,128,256]{2,1,0:T(8,128)(2,1)} %get-tuple-element.45), calls=%async_computation.1 | async-start | bytes 4194304 | tf_op jit(solution)/shard_map/all_to_all | solution.py:224
  110.9 9.7 %copy-start.10 = (bf16[4,128,256]{2,1,0:T(8,128)(2,1)S(1)}, bf16[4,128,256]{2,1,0:T(8,128)(2,1)}, u32[]{:S(2)}) copy-start(bf16[4,128,256]{2,1,0:T(8,128)(2,1)} %get-tuple-element.47) | copy-start | bytes 786436
  110.9 9.9 %copy-start.9 = (bf16[4,128,256]{2,1,0:T(8,128)(2,1)S(1)}, bf16[4,128,256]{2,1,0:T(8,128)(2,1)}, u32[]{:S(2)}) copy-start(bf16[4,128,256]{2,1,0:T(8,128)(2,1)} %get-tuple-element.51) | copy-start | bytes 786436
  110.9 18.2 %copy-start.8 = (bf16[4,128,256]{2,1,0:T(8,128)(2,1)S(1)}, bf16[4,128,256]{2,1,0:T(8,128)(2,1)}, u32[]{:S(2)}) copy-start(bf16[4,128,256]{2,1,0:T(8,128)(2,1)} %get-tuple-element.46) | copy-start | bytes 786436
  111.0 18.3 %copy-start.7 = (bf16[4,128,256]{2,1,0:T(8,128)(2,1)S(1)}, bf16[4,128,256]{2,1,0:T(8,128)(2,1)}, u32[]{:S(2)}) copy-start(bf16[4,128,256]{2,1,0:T(8,128)(2,1)} %get-tuple-element.50) | copy-start | bytes 786436
  111.1 28.2 %copy-start.14 = (bf16[4,128,256]{2,1,0:T(8,128)(2,1)S(1)}, bf16[4,128,256]{2,1,0:T(8,128)(2,1)}, u32[]{:S(2)}) copy-start(bf16[4,128,256]{2,1,0:T(8,128)(2,1)} %get-tuple-element.57) | copy-start | bytes 786436
  111.1 9.5 %collective-permute-start.13 = (bf16[4,128,256]{2,1,0:T(8,128)(2,1)S(1)}, bf16[4,128,256]{2,1,0:T(8,128)(2,1)S(1)}, u32[]{:S(2)}, u32[]{:S(2)}) collective-permute-start(bf16[4,128,256]{2,1,0:T(8,128)(2,1)S(1)} %pad_maximum_fusion.1), channel_id=1, source_target_pairs={{0,16},{16,32},{32,48},{48,64},{64,80},{80,96},{96,112},{112,0},{1... | collective-permute-start | bytes 786440 | tf_op jit(solution)/shard_map/ppermute | solution.py:189
  111.3 9.5 %collective-permute-start.16 = (bf16[4,128,256]{2,1,0:T(8,128)(2,1)S(1)}, bf16[4,128,256]{2,1,0:T(8,128)(2,1)S(1)}, u32[]{:S(2)}, u32[]{:S(2)}) collective-permute-start(bf16[4,128,256]{2,1,0:T(8,128)(2,1)S(1)} %pad_maximum_fusion.2), channel_id=1, source_target_pairs={{0,112},{16,0},{32,16},{48,32},{64,48},{80,64},{96,80},{112,96},{1... | collective-permute-start | bytes 786440 | tf_op jit(solution)/shard_map/ppermute | solution.py:193
  120.7 8.4 %collective-permute-start.14 = (bf16[4,128,256]{2,1,0:T(8,128)(2,1)S(1)}, bf16[4,128,256]{2,1,0:T(8,128)(2,1)S(1)}, u32[]{:S(2)}, u32[]{:S(2)}) collective-permute-start(bf16[4,128,256]{2,1,0:T(8,128)(2,1)S(1)} %add_convert_fusion.3), channel_id=1, source_target_pairs={{0,16},{16,32},{32,48},{48,64},{64,80},{80,96},{96,112},{112,0},{1... | collective-permute-start | bytes 786440 | tf_op jit(solution)/shard_map/ppermute | solution.py:189
  120.9 8.4 %collective-permute-start.17 = (bf16[4,128,256]{2,1,0:T(8,128)(2,1)S(1)}, bf16[4,128,256]{2,1,0:T(8,128)(2,1)S(1)}, u32[]{:S(2)}, u32[]{:S(2)}) collective-permute-start(bf16[4,128,256]{2,1,0:T(8,128)(2,1)S(1)} %add_convert_fusion.1), channel_id=1, source_target_pairs={{0,112},{16,0},{32,16},{48,32},{64,48},{80,64},{96,80},{112,96},{1... | collective-permute-start | bytes 786440 | tf_op jit(solution)/shard_map/ppermute | solution.py:193
  129.2 17.3 %copy-start.5 = (s32[2]{0:T(128)S(1)}, s32[2]{0:T(128)}, u32[]{:S(2)}) copy-start(s32[2]{0:T(128)} %copy-done.4) | copy-start | bytes 28
  129.2 7.5 %collective-permute-start.15 = (bf16[4,128,256]{2,1,0:T(8,128)(2,1)S(1)}, bf16[4,128,256]{2,1,0:T(8,128)(2,1)S(1)}, u32[]{:S(2)}, u32[]{:S(2)}) collective-permute-start(bf16[4,128,256]{2,1,0:T(8,128)(2,1)S(1)} %add_convert_fusion.2), channel_id=1, source_target_pairs={{0,16},{16,32},{32,48},{48,64},{64,80},{80,96},{96,112},{112,0},{1... | collective-permute-start | bytes 786440 | tf_op jit(solution)/shard_map/ppermute | solution.py:189
  129.4 7.3 %collective-permute-start.18 = (bf16[4,128,256]{2,1,0:T(8,128)(2,1)S(1)}, bf16[4,128,256]{2,1,0:T(8,128)(2,1)S(1)}, u32[]{:S(2)}, u32[]{:S(2)}) collective-permute-start(bf16[4,128,256]{2,1,0:T(8,128)(2,1)S(1)} %add_convert_fusion), channel_id=1, source_target_pairs={{0,112},{16,0},{32,16},{48,32},{64,48},{80,64},{96,80},{112,96},{1... | collective-permute-start | bytes 786440 | tf_op jit(solution)/shard_map/ppermute | solution.py:193
  139.4 5.6 %collective-permute-start.21 = (bf16[128,256]{1,0:T(8,128)(2,1)S(1)}, bf16[128,256]{1,0:T(8,128)(2,1)S(1)}, u32[]{:S(2)}, u32[]{:S(2)}) collective-permute-start(bf16[128,256]{1,0:T(8,128)(2,1)S(1)} %get-tuple-element.62), channel_id=1, source_target_pairs={{0,136},{8,128},{128,8},{136,0},{1,137},{9,129},{129,9},{137,1},{2... | collective-permute-start | bytes 196616 | tf_op jit(solution)/shard_map/ppermute | solution.py:198
  141.9 4.6 %collective-permute-start.20 = (bf16[128,256]{1,0:T(8,128)(2,1)S(1)}, bf16[128,256]{1,0:T(8,128)(2,1)S(1)}, u32[]{:S(2)}, u32[]{:S(2)}) collective-permute-start(bf16[128,256]{1,0:T(8,128)(2,1)S(1)} %get-tuple-element.63), channel_id=1, source_target_pairs={{0,128},{8,136},{128,0},{136,8},{1,129},{9,137},{129,1},{137,9},{2... | collective-permute-start | bytes 196616 | tf_op jit(solution)/shard_map/ppermute | solution.py:198
  142.3 4.2 %collective-permute-start.19 = (bf16[128,256]{1,0:T(8,128)(2,1)S(1)}, bf16[128,256]{1,0:T(8,128)(2,1)S(1)}, u32[]{:S(2)}, u32[]{:S(2)}) collective-permute-start(bf16[128,256]{1,0:T(8,128)(2,1)S(1)} %get-tuple-element.64), channel_id=1, source_target_pairs={{0,8},{8,0},{128,136},{136,128},{1,9},{9,1},{129,137},{137,129},{2... | collective-permute-start | bytes 196616 | tf_op jit(solution)/shard_map/ppermute | solution.py:198

commit v3 on v2

--- a/solution.py
+++ b/solution.py
@@ -15,7 +15,7 @@
 QUAD = ("xhi", "core")
 FACTOR = 1.0 / math.sqrt(HEAD_DIM)
 LOG2E = math.log2(math.e)
-UNROLL = 4
+UNROLL = 8
 VMEM_MIB = 8
 BIG_MIB = 60
 WIDE = 2 * HEAD_DIM
@@ -36,12 +36,12 @@
     return pl.ds(pl.multiple_of(block * HEAD_DIM, HEAD_DIM), HEAD_DIM)
 
 
-def call(kernel, name, in_specs, shapes, scratch=(), **params):
+def call(kernel, name, in_specs, shapes, scratch=(), out_specs=None, **params):
     return pl.pallas_call(
         kernel,
         out_shape=tuple(jax.ShapeDtypeStruct(shape, BF16) for shape in shapes),
         in_specs=in_specs,
-        out_specs=tuple(VMEM for _ in shapes),
+        out_specs=tuple(out_specs or [VMEM for _ in shapes]),
         scratch_shapes=scratch,
         name=name,
         compiler_params=pltpu.CompilerParams(vmem_limit_bytes=(BIG_MIB if name == 'attention' else VMEM_MIB) * 2**20),
@@ -97,26 +97,25 @@
 def attention_kernel(me_ref, seg_ref, spans_ref, qd_ref, *refs):
     pieces, (od_ref, *parts), (kv_ref, kvt_ref, acc_ref) = refs[:9], refs[9:19], refs[19:]
     quad, z = me_ref[0], me_ref[1]
-    cad_blocks = qd_ref.shape[0]
-
-    def places(first):
-        own, up1, down1, up2, down2, up3, down3, up4, down4 = first
-        return (
-            (own, 0), (down1, 1), (down2, 2), (down3, 3), (up3, 5), (up2, 6), (up1, 7)
-        ), (up4, down4)
-
-    whole, halves = places(pieces)
-    for piece, at in (*((p, 4 * o) for p, o in whole), (halves[0], 16), (halves[1], 18)):
-
-        @pl.loop(0, piece.shape[0])
-        def _(t):
-            tile = piece[t]
-            kv_ref[at + t] = tile
-            kvt_ref[at + t, :HEAD_DIM, :] = tile[:, :HEAD_DIM].T
-            kvt_ref[at + t, HEAD_DIM:, :] = tile[:, HEAD_DIM:].T
-            acc_ref[at + t] = jnp.zeros((BLOCK, WIDE), F32)
-
-    def one_block(s):
+
+    @pl.when(pl.program_id(0) == 0)
+    def _():
+        own, up1, down1, up2, down2, up3, down3, up4, down4 = pieces
+        for piece, at in (
+            (own, 0), (down1, 4), (down2, 8), (down3, 12), (up4, 16),
+            (down4, 18), (up3, 20), (up2, 24), (up1, 28),
+        ):
+
+            @pl.loop(0, piece.shape[0], unroll=True)
+            def _(t):
+                tile = piece[t]
+                kv_ref[at + t] = tile
+                kvt_ref[at + t, :HEAD_DIM, :] = tile[:, :HEAD_DIM].T
+                kvt_ref[at + t, HEAD_DIM:, :] = tile[:, HEAD_DIM:].T
+                acc_ref[at + t] = jnp.zeros((BLOCK, WIDE), F32)
+
+    def one_block(u):
+        s = pl.program_id(0) * UNROLL + u
         head, xhi, core = s // 4, (s // 2) % 2, s % 2
         seg = seg_ref[(xhi * 16 + z * 2 + core) * 8 + head]
         locs = []
@@ -124,59 +123,70 @@
             d = spans_ref[j, seg]
             away = ((d // 2) % 8 - z) & 7
             locs.append(away * 4 + (((d // 16) * 2 + d % 2) ^ quad))
-        q, do = qd_ref[s, :, :HEAD_DIM], qd_ref[s, :, HEAD_DIM:]
+        q, do = qd_ref[u, :, :HEAD_DIM], qd_ref[u, :, HEAD_DIM:]
         keys = jnp.concatenate([kv_ref[loc, :, :HEAD_DIM] for loc in locs], axis=0)
         scores = nt(keys, q)
+        values = jnp.concatenate([kv_ref[loc, :, HEAD_DIM:] for loc in locs], axis=0)
+        yield
+        dprob = nt(values, do)
         top = jnp.max(scores, axis=0, keepdims=True)
         expo = jnp.exp2((scores - top) * (FACTOR * LOG2E))
         prob = expo * (1.0 / jnp.sum(expo, axis=0, keepdims=True))
         prob_b = prob.astype(BF16)
         value_t = jnp.concatenate([kvt_ref[loc, HEAD_DIM:, :] for loc in locs], axis=1)
+        yield
         attn_t = nn(value_t, prob_b)
-        od_ref[s, :, :HEAD_DIM] = attn_t.T.astype(BF16)
-        values = jnp.concatenate([kv_ref[loc, :, HEAD_DIM:] for loc in locs], axis=0)
-        dprob = nt(values, do)
+        yield
+        value_slots = nn(prob_b, do)
+        od_ref[u, :, :HEAD_DIM] = attn_t.T.astype(BF16)
         delta = jnp.sum(do.astype(F32).T * attn_t, axis=0, keepdims=True)
         dscore_b = (prob * (dprob - delta)).astype(BF16)
         key_t = jnp.concatenate([kvt_ref[loc, :HEAD_DIM, :] for loc in locs], axis=1)
+        yield
         dq_t = nn(key_t, dscore_b) * FACTOR
-        od_ref[s, :, HEAD_DIM:] = dq_t.T.astype(BF16)
-        key_slots, value_slots = nn(dscore_b, q), nn(prob_b, do)
+        key_slots = nn(dscore_b, q)
+        yield
+        od_ref[u, :, HEAD_DIM:] = dq_t.T.astype(BF16)
         for j in range(SPANS):
             rows = slice(j * BLOCK, (j + 1) * BLOCK)
             acc_ref[locs[j], :, :HEAD_DIM] += key_slots[rows]
             acc_ref[locs[j], :, HEAD_DIM:] += value_slots[rows]
 
-    @pl.loop(0, cad_blocks // UNROLL)
-    def _(i):
-        for u in range(UNROLL):
-            one_block(i * UNROLL + u)
-
-    own, up1, up2, up3, up4, down1, down2, down3, down4 = parts
-    for part, at in (
-        (own, 0), (up1, 4), (up2, 8), (up3, 12), (up4, 16),
-        (down4, 18), (down3, 20), (down2, 24), (down1, 28),
-    ):
-
-        @pl.loop(0, part.shape[0])
-        def _(t):
-            part[t, :, :HEAD_DIM] = (acc_ref[at + t, :, :HEAD_DIM] * FACTOR).astype(BF16)
-            part[t, :, HEAD_DIM:] = acc_ref[at + t, :, HEAD_DIM:].astype(BF16)
+    live = [one_block(u) for u in range(UNROLL)]
+    while live:
+        live = [block for block in live if next(block, True) is None]
+
+    @pl.when(pl.program_id(0) == pl.num_programs(0) - 1)
+    def _():
+        own, up1, up2, up3, up4, down1, down2, down3, down4 = parts
+        for part, at in (
+            (own, 0), (up1, 4), (up2, 8), (up3, 12), (up4, 16),
+            (down4, 18), (down3, 20), (down2, 24), (down1, 28),
+        ):
+
+            @pl.loop(0, part.shape[0])
+            def _(t):
+                part[t, :, :HEAD_DIM] = (acc_ref[at + t, :, :HEAD_DIM] * FACTOR).astype(BF16)
+                part[t, :, HEAD_DIM:] = acc_ref[at + t, :, HEAD_DIM:].astype(BF16)
 
 
 def attention(me, seg_map, spans_t, qd, pieces):
     cad_blocks, doc_blocks = qd.shape[0], 4 * PLANES
+    step = pl.BlockSpec((UNROLL, BLOCK, WIDE), lambda i: (i, 0, 0))
     whole, half = (4, BLOCK, WIDE), (2, BLOCK, WIDE)
+    parts = [whole] * 4 + [half] + [whole] * 3 + [half]
     return call(
         attention_kernel,
         "attention",
-        [SMEM] * 3 + [VMEM] * 10,
-        [qd.shape] + ([whole] * 4 + [half] + [whole] * 3 + [half]),
+        [SMEM] * 3 + [step] + [VMEM] * 9,
+        [qd.shape] + parts,
         [
             pltpu.VMEM((doc_blocks, BLOCK, WIDE), BF16),
             pltpu.VMEM((doc_blocks, WIDE, BLOCK), BF16),
             pltpu.VMEM((doc_blocks, BLOCK, WIDE), F32),
         ],
+        [step] + [VMEM] * 9,
+        grid=(cad_blocks // UNROLL,),
         cost_estimate=pl.CostEstimate(
             flops=cad_blocks * SPANS * 12 * BLOCK * BLOCK * HEAD_DIM,
             bytes_accessed=2 * (2 * qd.size + 2 * doc_blocks * BLOCK * WIDE),
@@ -199,8 +209,7 @@
     ]
 
 
-def gather_z(own):
-    up1, down1 = up(own), down(own)
+def gather_z(own, up1, down1):
     up2, down2 = up(up1), down(down1)
     up3, down3 = up(up2), down(down2)
     up4, down4 = up(up3[:2]), down(down3[2:])
@@ -210,7 +219,6 @@
 def scatter_z(parts, beside):
     own, up1, up2, up3, up4, down1, down2, down3, down4 = parts
     ups, downs = up(up4), down(down4)
-    beside, ups, downs = lax.optimization_barrier((beside, ups, downs))
     beside = swap(beside)
     ups = up(jnp.concatenate([plus(up3[:2], ups), up3[2:]]))
     downs = down(jnp.concatenate([down3[:2], plus(down3[2:], downs)]))
@@ -228,7 +236,8 @@
     me = jnp.stack([lax.axis_index(QUAD), lax.axis_index("z")]).astype(jnp.int32)
     tiles = exchange(split_kv(me, key, value))
     qd, tiles = lax.optimization_barrier((split_heads(query, d_out), tiles))
-    qd, pieces = swap(qd), gather_z(jnp.stack(tiles))
+    kv = jnp.stack(tiles)
+    qd, pieces = swap(qd), gather_z(kv, up(kv), down(kv))
     od, *parts = attention(me, seg_map, spans.T, qd, pieces)
     tiles, od = scatter_z(parts, od)
     attn_out, d_query = join_heads(od)

time: 148 us -> 133 us (0.90)
  Pallas kernels: 42.9 us -> 30.4 us
  waiting for transfers between devices: 41.2 us -> 38.6 us
    pallas_call x1, Pallas kernels: 37.5 us -> 24.9 us  [attention(): call(attention_kernel, 'attention', [SMEM] * 3 + [step] + [VMEM] * 9, [qd...]
    ppermute x8, waiting for transfers between devices: 21.8 us -> 15.6 us  [up(): lax.ppermute(array, 'z', [(i, (i + 1) % PLANES) for i in range(PLANES)])]
    ppermute x8, waiting for transfers between devices: 15.3 us -> 20.6 us  [down(): lax.ppermute(array, 'z', [(i, (i - 1) % PLANES) for i in range(PLANES)])]
    ppermute x8, starting transfers between devices: 27.1 us -> 23.8 us  [down(): lax.ppermute(array, 'z', [(i, (i - 1) % PLANES) for i in range(PLANES)])]
    ppermute x6, starting transfers between devices: 10.3 us -> 13.5 us  [exchange(): lax.ppermute(tiles[t], QUAD, [(i, i ^ t) for i in range(4)])]
    all_to_all x2, waiting for transfers between devices: 2.6 us -> 0.21 us  [swap(): return lax.all_to_all(array, PLANE, split_axis=0, concat_axis=0, tiled=True)]
    ppermute x8, starting transfers between devices: 0.58 us -> 2.33 us  [up(): lax.ppermute(array, 'z', [(i, (i + 1) % PLANES) for i in range(PLANES)])]
    unnamed x44 -> x46, local copies, waits for them, and re-layouts: 6.27 us -> 6.27 us
  transfers between devices with their start and end apart: 24 -> 24, of which waited for: 11 -> 15; matrix products, arithmetic and copies ran while one was open for 0% -> 0% of each run, Pallas kernels for 2% -> 3%
where the time goes in v3:
time: 133 us
  starting transfers between devices  56.3 us (42%)
  waiting for transfers between devices  38.6 us (29%)
  Pallas kernels  30.4 us (23%)
  local copies, waits for them, and re-layouts  6.31 us (5%)
    pallas_call x1, Pallas kernels, attention(): call(attention_kernel, 'attention', [SMEM] * 3 + [step] + [VMEM] * 9, [qd...  24.9 us
    ppermute x8, starting transfers between devices, down(): lax.ppermute(array, 'z', [(i, (i - 1) % PLANES) for i in range(PLANES)])  23.8 us
    ppermute x8, waiting for transfers between devices, down(): lax.ppermute(array, 'z', [(i, (i - 1) % PLANES) for i in range(PLANES)])  20.6 us
    all_to_all x2, starting transfers between devices, swap(): return lax.all_to_all(array, PLANE, split_axis=0, concat_axis=0, tiled=True)  16.7 us
    ppermute x8, waiting for transfers between devices, up(): lax.ppermute(array, 'z', [(i, (i + 1) % PLANES) for i in range(PLANES)])  15.6 us
    ppermute x6, starting transfers between devices, exchange(): lax.ppermute(tiles[t], QUAD, [(i, i ^ t) for i in range(4)])  13.5 us
    unnamed x46, local copies, waits for them, and re-layouts  6.27 us
  transfers between devices with their start and end apart: 24, of which 15 were waited for; matrix products, arithmetic and copies ran while one was open for 0% of the time, Pallas kernels for 3%

profile of v3, /device:TPU:1, one launch (start us, length us, event | category | flops | bytes accessed | tf_op | source)
XLA Modules:
  0.0 133.1 jit_solution(16662828876582435481)
XLA Ops:
  0.7 0.9 copy-done.2
  1.6 0.9 copy-done.3
  2.5 0.6 split_kv.1
  3.1 3.3 %collective-permute-start = (bf16[128,256]{1,0:T(8,128)(2,1)S(1)}, bf16[128,256]{1,0:T(8,128)(2,1)S(1)}, u32[]{:S(2)}, u32[]{:S(2)}) collective-permute-start(bf16[128,256]{1,0:T(8,128)(2,1)S(1)} %get-tuple-element.31), channel_id=1, source_target_pairs={{0,8},{8,0},{128,136},{136,128},{1,9},{9,1},{129,137},{137,129},{2... | collective-permute-start | bytes 196616 | tf_op jit(solution)/shard_map/ppermute | solution.py:208
  6.5 1.0 collective-permute-start.1
  7.5 2.2 %collective-permute-start.2 = (bf16[128,256]{1,0:T(8,128)(2,1)S(1)}, bf16[128,256]{1,0:T(8,128)(2,1)S(1)}, u32[]{:S(2)}, u32[]{:S(2)}) collective-permute-start(bf16[128,256]{1,0:T(8,128)(2,1)S(1)} %get-tuple-element.33), channel_id=1, source_target_pairs={{0,136},{8,128},{128,8},{136,0},{1,137},{9,129},{129,9},{137,1},{2... | collective-permute-start | bytes 196616 | tf_op jit(solution)/shard_map/ppermute | solution.py:208
  9.7 1.2 copy-done
  10.9 1.2 copy-done.1
  12.1 1.7 %split_heads.1 = bf16[32,128,256]{2,1,0:T(8,128)(2,1)} custom-call(bf16[128,4096]{1,0:T(8,128)(2,1)S(1)} %copy-done, bf16[128,4096]{1,0:T(8,128)(2,1)S(1)} %copy-done.1), custom_call_target="tpu_custom_call" | custom-call | tf_op jit(solution)/shard_map/split_heads/pallas_call | solution.py:79
  13.9 5.5 %all-to-all-start = ((bf16[32,128,256]{2,1,0:T(8,128)(2,1)}), bf16[32,128,256]{2,1,0:T(8,128)(2,1)S(1)}, u32[]{:S(2)}, u32[]{:S(2)}) async-start(bf16[32,128,256]{2,1,0:T(8,128)(2,1)} %split_heads.1), calls=%async_computation | async-start | bytes 4194304 | tf_op jit(solution)/shard_map/all_to_all | solution.py:232
  19.4 5.7 %collective-permute-start.4 = (bf16[4,128,256]{2,1,0:T(8,128)(2,1)S(1)}, bf16[4,128,256]{2,1,0:T(8,128)(2,1)S(1)}, u32[]{:S(2)}, u32[]{:S(2)}) collective-permute-start(bf16[4,128,256]{2,1,0:T(8,128)(2,1)S(1)} %pad_maximum_fusion.refs_0_), channel_id=1, source_target_pairs={{0,112},{16,0},{32,16},{48,32},{64,48},{80,64},{96,80},{112,96},{1... | collective-permute-start | bytes 786440 | tf_op jit(solution)/shard_map/ppermute | solution.py:203
  25.1 5.5 %collective-permute-done.4.refs_2_ = bf16[4,128,256]{2,1,0:T(8,128)(2,1)S(1)} collective-permute-done((bf16[4,128,256]{2,1,0:T(8,128)(2,1)S(1)}, bf16[4,128,256]{2,1,0:T(8,128)(2,1)S(1)}, u32[]{:S(2)}, u32[]{:S(2)}) %collective-permute-start.4) | collective-permute-done | bytes 262176 | tf_op jit(solution)/shard_map/ppermute | solution.py:203
  30.6 3.4 %collective-permute-start.6 = (bf16[4,128,256]{2,1,0:T(8,128)(2,1)S(1)}, bf16[4,128,256]{2,1,0:T(8,128)(2,1)S(1)}, u32[]{:S(2)}, u32[]{:S(2)}) collective-permute-start(bf16[4,128,256]{2,1,0:T(8,128)(2,1)S(1)} %collective-permute-done.4.refs_2_), channel_id=1, source_target_pairs={{0,112},{16,0},{32,16},{48,32},{64,48},{80,64},{96,80},{112,96},{1... | collective-permute-start | bytes 786440 | tf_op jit(solution)/shard_map/ppermute | solution.py:203
  34.0 4.5 %collective-permute-done.6.refs_4_ = bf16[4,128,256]{2,1,0:T(8,128)(2,1)S(1)} collective-permute-done((bf16[4,128,256]{2,1,0:T(8,128)(2,1)S(1)}, bf16[4,128,256]{2,1,0:T(8,128)(2,1)S(1)}, u32[]{:S(2)}, u32[]{:S(2)}) %collective-permute-start.6) | collective-permute-done | bytes 262176 | tf_op jit(solution)/shard_map/ppermute | solution.py:203
  38.5 3.4 %collective-permute-start.8 = (bf16[4,128,256]{2,1,0:T(8,128)(2,1)S(1)}, bf16[4,128,256]{2,1,0:T(8,128)(2,1)S(1)}, u32[]{:S(2)}, u32[]{:S(2)}) collective-permute-start(bf16[4,128,256]{2,1,0:T(8,128)(2,1)S(1)} %collective-permute-done.6.refs_4_), channel_id=1, source_target_pairs={{0,112},{16,0},{32,16},{48,32},{64,48},{80,64},{96,80},{112,96},{1... | collective-permute-start | bytes 786440 | tf_op jit(solution)/shard_map/ppermute | solution.py:203
  42.0 3.6 %collective-permute-done.8.refs_6_ = bf16[4,128,256]{2,1,0:T(8,128)(2,1)S(1)} collective-permute-done((bf16[4,128,256]{2,1,0:T(8,128)(2,1)S(1)}, bf16[4,128,256]{2,1,0:T(8,128)(2,1)S(1)}, u32[]{:S(2)}, u32[]{:S(2)}) %collective-permute-start.8) | collective-permute-done | bytes 262176 | tf_op jit(solution)/shard_map/ppermute | solution.py:203
  45.6 3.5 %collective-permute-start.10 = (bf16[2,128,256]{2,1,0:T(8,128)(2,1)S(1)}, bf16[2,128,256]{2,1,0:T(8,128)(2,1)S(1)}, u32[]{:S(2)}, u32[]{:S(2)}) collective-permute-start(bf16[2,128,256]{2,1,0:T(8,128)(2,1)S(1)} %slice.73), channel_id=1, source_target_pairs={{0,112},{16,0},{32,16},{48,32},{64,48},{80,64},{96,80},{112,96},{1... | collective-permute-start | bytes 393224 | tf_op jit(solution)/shard_map/ppermute | solution.py:203
  49.1 0.3 collective-permute-start.9
  49.4 1.7 %collective-permute-done.10.refs_8_ = bf16[2,128,256]{2,1,0:T(8,128)(2,1)S(1)} collective-permute-done((bf16[2,128,256]{2,1,0:T(8,128)(2,1)S(1)}, bf16[2,128,256]{2,1,0:T(8,128)(2,1)S(1)}, u32[]{:S(2)}, u32[]{:S(2)}) %collective-permute-start.10) | collective-permute-done | bytes 131104 | tf_op jit(solution)/shard_map/ppermute | solution.py:203
  51.0 0.7 copy-done.22
  51.7 2.8 %collective-permute-done.9.refs_7_ = bf16[2,128,256]{2,1,0:T(8,128)(2,1)} collective-permute-done((bf16[2,128,256]{2,1,0:T(8,128)(2,1)S(1)}, bf16[2,128,256]{2,1,0:T(8,128)(2,1)}, u32[]{:S(2)}, u32[]{:S(2)}) %collective-permute-start.9) | collective-permute-done | bytes 131104 | tf_op jit(solution)/shard_map/ppermute | solution.py:199
  54.5 1.3 copy-done.6
  55.8 24.9 %attention.1 = (bf16[32,128,256]{2,1,0:T(8,128)(2,1)}, bf16[4,128,256]{2,1,0:T(8,128)(2,1)}, bf16[4,128,256]{2,1,0:T(8,128)(2,1)}, bf16[4,128,256]{2,1,0:T(8,128...) custom-call(s32[2]{0:T(128)} %copy-done.4, ...), custom_call_target="tpu_custom_call" | custom-call | flops 6442450944 | bytes 8388608 | tf_op jit(solution)/shard_map/attention/pallas_call | solution.py:178
  80.7 0.3 collective-permute-start.15
  81.1 11.2 %all-to-all-start.1 = ((bf16[32,128,256]{2,1,0:T(8,128)(2,1)}), bf16[32,128,256]{2,1,0:T(8,128)(2,1)S(1)}, u32[]{:S(2)}, u32[]{:S(2)}) async-start(bf16[32,128,256]{2,1,0:T(8,128)(2,1)} %get-tuple-element.39), calls=%async_computation.1 | async-start | bytes 4194304 | tf_op jit(solution)/shard_map/all_to_all | solution.py:232
  92.4 1.6 %collective-permute-start.11 = (bf16[2,128,256]{2,1,0:T(8,128)(2,1)S(1)}, bf16[2,128,256]{2,1,0:T(8,128)(2,1)S(1)}, u32[]{:S(2)}, u32[]{:S(2)}) collective-permute-start(bf16[2,128,256]{2,1,0:T(8,128)(2,1)S(1)} %copy-done.21), channel_id=1, source_target_pairs={{0,16},{16,32},{32,48},{48,64},{64,80},{80,96},{96,112},{112,0},{1... | collective-permute-start | bytes 393224 | tf_op jit(solution)/shard_map/ppermute | solution.py:199
  94.0 1.3 collective-permute-start.16
  95.3 3.2 %collective-permute-done.11 = bf16[2,128,256]{2,1,0:T(8,128)(2,1)S(1)} collective-permute-done((bf16[2,128,256]{2,1,0:T(8,128)(2,1)S(1)}, bf16[2,128,256]{2,1,0:T(8,128)(2,1)S(1)}, u32[]{:S(2)}, u32[]{:S(2)}) %collective-permute-start.11) | collective-permute-done | bytes 131104 | tf_op jit(solution)/shard_map/ppermute | solution.py:199
  98.6 0.3 collective-permute-start.12
  99.0 2.5 %collective-permute-done.16 = bf16[4,128,256]{2,1,0:T(8,128)(2,1)S(1)} collective-permute-done((bf16[4,128,256]{2,1,0:T(8,128)(2,1)S(1)}, bf16[4,128,256]{2,1,0:T(8,128)(2,1)S(1)}, u32[]{:S(2)}, u32[]{:S(2)}) %collective-permute-start.16) | collective-permute-done | bytes 262176 | tf_op jit(solution)/shard_map/ppermute | solution.py:203
  101.5 2.5 %collective-permute-start.17 = (bf16[4,128,256]{2,1,0:T(8,128)(2,1)S(1)}, bf16[4,128,256]{2,1,0:T(8,128)(2,1)S(1)}, u32[]{:S(2)}, u32[]{:S(2)}) collective-permute-start(bf16[4,128,256]{2,1,0:T(8,128)(2,1)S(1)} %add_convert_fusion.1), channel_id=1, source_target_pairs={{0,112},{16,0},{32,16},{48,32},{64,48},{80,64},{96,80},{112,96},{1... | collective-permute-start | bytes 786440 | tf_op jit(solution)/shard_map/ppermute | solution.py:203
  104.0 2.6 %collective-permute-done.12 = bf16[4,128,256]{2,1,0:T(8,128)(2,1)S(1)} collective-permute-done((bf16[4,128,256]{2,1,0:T(8,128)(2,1)S(1)}, bf16[4,128,256]{2,1,0:T(8,128)(2,1)S(1)}, u32[]{:S(2)}, u32[]{:S(2)}) %collective-permute-start.12) | collective-permute-done | bytes 262176 | tf_op jit(solution)/shard_map/ppermute | solution.py:199
  106.7 0.1 collective-permute-start.13
  106.8 1.4 %collective-permute-done.17 = bf16[4,128,256]{2,1,0:T(8,128)(2,1)S(1)} collective-permute-done((bf16[4,128,256]{2,1,0:T(8,128)(2,1)S(1)}, bf16[4,128,256]{2,1,0:T(8,128)(2,1)S(1)}, u32[]{:S(2)}, u32[]{:S(2)}) %collective-permute-start.17) | collective-permute-done | bytes 262176 | tf_op jit(solution)/shard_map/ppermute | solution.py:203
  108.3 3.7 %collective-permute-start.18 = (bf16[4,128,256]{2,1,0:T(8,128)(2,1)S(1)}, bf16[4,128,256]{2,1,0:T(8,128)(2,1)S(1)}, u32[]{:S(2)}, u32[]{:S(2)}) collective-permute-start(bf16[4,128,256]{2,1,0:T(8,128)(2,1)S(1)} %add_convert_fusion), channel_id=1, source_target_pairs={{0,112},{16,0},{32,16},{48,32},{64,48},{80,64},{96,80},{112,96},{1... | collective-permute-start | bytes 786440 | tf_op jit(solution)/shard_map/ppermute | solution.py:203
  112.0 1.8 %collective-permute-done.13 = bf16[4,128,256]{2,1,0:T(8,128)(2,1)S(1)} collective-permute-done((bf16[4,128,256]{2,1,0:T(8,128)(2,1)S(1)}, bf16[4,128,256]{2,1,0:T(8,128)(2,1)S(1)}, u32[]{:S(2)}, u32[]{:S(2)}) %collective-permute-start.13) | collective-permute-done | bytes 262176 | tf_op jit(solution)/shard_map/ppermute | solution.py:199
  113.9 0.1 collective-permute-start.14
  114.0 1.3 %collective-permute-done.18 = bf16[4,128,256]{2,1,0:T(8,128)(2,1)S(1)} collective-permute-done((bf16[4,128,256]{2,1,0:T(8,128)(2,1)S(1)}, bf16[4,128,256]{2,1,0:T(8,128)(2,1)S(1)}, u32[]{:S(2)}, u32[]{:S(2)}) %collective-permute-start.18) | collective-permute-done | bytes 262176 | tf_op jit(solution)/shard_map/ppermute | solution.py:203
  115.4 5.1 %collective-permute-done.14 = bf16[4,128,256]{2,1,0:T(8,128)(2,1)S(1)} collective-permute-done((bf16[4,128,256]{2,1,0:T(8,128)(2,1)S(1)}, bf16[4,128,256]{2,1,0:T(8,128)(2,1)S(1)}, u32[]{:S(2)}, u32[]{:S(2)}) %collective-permute-start.14) | collective-permute-done | bytes 262176 | tf_op jit(solution)/shard_map/ppermute | solution.py:199
  120.4 0.2 all-to-all-done.1.tiles
  120.6 0.1 fusion.3
  120.7 6.4 %collective-permute-start.21 = (bf16[128,256]{1,0:T(8,128)(2,1)S(1)}, bf16[128,256]{1,0:T(8,128)(2,1)S(1)}, u32[]{:S(2)}, u32[]{:S(2)}) collective-permute-start(bf16[128,256]{1,0:T(8,128)(2,1)S(1)} %get-tuple-element.56), channel_id=1, source_target_pairs={{0,136},{8,128},{128,8},{136,0},{1,137},{9,129},{129,9},{137,1},{2... | collective-permute-start | bytes 196616 | tf_op jit(solution)/shard_map/ppermute | solution.py:208
  127.2 0.4 collective-permute-start.20
  127.5 0.1 collective-permute-start.19
  127.6 1.9 %join_heads.1 = (bf16[128,4096]{1,0:T(8,128)(2,1)}, bf16[128,4096]{1,0:T(8,128)(2,1)}) custom-call(bf16[32,128,256]{2,1,0:T(8,128)(2,1)S(1)} %all-to-all-done.1.tiles), custom_call_target="tpu_custom_call" | custom-call | tf_op jit(solution)/shard_map/join_heads/pallas_call | solution.py:90
  129.5 0.5 collective-permute-done.21.refs_3_
  130.0 1.7 %collective-permute-done.20.refs_2_ = bf16[128,256]{1,0:T(8,128)(2,1)S(1)} collective-permute-done((bf16[128,256]{1,0:T(8,128)(2,1)S(1)}, bf16[128,256]{1,0:T(8,128)(2,1)S(1)}, u32[]{:S(2)}, u32[]{:S(2)}) %collective-permute-start.20) | collective-permute-done | bytes 65568 | tf_op jit(solution)/shard_map/ppermute | solution.py:208
  131.8 1.3 join_kv.1
  (66 shorter events, 0.6 us)
Async XLA Ops:
  0.7 0.9 copy-start.2
  1.6 0.9 copy-start.3
  2.5 11.3 %copy-start.4 = (s32[2]{0:T(128)}, s32[2]{0:T(128)S(1)}, u32[]{:S(2)}) copy-start(s32[2]{0:T(128)S(1)} %pad_add_fusion.me_ref) | copy-start | bytes 28
  3.1 10.7 %collective-permute-start = (bf16[128,256]{1,0:T(8,128)(2,1)S(1)}, bf16[128,256]{1,0:T(8,128)(2,1)S(1)}, u32[]{:S(2)}, u32[]{:S(2)}) collective-permute-start(bf16[128,256]{1,0:T(8,128)(2,1)S(1)} %get-tuple-element.31), channel_id=1, source_target_pairs={{0,8},{8,0},{128,136},{136,128},{1,9},{9,1},{129,137},{137,129},{2... | collective-permute-start | bytes 196616 | tf_op jit(solution)/shard_map/ppermute | solution.py:208
  6.5 7.4 %collective-permute-start.1 = (bf16[128,256]{1,0:T(8,128)(2,1)S(1)}, bf16[128,256]{1,0:T(8,128)(2,1)S(1)}, u32[]{:S(2)}, u32[]{:S(2)}) collective-permute-start(bf16[128,256]{1,0:T(8,128)(2,1)S(1)} %get-tuple-element.32), channel_id=1, source_target_pairs={{0,128},{8,136},{128,0},{136,8},{1,129},{9,137},{129,1},{137,9},{2... | collective-permute-start | bytes 196616 | tf_op jit(solution)/shard_map/ppermute | solution.py:208
  7.5 6.4 %collective-permute-start.2 = (bf16[128,256]{1,0:T(8,128)(2,1)S(1)}, bf16[128,256]{1,0:T(8,128)(2,1)S(1)}, u32[]{:S(2)}, u32[]{:S(2)}) collective-permute-start(bf16[128,256]{1,0:T(8,128)(2,1)S(1)} %get-tuple-element.33), channel_id=1, source_target_pairs={{0,136},{8,128},{128,8},{136,0},{1,137},{9,129},{129,9},{137,1},{2... | collective-permute-start | bytes 196616 | tf_op jit(solution)/shard_map/ppermute | solution.py:208
  9.7 1.2 copy-start
  10.9 1.2 copy-start.1
  13.9 40.6 %all-to-all-start = ((bf16[32,128,256]{2,1,0:T(8,128)(2,1)}), bf16[32,128,256]{2,1,0:T(8,128)(2,1)S(1)}, u32[]{:S(2)}, u32[]{:S(2)}) async-start(bf16[32,128,256]{2,1,0:T(8,128)(2,1)} %split_heads.1), calls=%async_computation | async-start | bytes 4194304 | tf_op jit(solution)/shard_map/all_to_all | solution.py:232
  19.4 35.1 %copy-start.13 = (bf16[4,128,256]{2,1,0:T(8,128)(2,1)}, bf16[4,128,256]{2,1,0:T(8,128)(2,1)S(1)}, u32[]{:S(2)}) copy-start(bf16[4,128,256]{2,1,0:T(8,128)(2,1)S(1)} %pad_maximum_fusion.refs_0_) | copy-start | bytes 786436
  19.4 11.1 %collective-permute-start.4 = (bf16[4,128,256]{2,1,0:T(8,128)(2,1)S(1)}, bf16[4,128,256]{2,1,0:T(8,128)(2,1)S(1)}, u32[]{:S(2)}, u32[]{:S(2)}) collective-permute-start(bf16[4,128,256]{2,1,0:T(8,128)(2,1)S(1)} %pad_maximum_fusion.refs_0_), channel_id=1, source_target_pairs={{0,112},{16,0},{32,16},{48,32},{64,48},{80,64},{96,80},{112,96},{1... | collective-permute-start | bytes 786440 | tf_op jit(solution)/shard_map/ppermute | solution.py:203
  25.1 8.9 %collective-permute-start.3 = (bf16[4,128,256]{2,1,0:T(8,128)(2,1)S(1)}, bf16[4,128,256]{2,1,0:T(8,128)(2,1)S(1)}, u32[]{:S(2)}, u32[]{:S(2)}) collective-permute-start(bf16[4,128,256]{2,1,0:T(8,128)(2,1)S(1)} %pad_maximum_fusion.refs_0_), channel_id=1, source_target_pairs={{0,16},{16,32},{32,48},{48,64},{64,80},{80,96},{96,112},{112,0},{1... | collective-permute-start | bytes 786440 | tf_op jit(solution)/shard_map/ppermute | solution.py:199
  30.6 23.9 %copy-start.17 = (bf16[4,128,256]{2,1,0:T(8,128)(2,1)}, bf16[4,128,256]{2,1,0:T(8,128)(2,1)S(1)}, u32[]{:S(2)}) copy-start(bf16[4,128,256]{2,1,0:T(8,128)(2,1)S(1)} %collective-permute-done.4.refs_2_) | copy-start | bytes 786436
  30.6 8.0 %collective-permute-start.6 = (bf16[4,128,256]{2,1,0:T(8,128)(2,1)S(1)}, bf16[4,128,256]{2,1,0:T(8,128)(2,1)S(1)}, u32[]{:S(2)}, u32[]{:S(2)}) collective-permute-start(bf16[4,128,256]{2,1,0:T(8,128)(2,1)S(1)} %collective-permute-done.4.refs_2_), channel_id=1, source_target_pairs={{0,112},{16,0},{32,16},{48,32},{64,48},{80,64},{96,80},{112,96},{1... | collective-permute-start | bytes 786440 | tf_op jit(solution)/shard_map/ppermute | solution.py:203
  34.0 20.5 %copy-start.18 = (bf16[4,128,256]{2,1,0:T(8,128)(2,1)}, bf16[4,128,256]{2,1,0:T(8,128)(2,1)S(1)}, u32[]{:S(2)}) copy-start(bf16[4,128,256]{2,1,0:T(8,128)(2,1)S(1)} %collective-permute-done.3.refs_1_) | copy-start | bytes 786436
  34.0 8.0 %collective-permute-start.5 = (bf16[4,128,256]{2,1,0:T(8,128)(2,1)S(1)}, bf16[4,128,256]{2,1,0:T(8,128)(2,1)S(1)}, u32[]{:S(2)}, u32[]{:S(2)}) collective-permute-start(bf16[4,128,256]{2,1,0:T(8,128)(2,1)S(1)} %collective-permute-done.3.refs_1_), channel_id=1, source_target_pairs={{0,16},{16,32},{32,48},{48,64},{64,80},{80,96},{96,112},{112,0},{1... | collective-permute-start | bytes 786440 | tf_op jit(solution)/shard_map/ppermute | solution.py:199
  38.5 3.4 %copy-start.19 = (bf16[4,128,256]{2,1,0:T(8,128)(2,1)}, bf16[4,128,256]{2,1,0:T(8,128)(2,1)S(1)}, u32[]{:S(2)}) copy-start(bf16[4,128,256]{2,1,0:T(8,128)(2,1)S(1)} %collective-permute-done.6.refs_4_) | copy-start | bytes 786436
  38.5 7.0 %collective-permute-start.8 = (bf16[4,128,256]{2,1,0:T(8,128)(2,1)S(1)}, bf16[4,128,256]{2,1,0:T(8,128)(2,1)S(1)}, u32[]{:S(2)}, u32[]{:S(2)}) collective-permute-start(bf16[4,128,256]{2,1,0:T(8,128)(2,1)S(1)} %collective-permute-done.6.refs_4_), channel_id=1, source_target_pairs={{0,112},{16,0},{32,16},{48,32},{64,48},{80,64},{96,80},{112,96},{1... | collective-permute-start | bytes 786440 | tf_op jit(solution)/shard_map/ppermute | solution.py:203
  42.0 7.1 %copy-start.20 = (bf16[4,128,256]{2,1,0:T(8,128)(2,1)}, bf16[4,128,256]{2,1,0:T(8,128)(2,1)S(1)}, u32[]{:S(2)}) copy-start(bf16[4,128,256]{2,1,0:T(8,128)(2,1)S(1)} %collective-permute-done.5.refs_3_) | copy-start | bytes 786436
  42.0 7.1 %collective-permute-start.7 = (bf16[4,128,256]{2,1,0:T(8,128)(2,1)S(1)}, bf16[4,128,256]{2,1,0:T(8,128)(2,1)S(1)}, u32[]{:S(2)}, u32[]{:S(2)}) collective-permute-start(bf16[4,128,256]{2,1,0:T(8,128)(2,1)S(1)} %collective-permute-done.5.refs_3_), channel_id=1, source_target_pairs={{0,16},{16,32},{32,48},{48,64},{64,80},{80,96},{96,112},{112,0},{1... | collective-permute-start | bytes 786440 | tf_op jit(solution)/shard_map/ppermute | solution.py:199
  45.6 9.0 %copy-start.15 = (bf16[4,128,256]{2,1,0:T(8,128)(2,1)}, bf16[4,128,256]{2,1,0:T(8,128)(2,1)S(1)}, u32[]{:S(2)}) copy-start(bf16[4,128,256]{2,1,0:T(8,128)(2,1)S(1)} %collective-permute-done.8.refs_6_) | copy-start | bytes 786436
  45.6 5.4 %collective-permute-start.10 = (bf16[2,128,256]{2,1,0:T(8,128)(2,1)S(1)}, bf16[2,128,256]{2,1,0:T(8,128)(2,1)S(1)}, u32[]{:S(2)}, u32[]{:S(2)}) collective-permute-start(bf16[2,128,256]{2,1,0:T(8,128)(2,1)S(1)} %slice.73), channel_id=1, source_target_pairs={{0,112},{16,0},{32,16},{48,32},{64,48},{80,64},{96,80},{112,96},{1... | collective-permute-start | bytes 393224 | tf_op jit(solution)/shard_map/ppermute | solution.py:203
  49.1 5.5 %copy-start.16 = (bf16[4,128,256]{2,1,0:T(8,128)(2,1)}, bf16[4,128,256]{2,1,0:T(8,128)(2,1)S(1)}, u32[]{:S(2)}) copy-start(bf16[4,128,256]{2,1,0:T(8,128)(2,1)S(1)} %collective-permute-done.7.refs_5_) | copy-start | bytes 786436
  49.1 5.4 %collective-permute-start.9 = (bf16[2,128,256]{2,1,0:T(8,128)(2,1)S(1)}, bf16[2,128,256]{2,1,0:T(8,128)(2,1)}, u32[]{:S(2)}, u32[]{:S(2)}) collective-permute-start(bf16[2,128,256]{2,1,0:T(8,128)(2,1)S(1)} %slice.72), channel_id=1, source_target_pairs={{0,16},{16,32},{32,48},{48,64},{64,80},{80,96},{96,112},{112,0},{1... | collective-permute-start | bytes 393224 | tf_op jit(solution)/shard_map/ppermute | solution.py:199
  51.0 0.7 copy-start.22
  54.5 1.3 %copy-start.6 = (bf16[32,128,256]{2,1,0:T(8,128)(2,1)}, bf16[32,128,256]{2,1,0:T(8,128)(2,1)S(1)}, u32[]{:S(2)}) copy-start(bf16[32,128,256]{2,1,0:T(8,128)(2,1)S(1)} %all-to-all-done.qd_ref) | copy-start | bytes 6291460
  80.7 13.2 %collective-permute-start.15 = (bf16[2,128,256]{2,1,0:T(8,128)(2,1)}, bf16[2,128,256]{2,1,0:T(8,128)(2,1)S(1)}, u32[]{:S(2)}, u32[]{:S(2)}) collective-permute-start(bf16[2,128,256]{2,1,0:T(8,128)(2,1)} %get-tuple-element.47), channel_id=1, source_target_pairs={{0,112},{16,0},{32,16},{48,32},{64,48},{80,64},{96,80},{112,96},{1... | collective-permute-start | bytes 393224 | tf_op jit(solution)/shard_map/ppermute | solution.py:203
  81.1 11.2 %copy-start.11 = (bf16[4,128,256]{2,1,0:T(8,128)(2,1)S(1)}, bf16[4,128,256]{2,1,0:T(8,128)(2,1)}, u32[]{:S(2)}) copy-start(bf16[4,128,256]{2,1,0:T(8,128)(2,1)} %get-tuple-element.42) | copy-start | bytes 786436
  81.1 11.3 %copy-start.12 = (bf16[4,128,256]{2,1,0:T(8,128)(2,1)S(1)}, bf16[4,128,256]{2,1,0:T(8,128)(2,1)}, u32[]{:S(2)}) copy-start(bf16[4,128,256]{2,1,0:T(8,128)(2,1)} %get-tuple-element.46) | copy-start | bytes 786436
  81.1 11.3 %copy-start.21 = (bf16[2,128,256]{2,1,0:T(8,128)(2,1)S(1)}, bf16[2,128,256]{2,1,0:T(8,128)(2,1)}, u32[]{:S(2)}) copy-start(bf16[2,128,256]{2,1,0:T(8,128)(2,1)} %get-tuple-element.43) | copy-start | bytes 393220
  81.1 39.5 %all-to-all-start.1 = ((bf16[32,128,256]{2,1,0:T(8,128)(2,1)}), bf16[32,128,256]{2,1,0:T(8,128)(2,1)S(1)}, u32[]{:S(2)}, u32[]{:S(2)}) async-start(bf16[32,128,256]{2,1,0:T(8,128)(2,1)} %get-tuple-element.39), calls=%async_computation.1 | async-start | bytes 4194304 | tf_op jit(solution)/shard_map/all_to_all | solution.py:232
  92.3 9.2 %copy-start.10 = (bf16[4,128,256]{2,1,0:T(8,128)(2,1)S(1)}, bf16[4,128,256]{2,1,0:T(8,128)(2,1)}, u32[]{:S(2)}) copy-start(bf16[4,128,256]{2,1,0:T(8,128)(2,1)} %get-tuple-element.45) | copy-start | bytes 786436
  92.3 14.4 %copy-start.9 = (bf16[4,128,256]{2,1,0:T(8,128)(2,1)S(1)}, bf16[4,128,256]{2,1,0:T(8,128)(2,1)}, u32[]{:S(2)}) copy-start(bf16[4,128,256]{2,1,0:T(8,128)(2,1)} %get-tuple-element.41) | copy-start | bytes 786436
  92.3 16.0 %copy-start.8 = (bf16[4,128,256]{2,1,0:T(8,128)(2,1)S(1)}, bf16[4,128,256]{2,1,0:T(8,128)(2,1)}, u32[]{:S(2)}) copy-start(bf16[4,128,256]{2,1,0:T(8,128)(2,1)} %get-tuple-element.44) | copy-start | bytes 786436
  92.4 21.5 %copy-start.7 = (bf16[4,128,256]{2,1,0:T(8,128)(2,1)S(1)}, bf16[4,128,256]{2,1,0:T(8,128)(2,1)}, u32[]{:S(2)}) copy-start(bf16[4,128,256]{2,1,0:T(8,128)(2,1)} %get-tuple-element.40) | copy-start | bytes 786436
  92.4 6.2 %collective-permute-start.11 = (bf16[2,128,256]{2,1,0:T(8,128)(2,1)S(1)}, bf16[2,128,256]{2,1,0:T(8,128)(2,1)S(1)}, u32[]{:S(2)}, u32[]{:S(2)}) collective-permute-start(bf16[2,128,256]{2,1,0:T(8,128)(2,1)S(1)} %copy-done.21), channel_id=1, source_target_pairs={{0,16},{16,32},{32,48},{48,64},{64,80},{80,96},{96,112},{112,0},{1... | collective-permute-start | bytes 393224 | tf_op jit(solution)/shard_map/ppermute | solution.py:199
  94.0 26.6 %copy-start.14 = (bf16[4,128,256]{2,1,0:T(8,128)(2,1)S(1)}, bf16[4,128,256]{2,1,0:T(8,128)(2,1)}, u32[]{:S(2)}) copy-start(bf16[4,128,256]{2,1,0:T(8,128)(2,1)} %get-tuple-element.51) | copy-start | bytes 786436
  94.0 7.4 %collective-permute-start.16 = (bf16[4,128,256]{2,1,0:T(8,128)(2,1)S(1)}, bf16[4,128,256]{2,1,0:T(8,128)(2,1)S(1)}, u32[]{:S(2)}, u32[]{:S(2)}) collective-permute-start(bf16[4,128,256]{2,1,0:T(8,128)(2,1)S(1)} %pad_maximum_fusion.2), channel_id=1, source_target_pairs={{0,112},{16,0},{32,16},{48,32},{64,48},{80,64},{96,80},{112,96},{1... | collective-permute-start | bytes 786440 | tf_op jit(solution)/shard_map/ppermute | solution.py:203
  98.6 8.0 %collective-permute-start.12 = (bf16[4,128,256]{2,1,0:T(8,128)(2,1)S(1)}, bf16[4,128,256]{2,1,0:T(8,128)(2,1)S(1)}, u32[]{:S(2)}, u32[]{:S(2)}) collective-permute-start(bf16[4,128,256]{2,1,0:T(8,128)(2,1)S(1)} %pad_maximum_fusion.1), channel_id=1, source_target_pairs={{0,16},{16,32},{32,48},{48,64},{64,80},{80,96},{96,112},{112,0},{1... | collective-permute-start | bytes 786440 | tf_op jit(solution)/shard_map/ppermute | solution.py:199
  101.5 6.7 %collective-permute-start.17 = (bf16[4,128,256]{2,1,0:T(8,128)(2,1)S(1)}, bf16[4,128,256]{2,1,0:T(8,128)(2,1)S(1)}, u32[]{:S(2)}, u32[]{:S(2)}) collective-permute-start(bf16[4,128,256]{2,1,0:T(8,128)(2,1)S(1)} %add_convert_fusion.1), channel_id=1, source_target_pairs={{0,112},{16,0},{32,16},{48,32},{64,48},{80,64},{96,80},{112,96},{1... | collective-permute-start | bytes 786440 | tf_op jit(solution)/shard_map/ppermute | solution.py:203
  106.7 7.1 %collective-permute-start.13 = (bf16[4,128,256]{2,1,0:T(8,128)(2,1)S(1)}, bf16[4,128,256]{2,1,0:T(8,128)(2,1)S(1)}, u32[]{:S(2)}, u32[]{:S(2)}) collective-permute-start(bf16[4,128,256]{2,1,0:T(8,128)(2,1)S(1)} %add_convert_fusion.3), channel_id=1, source_target_pairs={{0,16},{16,32},{32,48},{48,64},{64,80},{80,96},{96,112},{112,0},{1... | collective-permute-start | bytes 786440 | tf_op jit(solution)/shard_map/ppermute | solution.py:199
  108.3 23.5 %copy-start.5 = (s32[2]{0:T(128)S(1)}, s32[2]{0:T(128)}, u32[]{:S(2)}) copy-start(s32[2]{0:T(128)} %copy-done.4) | copy-start | bytes 28
  108.3 7.0 %collective-permute-start.18 = (bf16[4,128,256]{2,1,0:T(8,128)(2,1)S(1)}, bf16[4,128,256]{2,1,0:T(8,128)(2,1)S(1)}, u32[]{:S(2)}, u32[]{:S(2)}) collective-permute-start(bf16[4,128,256]{2,1,0:T(8,128)(2,1)S(1)} %add_convert_fusion), channel_id=1, source_target_pairs={{0,112},{16,0},{32,16},{48,32},{64,48},{80,64},{96,80},{112,96},{1... | collective-permute-start | bytes 786440 | tf_op jit(solution)/shard_map/ppermute | solution.py:203
  113.9 6.5 %collective-permute-start.14 = (bf16[4,128,256]{2,1,0:T(8,128)(2,1)S(1)}, bf16[4,128,256]{2,1,0:T(8,128)(2,1)S(1)}, u32[]{:S(2)}, u32[]{:S(2)}) collective-permute-start(bf16[4,128,256]{2,1,0:T(8,128)(2,1)S(1)} %add_convert_fusion.2), channel_id=1, source_target_pairs={{0,16},{16,32},{32,48},{48,64},{64,80},{80,96},{96,112},{112,0},{1... | collective-permute-start | bytes 786440 | tf_op jit(solution)/shard_map/ppermute | solution.py:199
  120.7 9.3 %collective-permute-start.21 = (bf16[128,256]{1,0:T(8,128)(2,1)S(1)}, bf16[128,256]{1,0:T(8,128)(2,1)S(1)}, u32[]{:S(2)}, u32[]{:S(2)}) collective-permute-start(bf16[128,256]{1,0:T(8,128)(2,1)S(1)} %get-tuple-element.56), channel_id=1, source_target_pairs={{0,136},{8,128},{128,8},{136,0},{1,137},{9,129},{129,9},{137,1},{2... | collective-permute-start | bytes 196616 | tf_op jit(solution)/shard_map/ppermute | solution.py:208
  127.2 4.6 %collective-permute-start.20 = (bf16[128,256]{1,0:T(8,128)(2,1)S(1)}, bf16[128,256]{1,0:T(8,128)(2,1)S(1)}, u32[]{:S(2)}, u32[]{:S(2)}) collective-permute-start(bf16[128,256]{1,0:T(8,128)(2,1)S(1)} %get-tuple-element.57), channel_id=1, source_target_pairs={{0,128},{8,136},{128,0},{136,8},{1,129},{9,137},{129,1},{137,9},{2... | collective-permute-start | bytes 196616 | tf_op jit(solution)/shard_map/ppermute | solution.py:208
  127.5 4.3 %collective-permute-start.19 = (bf16[128,256]{1,0:T(8,128)(2,1)S(1)}, bf16[128,256]{1,0:T(8,128)(2,1)S(1)}, u32[]{:S(2)}, u32[]{:S(2)}) collective-permute-start(bf16[128,256]{1,0:T(8,128)(2,1)S(1)} %get-tuple-element.58), channel_id=1, source_target_pairs={{0,8},{8,0},{128,136},{136,128},{1,9},{9,1},{129,137},{137,129},{2... | collective-permute-start | bytes 196616 | tf_op jit(solution)/shard_map/ppermute | solution.py:208

commit v4 on v3

v4 whole, which is shorter than its diff:
```python
import math

import jax
import jax.numpy as jnp
from jax import lax
from jax.experimental import pallas as pl
from jax.experimental.pallas import tpu as pltpu
from jax.sharding import Mesh, PartitionSpec as P

HEAD_DIM = 128
BLOCK = 128
SPANS = 8
PLANES = 8
PLANE = ("head", "xhi", "core")
QUAD = ("xhi", "core")
FACTOR = 1.0 / math.sqrt(HEAD_DIM)
LOG2E = math.log2(math.e)
UNROLL = 8
VMEM_MIB, SMALL_MIB = 60, 8
WIDE = 2 * HEAD_DIM
BF16, F32 = jnp.bfloat16, jnp.float32
SMEM = pl.BlockSpec(memory_space=pltpu.SMEM)
VMEM = pl.BlockSpec(memory_space=pltpu.VMEM)


def nt(a, b):
    return lax.dot_general(a, b, (((1,), (1,)), ((), ())), preferred_element_type=F32)


def nn(a, b):
    return lax.dot_general(a, b, (((1,), (0,)), ((), ())), preferred_element_type=F32)


def columns(block):
    return pl.ds(pl.multiple_of(block * HEAD_DIM, HEAD_DIM), HEAD_DIM)


def call(kernel, name, in_specs, shapes, scratch=(), out_specs=None, **params):
    return pl.pallas_call(
        kernel,
        out_shape=tuple(jax.ShapeDtypeStruct(shape, BF16) for shape in shapes),
        in_specs=in_specs,
        out_specs=tuple(out_specs or [VMEM for _ in shapes]),
        scratch_shapes=scratch,
        name=name,
        compiler_params=pltpu.CompilerParams(vmem_limit_bytes=(SMALL_MIB if name.startswith("join") else VMEM_MIB) * 2**20),
        **params,
    )


def split_kv(me, key, value):
    def kernel(me_ref, key_ref, value_ref, *tiles):
        for t, tile in enumerate(tiles):
            tile[:, :HEAD_DIM] = key_ref[:, columns(me_ref[0] ^ t)]
            tile[:, HEAD_DIM:] = value_ref[:, columns(me_ref[0] ^ t)]

    return call(kernel, "split_kv", [SMEM, VMEM, VMEM], [(BLOCK, WIDE)] * 4)(me, key, value)


def join_kv(me, tiles):
    def kernel(me_ref, *refs):
        *tiles, key_ref, value_ref = refs
        for t, tile in enumerate(tiles):
            key_ref[:, columns(me_ref[0] ^ t)] = tile[:, :HEAD_DIM]
            value_ref[:, columns(me_ref[0] ^ t)] = tile[:, HEAD_DIM:]

    return call(kernel, "join_kv", [SMEM] + [VMEM] * 4, [(BLOCK, 4 * HEAD_DIM)] * 2)(me, *tiles)


def split_heads(query, d_out):
    heads = query.shape[1] // HEAD_DIM

    def kernel(query_ref, d_out_ref, tiles):
        for h in range(heads):
            tiles[h, :, :HEAD_DIM] = query_ref[:, columns(h)]
            tiles[h, :, HEAD_DIM:] = d_out_ref[:, columns(h)]

    return call(kernel, "split_heads", [VMEM] * 2, [(heads, BLOCK, WIDE)])(query, d_out)[0]


def join_heads(tiles):
    heads = tiles.shape[0]

    def kernel(tiles, attn_ref, grad_ref):
        for h in range(heads):
            attn_ref[:, columns(h)] = tiles[h, :, :HEAD_DIM]
            grad_ref[:, columns(h)] = tiles[h, :, HEAD_DIM:]

    return call(kernel, "join_heads", [VMEM], [(BLOCK, heads * HEAD_DIM)] * 2)(tiles)


def plus(*terms):
    return sum(term.astype(F32) for term in terms).astype(BF16)


def attention_kernel(me_ref, seg_ref, spans_ref, qd_ref, *refs):
    keys_in, values_in, od_ref = refs[:PLANES], refs[PLANES : 2 * PLANES], refs[2 * PLANES]
    key_parts, value_parts = refs[2 * PLANES + 1 : 3 * PLANES + 1], refs[3 * PLANES + 1 : 4 * PLANES + 1]
    k_ref, v_ref, kt_ref, vt_ref, dk_ref, dv_ref = refs[4 * PLANES + 1 :]
    quad, z = me_ref[0], me_ref[1]

    @pl.when(pl.program_id(0) == 0)
    def _():
        for o in range(PLANES):

            @pl.loop(0, 4, unroll=True)
            def _(t):
                for piece, held, turned, total in (
                    (keys_in[o], k_ref, kt_ref, dk_ref),
                    (values_in[o], v_ref, vt_ref, dv_ref),
                ):
                    tile = piece[t]
                    held[4 * o + t] = tile
                    turned[4 * o + t] = tile.T
                    total[4 * o + t] = jnp.zeros((BLOCK, HEAD_DIM), F32)

    def one_block(u):
        s = pl.program_id(0) * UNROLL + u
        head, xhi, core = s // 4, (s // 2) % 2, s % 2
        seg = seg_ref[(xhi * 16 + z * 2 + core) * 8 + head]
        locs = []
        for j in range(SPANS):
            d = spans_ref[j, seg]
            away = ((d // 2) % 8 - z) & 7
            locs.append(away * 4 + (((d // 16) * 2 + d % 2) ^ quad))
        q, do = qd_ref[u, :, :HEAD_DIM], qd_ref[u, :, HEAD_DIM:]
        keys = jnp.concatenate([k_ref[loc] for loc in locs], axis=0)
        scores = nt(keys, q)
        values = jnp.concatenate([v_ref[loc] for loc in locs], axis=0)
        yield
        dprob = nt(values, do)
        top = jnp.max(scores, axis=0, keepdims=True)
        expo = jnp.exp2((scores - top) * (FACTOR * LOG2E))
        prob = expo * (1.0 / jnp.sum(expo, axis=0, keepdims=True))
        prob_b = prob.astype(BF16)
        value_t = jnp.concatenate([vt_ref[loc] for loc in locs], axis=1)
        yield
        attn_t = nn(value_t, prob_b)
        yield
        value_slots = nn(prob_b, do)
        od_ref[u, :, :HEAD_DIM] = attn_t.T.astype(BF16)
        delta = jnp.sum(do.astype(F32).T * attn_t, axis=0, keepdims=True)
        dscore_b = (prob * (dprob - delta)).astype(BF16)
        key_t = jnp.concatenate([kt_ref[loc] for loc in locs], axis=1)
        yield
        dq_t = nn(key_t, dscore_b) * FACTOR
        key_slots = nn(dscore_b, q)
        yield
        od_ref[u, :, HEAD_DIM:] = dq_t.T.astype(BF16)
        for j in range(SPANS):
            rows = slice(j * BLOCK, (j + 1) * BLOCK)
            dk_ref[locs[j]] += key_slots[rows]
            dv_ref[locs[j]] += value_slots[rows]

    live = [one_block(u) for u in range(UNROLL)]
    while live:
        live = [block for block in live if next(block, True) is None]

    @pl.when(pl.program_id(0) == pl.num_programs(0) - 1)
    def _():
        for o in range(PLANES):

            @pl.loop(0, 4)
            def _(t):
                key_parts[o][t] = (dk_ref[4 * o + t] * FACTOR).astype(BF16)
                value_parts[o][t] = dv_ref[4 * o + t].astype(BF16)


def attention(me, seg_map, spans_t, qd, keys, values):
    cad_blocks, doc_blocks = qd.shape[0], 4 * PLANES
    step = pl.BlockSpec((UNROLL, BLOCK, WIDE), lambda i: (i, 0, 0))
    square = (doc_blocks, BLOCK, HEAD_DIM)
    od, *parts = call(
        attention_kernel,
        "attention",
        [SMEM] * 3 + [step] + [VMEM] * 2 * PLANES,
        [qd.shape] + [(4, BLOCK, HEAD_DIM)] * 2 * PLANES,
        [pltpu.VMEM(square, BF16)] * 4 + [pltpu.VMEM(square, F32)] * 2,
        [step] + [VMEM] * 2 * PLANES,
        grid=(cad_blocks // UNROLL,),
        cost_estimate=pl.CostEstimate(
            flops=cad_blocks * SPANS * 12 * BLOCK * BLOCK * HEAD_DIM,
            bytes_accessed=2 * (2 * qd.size + 4 * doc_blocks * BLOCK * HEAD_DIM),
            transcendentals=cad_blocks * SPANS * BLOCK * BLOCK,
        ),
    )(me, seg_map, spans_t, qd, *keys, *values)
    return od, parts[:PLANES], parts[PLANES:]


def up(array):
    return lax.ppermute(array, "z", [(i, (i + 1) % PLANES) for i in range(PLANES)])


def down(array):
    return lax.ppermute(array, "z", [(i, (i - 1) % PLANES) for i in range(PLANES)])


def exchange(tiles):
    return [tiles[0]] + [
        lax.ppermute(tiles[t], QUAD, [(i, i ^ t) for i in range(4)]) for t in (1, 2, 3)
    ]


def relay(own, move, steps):
    held = [own]
    for _ in range(steps):
        held.append(move(held[-1]))
    return held


def gather_z(own, ups):
    rising, falling = relay(own, up, ups), relay(own, down, PLANES - 1 - ups)
    return falling + rising[:0:-1]


def collect(parts, move):
    total = move(parts[0])
    for part in parts[1:]:
        total = move(plus(part, total))
    return total


def scatter_z(parts, ups):
    return parts[0], collect(parts[ups:0:-1], up), collect(parts[ups + 1 :], down)


def swap(array):
    return lax.all_to_all(array, PLANE, split_axis=0, concat_axis=0, tiled=True)


def body(query, key, value, d_out, seg_map, spans):
    me = jnp.stack([lax.axis_index(QUAD), lax.axis_index("z")]).astype(jnp.int32)
    tiles = exchange(split_kv(me, key, value))
    qd, tiles = lax.optimization_barrier((split_heads(query, d_out), tiles))
    own_keys = jnp.stack([tile[:, :HEAD_DIM] for tile in tiles])
    own_values = jnp.stack([tile[:, HEAD_DIM:] for tile in tiles])
    qd, keys, values = swap(qd), gather_z(own_keys, 4), gather_z(own_values, 3)
    od, key_parts, value_parts = attention(me, seg_map, spans.T, qd, keys, values)
    od = swap(od)
    sums = scatter_z(key_parts, 4), scatter_z(value_parts, 3)
    tiles = [jnp.concatenate([plus(*(x[t] for x in s)) for s in sums], axis=1) for t in range(4)]
    od, tiles = lax.optimization_barrier((od, tiles))
    attn_out, d_query = join_heads(od)
    d_key, d_value = join_kv(me, exchange(tiles))
    return attn_out, d_query, d_key, d_value


def solution(mesh):
    fine = Mesh(mesh.devices.reshape(2, PLANES, 2, 8), ("xhi", "z", "core", "head"))
    blk = ("xhi", "z", "core")
    rows, tiles = P((*blk, "head"), None), P(blk, "head")
    return jax.shard_map(
        body,
        mesh=fine,
        in_specs=(rows, tiles, tiles, rows, P(), P()),
        out_specs=(rows, rows, tiles, tiles),
        check_vma=False,
    )
```

time: 133 us -> 126 us (0.947)
  waiting for transfers between devices: 38.6 us -> 21.6 us
  starting transfers between devices: 56.3 us -> 65.4 us
  local copies, waits for them, and re-layouts: 6.31 us -> 2.04 us
  Pallas kernels: 30.4 us -> 33.4 us
    ppermute x8 -> x14, waiting for transfers between devices: 20.6 us -> 6.28 us  [down(): lax.ppermute(array, 'z', [(i, (i - 1) % PLANES) for i in range(PLANES)])]
    ppermute x8 -> x14, starting transfers between devices: 23.8 us -> 35.4 us  [down(): lax.ppermute(array, 'z', [(i, (i - 1) % PLANES) for i in range(PLANES)])]
    ppermute x8 -> x14, waiting for transfers between devices: 15.6 us -> 8.19 us  [up(): lax.ppermute(array, 'z', [(i, (i + 1) % PLANES) for i in range(PLANES)])]
    unnamed x46 -> x66, local copies, waits for them, and re-layouts: 6.27 us -> 1.99 us
    ppermute x6, starting transfers between devices: 13.5 us -> 10.1 us  [exchange(): lax.ppermute(tiles[t], QUAD, [(i, i ^ t) for i in range(4)])]
    all_to_all x2, waiting for transfers between devices: 0.21 us -> 3.2 us  [swap(): return lax.all_to_all(array, PLANE, split_axis=0, concat_axis=0, tiled=True)]
    ppermute x6, waiting for transfers between devices: 2.24 us -> 3.91 us  [exchange(): lax.ppermute(tiles[t], QUAD, [(i, i ^ t) for i in range(4)])]
    pallas_call x1, Pallas kernels: 1.69 us -> 3.22 us  [split_heads(): call(kernel, 'split_heads', [VMEM] * 2, [(heads, BLOCK, WIDE)])]
  transfers between devices with their start and end apart: 24 -> 36, of which waited for: 15 -> 13; matrix products, arithmetic and copies ran while one was open for 0% -> 1% of each run, Pallas kernels for 3% -> 4%
where the time goes in v4:
time: 126 us; the launch traced here: 125 us
  starting transfers between devices  65.4 us (52%)
  Pallas kernels  33.4 us (27%)
  waiting for transfers between devices  21.6 us (17%)
  local copies, waits for them, and re-layouts  2.04 us (2%)
    ppermute x14, starting transfers between devices, down(): lax.ppermute(array, 'z', [(i, (i - 1) % PLANES) for i in range(PLANES)])  35.4 us
    pallas_call x1, Pallas kernels, attention(): call(attention_kernel, 'attention', [SMEM] * 3 + [step] + [VMEM] * 2 * PL...  25.3 us
    all_to_all x2, starting transfers between devices, swap(): return lax.all_to_all(array, PLANE, split_axis=0, concat_axis=0, tiled=True)  16.3 us
    ppermute x6, starting transfers between devices, exchange(): lax.ppermute(tiles[t], QUAD, [(i, i ^ t) for i in range(4)])  10.1 us
    ppermute x14, waiting for transfers between devices, up(): lax.ppermute(array, 'z', [(i, (i + 1) % PLANES) for i in range(PLANES)])  8.19 us
    ppermute x14, waiting for transfers between devices, down(): lax.ppermute(array, 'z', [(i, (i - 1) % PLANES) for i in range(PLANES)])  6.28 us
    ppermute x6, waiting for transfers between devices, exchange(): lax.ppermute(tiles[t], QUAD, [(i, i ^ t) for i in range(4)])  3.91 us
    ppermute x14, starting transfers between devices, up(): lax.ppermute(array, 'z', [(i, (i + 1) % PLANES) for i in range(PLANES)])  3.64 us
  transfers between devices with their start and end apart: 36, of which 13 were waited for; matrix products, arithmetic and copies ran while one was open for 1% of the time, Pallas kernels for 4%

profile of v4, /device:TPU:1, one launch (start us, length us, event | category | flops | bytes accessed | tf_op | source)
XLA Modules:
  0.0 124.8 jit_solution(17080798797713250374)
XLA Ops:
  0.6 0.6 pad_add_fusion.me_ref
  1.2 1.7 %split_kv.1 = (bf16[128,256]{1,0:T(8,128)(2,1)}, bf16[128,256]{1,0:T(8,128)(2,1)}, bf16[128,256]{1,0:T(8,128)(2,1)}, bf16[128,256]{1,0:T(8,128)(2,1)}) custom-call(s32[2]{0:T(128)} %pad_add_fusion.me_ref, bf16[128,512]{1,0:T(8,128)(2,1)} %key_ref.1, bf16[128,512]{1,0:T(8,128)(2,1)} %value_ref.1), custom_call_target="tpu_custom_call" | custom-call | tf_op jit(solution)/shard_map/split_kv/pallas_call | solution.py:57
  3.0 3.2 %collective-permute-start = (bf16[128,256]{1,0:T(8,128)(2,1)}, bf16[128,256]{1,0:T(8,128)(2,1)S(1)}, u32[]{:S(2)}, u32[]{:S(2)}) collective-permute-start(bf16[128,256]{1,0:T(8,128)(2,1)} %get-tuple-element.40), channel_id=1, source_target_pairs={{0,8},{8,0},{128,136},{136,128},{1,9},{9,1},{129,137},{137,129},{2... | collective-permute-start | bytes 196616 | tf_op jit(solution)/shard_map/ppermute | solution.py:200
  6.2 1.0 collective-permute-start.1
  7.2 2.2 %collective-permute-start.2 = (bf16[128,256]{1,0:T(8,128)(2,1)}, bf16[128,256]{1,0:T(8,128)(2,1)S(1)}, u32[]{:S(2)}, u32[]{:S(2)}) collective-permute-start(bf16[128,256]{1,0:T(8,128)(2,1)} %get-tuple-element.42), channel_id=1, source_target_pairs={{0,136},{8,128},{128,8},{136,0},{1,137},{9,129},{129,9},{137,1},{2... | collective-permute-start | bytes 196616 | tf_op jit(solution)/shard_map/ppermute | solution.py:200
  9.4 3.2 %split_heads.1 = bf16[32,128,256]{2,1,0:T(8,128)(2,1)} custom-call(bf16[128,4096]{1,0:T(8,128)(2,1)} %query_ref.1, bf16[128,4096]{1,0:T(8,128)(2,1)} %d_out_ref.1), custom_call_target="tpu_custom_call" | custom-call | tf_op jit(solution)/shard_map/split_heads/pallas_call | solution.py:78
  12.6 0.6 collective-permute-done.2
  13.2 5.7 %all-to-all-start = ((bf16[32,128,256]{2,1,0:T(8,128)(2,1)}), bf16[32,128,256]{2,1,0:T(8,128)(2,1)S(1)}, u32[]{:S(2)}, u32[]{:S(2)}) async-start(bf16[32,128,256]{2,1,0:T(8,128)(2,1)} %split_heads.1), calls=%async_computation | async-start | bytes 4194304 | tf_op jit(solution)/shard_map/all_to_all | solution.py:228
  19.0 1.7 %collective-permute-start.6 = (bf16[4,128,128]{2,1,0:T(8,128)(2,1)S(1)}, bf16[4,128,128]{2,1,0:T(8,128)(2,1)S(1)}, u32[]{:S(2)}, u32[]{:S(2)}) collective-permute-start(bf16[4,128,128]{2,1,0:T(8,128)(2,1)S(1)} %pad_maximum_fusion.refs_0_), channel_id=1, source_target_pairs={{0,16},{16,32},{32,48},{48,64},{64,80},{80,96},{96,112},{112,0},{1... | collective-permute-start | bytes 393224 | tf_op jit(solution)/shard_map/ppermute | solution.py:191
  20.7 4.0 %collective-permute-start.10 = (bf16[4,128,128]{2,1,0:T(8,128)(2,1)S(1)}, bf16[4,128,128]{2,1,0:T(8,128)(2,1)S(1)}, u32[]{:S(2)}, u32[]{:S(2)}) collective-permute-start(bf16[4,128,128]{2,1,0:T(8,128)(2,1)S(1)} %pad_maximum_fusion.1.refs_8_), channel_id=1, source_target_pairs={{0,112},{16,0},{32,16},{48,32},{64,48},{80,64},{96,80},{112,96},{1... | collective-permute-start | bytes 393224 | tf_op jit(solution)/shard_map/ppermute | solution.py:195
  24.8 1.4 %collective-permute-start.3 = (bf16[4,128,128]{2,1,0:T(8,128)(2,1)S(1)}, bf16[4,128,128]{2,1,0:T(8,128)(2,1)S(1)}, u32[]{:S(2)}, u32[]{:S(2)}) collective-permute-start(bf16[4,128,128]{2,1,0:T(8,128)(2,1)S(1)} %pad_maximum_fusion.refs_0_), channel_id=1, source_target_pairs={{0,112},{16,0},{32,16},{48,32},{64,48},{80,64},{96,80},{112,96},{1... | collective-permute-start | bytes 393224 | tf_op jit(solution)/shard_map/ppermute | solution.py:195
  26.2 2.1 %collective-permute-done.6.refs_7_ = bf16[4,128,128]{2,1,0:T(8,128)(2,1)S(1)} collective-permute-done((bf16[4,128,128]{2,1,0:T(8,128)(2,1)S(1)}, bf16[4,128,128]{2,1,0:T(8,128)(2,1)S(1)}, u32[]{:S(2)}, u32[]{:S(2)}) %collective-permute-start.6) | collective-permute-done | bytes 131104 | tf_op jit(solution)/shard_map/ppermute | solution.py:191
  28.4 2.7 %collective-permute-start.11 = (bf16[4,128,128]{2,1,0:T(8,128)(2,1)S(1)}, bf16[4,128,128]{2,1,0:T(8,128)(2,1)S(1)}, u32[]{:S(2)}, u32[]{:S(2)}) collective-permute-start(bf16[4,128,128]{2,1,0:T(8,128)(2,1)S(1)} %collective-permute-done.10.refs_9_), channel_id=1, source_target_pairs={{0,112},{16,0},{32,16},{48,32},{64,48},{80,64},{96,80},{112,96},{1... | collective-permute-start | bytes 393224 | tf_op jit(solution)/shard_map/ppermute | solution.py:195
  31.1 2.6 %collective-permute-start.4 = (bf16[4,128,128]{2,1,0:T(8,128)(2,1)S(1)}, bf16[4,128,128]{2,1,0:T(8,128)(2,1)S(1)}, u32[]{:S(2)}, u32[]{:S(2)}) collective-permute-start(bf16[4,128,128]{2,1,0:T(8,128)(2,1)S(1)} %collective-permute-done.3.refs_1_), channel_id=1, source_target_pairs={{0,112},{16,0},{32,16},{48,32},{64,48},{80,64},{96,80},{112,96},{1... | collective-permute-start | bytes 393224 | tf_op jit(solution)/shard_map/ppermute | solution.py:195
  33.7 1.4 %collective-permute-done.7.refs_6_ = bf16[4,128,128]{2,1,0:T(8,128)(2,1)S(1)} collective-permute-done((bf16[4,128,128]{2,1,0:T(8,128)(2,1)S(1)}, bf16[4,128,128]{2,1,0:T(8,128)(2,1)S(1)}, u32[]{:S(2)}, u32[]{:S(2)}) %collective-permute-start.7) | collective-permute-done | bytes 131104 | tf_op jit(solution)/shard_map/ppermute | solution.py:191
  35.1 2.7 %collective-permute-start.12 = (bf16[4,128,128]{2,1,0:T(8,128)(2,1)S(1)}, bf16[4,128,128]{2,1,0:T(8,128)(2,1)S(1)}, u32[]{:S(2)}, u32[]{:S(2)}) collective-permute-start(bf16[4,128,128]{2,1,0:T(8,128)(2,1)S(1)} %collective-permute-done.11.refs_10_), channel_id=1, source_target_pairs={{0,112},{16,0},{32,16},{48,32},{64,48},{80,64},{96,80},{112,96},{1... | collective-permute-start | bytes 393224 | tf_op jit(solution)/shard_map/ppermute | solution.py:195
  37.7 2.6 %collective-permute-start.5 = (bf16[4,128,128]{2,1,0:T(8,128)(2,1)S(1)}, bf16[4,128,128]{2,1,0:T(8,128)(2,1)S(1)}, u32[]{:S(2)}, u32[]{:S(2)}) collective-permute-start(bf16[4,128,128]{2,1,0:T(8,128)(2,1)S(1)} %collective-permute-done.4.refs_2_), channel_id=1, source_target_pairs={{0,112},{16,0},{32,16},{48,32},{64,48},{80,64},{96,80},{112,96},{1... | collective-permute-start | bytes 393224 | tf_op jit(solution)/shard_map/ppermute | solution.py:195
  40.3 1.0 collective-permute-done.8.refs_5_
  41.4 2.7 %collective-permute-start.13 = (bf16[4,128,128]{2,1,0:T(8,128)(2,1)S(1)}, bf16[4,128,128]{2,1,0:T(8,128)(2,1)}, u32[]{:S(2)}, u32[]{:S(2)}) collective-permute-start(bf16[4,128,128]{2,1,0:T(8,128)(2,1)S(1)} %collective-permute-done.12.refs_11_), channel_id=1, source_target_pairs={{0,112},{16,0},{32,16},{48,32},{64,48},{80,64},{96,80},{112,96},{1... | collective-permute-start | bytes 393224 | tf_op jit(solution)/shard_map/ppermute | solution.py:195
  44.0 1.6 %collective-permute-done.16.refs_13_ = bf16[4,128,128]{2,1,0:T(8,128)(2,1)S(1)} collective-permute-done((bf16[4,128,128]{2,1,0:T(8,128)(2,1)S(1)}, bf16[4,128,128]{2,1,0:T(8,128)(2,1)S(1)}, u32[]{:S(2)}, u32[]{:S(2)}) %collective-permute-start.16) | collective-permute-done | bytes 131104 | tf_op jit(solution)/shard_map/ppermute | solution.py:191
  45.7 1.8 %collective-permute-done.9.refs_4_ = bf16[4,128,128]{2,1,0:T(8,128)(2,1)S(1)} collective-permute-done((bf16[4,128,128]{2,1,0:T(8,128)(2,1)S(1)}, bf16[4,128,128]{2,1,0:T(8,128)(2,1)S(1)}, u32[]{:S(2)}, u32[]{:S(2)}) %collective-permute-start.9) | collective-permute-done | bytes 131104 | tf_op jit(solution)/shard_map/ppermute | solution.py:191
  47.5 0.7 copy-done.32
  48.3 1.2 copy-done.1
  49.5 25.3 %attention.1 = (bf16[32,128,256]{2,1,0:T(8,128)(2,1)}, bf16[4,128,128]{2,1,0:T(8,128)(2,1)}, bf16[4,128,128]{2,1,0:T(8,128)(2,1)}, bf16[4,128,128]{2,1,0:T(8,128...) custom-call(s32[2]{0:T(128)} %pad_add_fusion.me_ref, ...), custom_call_target="tpu_custom_call" | custom-call | flops 6442450944 | bytes 8388608 | tf_op jit(solution)/shard_map/attention/pallas_call | solution.py:173
  74.8 0.8 collective-permute-start.17
  75.6 10.7 %all-to-all-start.1 = ((bf16[32,128,256]{2,1,0:T(8,128)(2,1)}), bf16[32,128,256]{2,1,0:T(8,128)(2,1)S(1)}, u32[]{:S(2)}, u32[]{:S(2)}) async-start(bf16[32,128,256]{2,1,0:T(8,128)(2,1)} %get-tuple-element.48), calls=%async_computation.1 | async-start | bytes 4194304 | tf_op jit(solution)/shard_map/all_to_all | solution.py:228
  86.4 1.4 %collective-permute-start.21 = (bf16[4,128,128]{2,1,0:T(8,128)(2,1)S(1)}, bf16[4,128,128]{2,1,0:T(8,128)(2,1)S(1)}, u32[]{:S(2)}, u32[]{:S(2)}) collective-permute-start(bf16[4,128,128]{2,1,0:T(8,128)(2,1)S(1)} %copy-done.30), channel_id=1, source_target_pairs={{0,112},{16,0},{32,16},{48,32},{64,48},{80,64},{96,80},{112,96},{1... | collective-permute-start | bytes 393224 | tf_op jit(solution)/shard_map/ppermute | solution.py:195
  87.8 0.5 collective-permute-start.24
  88.3 2.2 %collective-permute-start.27 = (bf16[4,128,128]{2,1,0:T(8,128)(2,1)S(1)}, bf16[4,128,128]{2,1,0:T(8,128)(2,1)S(1)}, u32[]{:S(2)}, u32[]{:S(2)}) collective-permute-start(bf16[4,128,128]{2,1,0:T(8,128)(2,1)S(1)} %copy-done.25), channel_id=1, source_target_pairs={{0,112},{16,0},{32,16},{48,32},{64,48},{80,64},{96,80},{112,96},{1... | collective-permute-start | bytes 393224 | tf_op jit(solution)/shard_map/ppermute | solution.py:195
  90.5 0.3 collective-permute-start.18
  90.8 1.1 collective-permute-done.21
  92.0 2.0 %collective-permute-start.22 = (bf16[4,128,128]{2,1,0:T(8,128)(2,1)S(1)}, bf16[4,128,128]{2,1,0:T(8,128)(2,1)S(1)}, u32[]{:S(2)}, u32[]{:S(2)}) collective-permute-start(bf16[4,128,128]{2,1,0:T(8,128)(2,1)S(1)} %add_convert_fusion.6), channel_id=1, source_target_pairs={{0,112},{16,0},{32,16},{48,32},{64,48},{80,64},{96,80},{112,96},{1... | collective-permute-start | bytes 393224 | tf_op jit(solution)/shard_map/ppermute | solution.py:195
  94.0 0.1 collective-permute-start.25
  94.1 0.6 collective-permute-done.27
  94.8 2.1 %collective-permute-start.28 = (bf16[4,128,128]{2,1,0:T(8,128)(2,1)S(1)}, bf16[4,128,128]{2,1,0:T(8,128)(2,1)S(1)}, u32[]{:S(2)}, u32[]{:S(2)}) collective-permute-start(bf16[4,128,128]{2,1,0:T(8,128)(2,1)S(1)} %add_convert_fusion.2), channel_id=1, source_target_pairs={{0,112},{16,0},{32,16},{48,32},{64,48},{80,64},{96,80},{112,96},{1... | collective-permute-start | bytes 393224 | tf_op jit(solution)/shard_map/ppermute | solution.py:195
  97.1 2.7 %collective-permute-start.23 = (bf16[4,128,128]{2,1,0:T(8,128)(2,1)S(1)}, bf16[4,128,128]{2,1,0:T(8,128)(2,1)S(1)}, u32[]{:S(2)}, u32[]{:S(2)}) collective-permute-start(bf16[4,128,128]{2,1,0:T(8,128)(2,1)S(1)} %add_convert_fusion.5), channel_id=1, source_target_pairs={{0,112},{16,0},{32,16},{48,32},{64,48},{80,64},{96,80},{112,96},{1... | collective-permute-start | bytes 393224 | tf_op jit(solution)/shard_map/ppermute | solution.py:195
  100.1 2.7 %collective-permute-start.29 = (bf16[4,128,128]{2,1,0:T(8,128)(2,1)S(1)}, bf16[4,128,128]{2,1,0:T(8,128)(2,1)S(1)}, u32[]{:S(2)}, u32[]{:S(2)}) collective-permute-start(bf16[4,128,128]{2,1,0:T(8,128)(2,1)S(1)} %add_convert_fusion.1), channel_id=1, source_target_pairs={{0,112},{16,0},{32,16},{48,32},{64,48},{80,64},{96,80},{112,96},{1... | collective-permute-start | bytes 393224 | tf_op jit(solution)/shard_map/ppermute | solution.py:195
  102.9 2.9 %collective-permute-done.29 = bf16[4,128,128]{2,1,0:T(8,128)(2,1)S(1)} collective-permute-done((bf16[4,128,128]{2,1,0:T(8,128)(2,1)S(1)}, bf16[4,128,128]{2,1,0:T(8,128)(2,1)S(1)}, u32[]{:S(2)}, u32[]{:S(2)}) %collective-permute-start.29) | collective-permute-done | bytes 131104 | tf_op jit(solution)/shard_map/ppermute | solution.py:195
  105.9 3.5 %collective-permute-start.30 = (bf16[4,128,128]{2,1,0:T(8,128)(2,1)S(1)}, bf16[4,128,128]{2,1,0:T(8,128)(2,1)S(1)}, u32[]{:S(2)}, u32[]{:S(2)}) collective-permute-start(bf16[4,128,128]{2,1,0:T(8,128)(2,1)S(1)} %add_convert_fusion), channel_id=1, source_target_pairs={{0,112},{16,0},{32,16},{48,32},{64,48},{80,64},{96,80},{112,96},{1... | collective-permute-start | bytes 393224 | tf_op jit(solution)/shard_map/ppermute | solution.py:195
  109.4 0.2 collective-permute-done.20
  109.7 1.7 %collective-permute-done.30 = bf16[4,128,128]{2,1,0:T(8,128)(2,1)S(1)} collective-permute-done((bf16[4,128,128]{2,1,0:T(8,128)(2,1)S(1)}, bf16[4,128,128]{2,1,0:T(8,128)(2,1)S(1)}, u32[]{:S(2)}, u32[]{:S(2)}) %collective-permute-start.30) | collective-permute-done | bytes 131104 | tf_op jit(solution)/shard_map/ppermute | solution.py:195
  111.5 3.2 %all-to-all-done.1.tiles = bf16[32,128,256]{2,1,0:T(8,128)(2,1)S(1)} async-done(((bf16[32,128,256]{2,1,0:T(8,128)(2,1)}), bf16[32,128,256]{2,1,0:T(8,128)(2,1)S(1)}, u32[]{:S(2)}, u32[]{:S(2)}) %all-to-all-start.1) | async-done | bytes 2097184 | tf_op jit(solution)/shard_map/all_to_all | solution.py:228
  114.7 0.2 collective-permute-start.31
  114.9 3.1 %collective-permute-start.32 = (bf16[128,256]{1,0:T(8,128)(2,1)S(1)}, bf16[128,256]{1,0:T(8,128)(2,1)S(1)}, u32[]{:S(2)}, u32[]{:S(2)}) collective-permute-start(bf16[128,256]{1,0:T(8,128)(2,1)S(1)} %pad_maximum_fusion.4), channel_id=1, source_target_pairs={{0,128},{8,136},{128,0},{136,8},{1,129},{9,137},{129,1},{137,9},{2... | collective-permute-start | bytes 196616 | tf_op jit(solution)/shard_map/ppermute | solution.py:200
  118.0 0.4 collective-permute-start.33
  118.3 1.9 %join_heads.1 = (bf16[128,4096]{1,0:T(8,128)(2,1)}, bf16[128,4096]{1,0:T(8,128)(2,1)}) custom-call(bf16[32,128,256]{2,1,0:T(8,128)(2,1)S(1)} %all-to-all-done.1.tiles), custom_call_target="tpu_custom_call" | custom-call | tf_op jit(solution)/shard_map/join_heads/pallas_call | solution.py:89
  120.2 3.3 %collective-permute-done.33.refs_3_ = bf16[128,256]{1,0:T(8,128)(2,1)S(1)} collective-permute-done((bf16[128,256]{1,0:T(8,128)(2,1)S(1)}, bf16[128,256]{1,0:T(8,128)(2,1)S(1)}, u32[]{:S(2)}, u32[]{:S(2)}) %collective-permute-start.33) | collective-permute-done | bytes 65568 | tf_op jit(solution)/shard_map/ppermute | solution.py:200
  123.5 1.3 %join_kv.1 = (bf16[128,512]{1,0:T(8,128)(2,1)}, bf16[128,512]{1,0:T(8,128)(2,1)}) custom-call(s32[2]{0:T(128)S(1)} %copy-done, bf16[128,256]{1,0:T(8,128)(2,1)S(1)} %pad_maximum_fusion.2.refs_0_, bf16[128,256]{1,0:T(8,128)(2,1)S(1)} %collective-permute-done.31.refs_1_, bf16[128,256]{1,0:T(8,128)(2,1)S(1)} %collective-permute-done.32.refs_2_, ...), custom_call_target="tpu_custom_call" | custom-call | tf_op jit(solution)/shard_map/join_kv/pallas_call | solution.py:67
  (116 shorter events, 1.1 us)
Async XLA Ops:
  3.0 9.7 %collective-permute-start = (bf16[128,256]{1,0:T(8,128)(2,1)}, bf16[128,256]{1,0:T(8,128)(2,1)S(1)}, u32[]{:S(2)}, u32[]{:S(2)}) collective-permute-start(bf16[128,256]{1,0:T(8,128)(2,1)} %get-tuple-element.40), channel_id=1, source_target_pairs={{0,8},{8,0},{128,136},{136,128},{1,9},{9,1},{129,137},{137,129},{2... | collective-permute-start | bytes 196616 | tf_op jit(solution)/shard_map/ppermute | solution.py:200
  6.2 6.4 %collective-permute-start.1 = (bf16[128,256]{1,0:T(8,128)(2,1)}, bf16[128,256]{1,0:T(8,128)(2,1)S(1)}, u32[]{:S(2)}, u32[]{:S(2)}) collective-permute-start(bf16[128,256]{1,0:T(8,128)(2,1)} %get-tuple-element.41), channel_id=1, source_target_pairs={{0,128},{8,136},{128,0},{136,8},{1,129},{9,137},{129,1},{137,9},{2... | collective-permute-start | bytes 196616 | tf_op jit(solution)/shard_map/ppermute | solution.py:200
  7.2 6.0 %collective-permute-start.2 = (bf16[128,256]{1,0:T(8,128)(2,1)}, bf16[128,256]{1,0:T(8,128)(2,1)S(1)}, u32[]{:S(2)}, u32[]{:S(2)}) collective-permute-start(bf16[128,256]{1,0:T(8,128)(2,1)} %get-tuple-element.42), channel_id=1, source_target_pairs={{0,136},{8,128},{128,8},{136,0},{1,137},{9,129},{129,9},{137,1},{2... | collective-permute-start | bytes 196616 | tf_op jit(solution)/shard_map/ppermute | solution.py:200
  13.2 35.0 %all-to-all-start = ((bf16[32,128,256]{2,1,0:T(8,128)(2,1)}), bf16[32,128,256]{2,1,0:T(8,128)(2,1)S(1)}, u32[]{:S(2)}, u32[]{:S(2)}) async-start(bf16[32,128,256]{2,1,0:T(8,128)(2,1)} %split_heads.1), calls=%async_computation | async-start | bytes 4194304 | tf_op jit(solution)/shard_map/all_to_all | solution.py:228
  19.0 29.2 %copy-start.12 = (bf16[4,128,128]{2,1,0:T(8,128)(2,1)}, bf16[4,128,128]{2,1,0:T(8,128)(2,1)S(1)}, u32[]{:S(2)}) copy-start(bf16[4,128,128]{2,1,0:T(8,128)(2,1)S(1)} %pad_maximum_fusion.refs_0_) | copy-start | bytes 393220
  19.0 9.4 %collective-permute-start.6 = (bf16[4,128,128]{2,1,0:T(8,128)(2,1)S(1)}, bf16[4,128,128]{2,1,0:T(8,128)(2,1)S(1)}, u32[]{:S(2)}, u32[]{:S(2)}) collective-permute-start(bf16[4,128,128]{2,1,0:T(8,128)(2,1)S(1)} %pad_maximum_fusion.refs_0_), channel_id=1, source_target_pairs={{0,16},{16,32},{32,48},{48,64},{64,80},{80,96},{96,112},{112,0},{1... | collective-permute-start | bytes 393224 | tf_op jit(solution)/shard_map/ppermute | solution.py:191
  20.7 27.5 %copy-start.13 = (bf16[4,128,128]{2,1,0:T(8,128)(2,1)}, bf16[4,128,128]{2,1,0:T(8,128)(2,1)S(1)}, u32[]{:S(2)}) copy-start(bf16[4,128,128]{2,1,0:T(8,128)(2,1)S(1)} %pad_maximum_fusion.1.refs_8_) | copy-start | bytes 393220
  20.7 7.6 %collective-permute-start.10 = (bf16[4,128,128]{2,1,0:T(8,128)(2,1)S(1)}, bf16[4,128,128]{2,1,0:T(8,128)(2,1)S(1)}, u32[]{:S(2)}, u32[]{:S(2)}) collective-permute-start(bf16[4,128,128]{2,1,0:T(8,128)(2,1)S(1)} %pad_maximum_fusion.1.refs_8_), channel_id=1, source_target_pairs={{0,112},{16,0},{32,16},{48,32},{64,48},{80,64},{96,80},{112,96},{1... | collective-permute-start | bytes 393224 | tf_op jit(solution)/shard_map/ppermute | solution.py:195
  24.8 6.3 %collective-permute-start.3 = (bf16[4,128,128]{2,1,0:T(8,128)(2,1)S(1)}, bf16[4,128,128]{2,1,0:T(8,128)(2,1)S(1)}, u32[]{:S(2)}, u32[]{:S(2)}) collective-permute-start(bf16[4,128,128]{2,1,0:T(8,128)(2,1)S(1)} %pad_maximum_fusion.refs_0_), channel_id=1, source_target_pairs={{0,112},{16,0},{32,16},{48,32},{64,48},{80,64},{96,80},{112,96},{1... | collective-permute-start | bytes 393224 | tf_op jit(solution)/shard_map/ppermute | solution.py:195
  26.2 7.4 %collective-permute-start.14 = (bf16[4,128,128]{2,1,0:T(8,128)(2,1)S(1)}, bf16[4,128,128]{2,1,0:T(8,128)(2,1)S(1)}, u32[]{:S(2)}, u32[]{:S(2)}) collective-permute-start(bf16[4,128,128]{2,1,0:T(8,128)(2,1)S(1)} %pad_maximum_fusion.1.refs_8_), channel_id=1, source_target_pairs={{0,16},{16,32},{32,48},{48,64},{64,80},{80,96},{96,112},{112,0},{1... | collective-permute-start | bytes 393224 | tf_op jit(solution)/shard_map/ppermute | solution.py:191
  28.4 19.9 %copy-start.17 = (bf16[4,128,128]{2,1,0:T(8,128)(2,1)}, bf16[4,128,128]{2,1,0:T(8,128)(2,1)S(1)}, u32[]{:S(2)}) copy-start(bf16[4,128,128]{2,1,0:T(8,128)(2,1)S(1)} %collective-permute-done.6.refs_7_) | copy-start | bytes 393220
  28.4 6.7 %collective-permute-start.7 = (bf16[4,128,128]{2,1,0:T(8,128)(2,1)S(1)}, bf16[4,128,128]{2,1,0:T(8,128)(2,1)S(1)}, u32[]{:S(2)}, u32[]{:S(2)}) collective-permute-start(bf16[4,128,128]{2,1,0:T(8,128)(2,1)S(1)} %collective-permute-done.6.refs_7_), channel_id=1, source_target_pairs={{0,16},{16,32},{32,48},{48,64},{64,80},{80,96},{96,112},{112,0},{1... | collective-permute-start | bytes 393224 | tf_op jit(solution)/shard_map/ppermute | solution.py:191
  28.4 19.8 %copy-start.18 = (bf16[4,128,128]{2,1,0:T(8,128)(2,1)}, bf16[4,128,128]{2,1,0:T(8,128)(2,1)S(1)}, u32[]{:S(2)}) copy-start(bf16[4,128,128]{2,1,0:T(8,128)(2,1)S(1)} %collective-permute-done.10.refs_9_) | copy-start | bytes 393220
  28.4 6.7 %collective-permute-start.11 = (bf16[4,128,128]{2,1,0:T(8,128)(2,1)S(1)}, bf16[4,128,128]{2,1,0:T(8,128)(2,1)S(1)}, u32[]{:S(2)}, u32[]{:S(2)}) collective-permute-start(bf16[4,128,128]{2,1,0:T(8,128)(2,1)S(1)} %collective-permute-done.10.refs_9_), channel_id=1, source_target_pairs={{0,112},{16,0},{32,16},{48,32},{64,48},{80,64},{96,80},{112,96},{1... | collective-permute-start | bytes 393224 | tf_op jit(solution)/shard_map/ppermute | solution.py:195
  31.1 6.7 %collective-permute-start.4 = (bf16[4,128,128]{2,1,0:T(8,128)(2,1)S(1)}, bf16[4,128,128]{2,1,0:T(8,128)(2,1)S(1)}, u32[]{:S(2)}, u32[]{:S(2)}) collective-permute-start(bf16[4,128,128]{2,1,0:T(8,128)(2,1)S(1)} %collective-permute-done.3.refs_1_), channel_id=1, source_target_pairs={{0,112},{16,0},{32,16},{48,32},{64,48},{80,64},{96,80},{112,96},{1... | collective-permute-start | bytes 393224 | tf_op jit(solution)/shard_map/ppermute | solution.py:195
  33.7 6.7 %collective-permute-start.15 = (bf16[4,128,128]{2,1,0:T(8,128)(2,1)S(1)}, bf16[4,128,128]{2,1,0:T(8,128)(2,1)S(1)}, u32[]{:S(2)}, u32[]{:S(2)}) collective-permute-start(bf16[4,128,128]{2,1,0:T(8,128)(2,1)S(1)} %collective-permute-done.14.refs_15_), channel_id=1, source_target_pairs={{0,16},{16,32},{32,48},{48,64},{64,80},{80,96},{96,112},{112,0},{1... | collective-permute-start | bytes 393224 | tf_op jit(solution)/shard_map/ppermute | solution.py:191
  35.0 6.3 %collective-permute-start.8 = (bf16[4,128,128]{2,1,0:T(8,128)(2,1)S(1)}, bf16[4,128,128]{2,1,0:T(8,128)(2,1)S(1)}, u32[]{:S(2)}, u32[]{:S(2)}) collective-permute-start(bf16[4,128,128]{2,1,0:T(8,128)(2,1)S(1)} %collective-permute-done.7.refs_6_), channel_id=1, source_target_pairs={{0,16},{16,32},{32,48},{48,64},{64,80},{80,96},{96,112},{112,0},{1... | collective-permute-start | bytes 393224 | tf_op jit(solution)/shard_map/ppermute | solution.py:191
  35.1 6.3 %collective-permute-start.12 = (bf16[4,128,128]{2,1,0:T(8,128)(2,1)S(1)}, bf16[4,128,128]{2,1,0:T(8,128)(2,1)S(1)}, u32[]{:S(2)}, u32[]{:S(2)}) collective-permute-start(bf16[4,128,128]{2,1,0:T(8,128)(2,1)S(1)} %collective-permute-done.11.refs_10_), channel_id=1, source_target_pairs={{0,112},{16,0},{32,16},{48,32},{64,48},{80,64},{96,80},{112,96},{1... | collective-permute-start | bytes 393224 | tf_op jit(solution)/shard_map/ppermute | solution.py:195
  37.7 6.3 %collective-permute-start.5 = (bf16[4,128,128]{2,1,0:T(8,128)(2,1)S(1)}, bf16[4,128,128]{2,1,0:T(8,128)(2,1)S(1)}, u32[]{:S(2)}, u32[]{:S(2)}) collective-permute-start(bf16[4,128,128]{2,1,0:T(8,128)(2,1)S(1)} %collective-permute-done.4.refs_2_), channel_id=1, source_target_pairs={{0,112},{16,0},{32,16},{48,32},{64,48},{80,64},{96,80},{112,96},{1... | collective-permute-start | bytes 393224 | tf_op jit(solution)/shard_map/ppermute | solution.py:195
  40.3 5.3 %collective-permute-start.16 = (bf16[4,128,128]{2,1,0:T(8,128)(2,1)S(1)}, bf16[4,128,128]{2,1,0:T(8,128)(2,1)S(1)}, u32[]{:S(2)}, u32[]{:S(2)}) collective-permute-start(bf16[4,128,128]{2,1,0:T(8,128)(2,1)S(1)} %collective-permute-done.15.refs_14_), channel_id=1, source_target_pairs={{0,16},{16,32},{32,48},{48,64},{64,80},{80,96},{96,112},{112,0},{1... | collective-permute-start | bytes 393224 | tf_op jit(solution)/shard_map/ppermute | solution.py:191
  41.3 6.2 %collective-permute-start.9 = (bf16[4,128,128]{2,1,0:T(8,128)(2,1)S(1)}, bf16[4,128,128]{2,1,0:T(8,128)(2,1)S(1)}, u32[]{:S(2)}, u32[]{:S(2)}) collective-permute-start(bf16[4,128,128]{2,1,0:T(8,128)(2,1)S(1)} %collective-permute-done.8.refs_5_), channel_id=1, source_target_pairs={{0,16},{16,32},{32,48},{48,64},{64,80},{80,96},{96,112},{112,0},{1... | collective-permute-start | bytes 393224 | tf_op jit(solution)/shard_map/ppermute | solution.py:191
  41.4 6.8 %collective-permute-start.13 = (bf16[4,128,128]{2,1,0:T(8,128)(2,1)S(1)}, bf16[4,128,128]{2,1,0:T(8,128)(2,1)}, u32[]{:S(2)}, u32[]{:S(2)}) collective-permute-start(bf16[4,128,128]{2,1,0:T(8,128)(2,1)S(1)} %collective-permute-done.12.refs_11_), channel_id=1, source_target_pairs={{0,112},{16,0},{32,16},{48,32},{64,48},{80,64},{96,80},{112,96},{1... | collective-permute-start | bytes 393224 | tf_op jit(solution)/shard_map/ppermute | solution.py:195
  74.8 15.7 %collective-permute-start.17 = (bf16[4,128,128]{2,1,0:T(8,128)(2,1)}, bf16[4,128,128]{2,1,0:T(8,128)(2,1)S(1)}, u32[]{:S(2)}, u32[]{:S(2)}) collective-permute-start(bf16[4,128,128]{2,1,0:T(8,128)(2,1)} %get-tuple-element.53), channel_id=1, source_target_pairs={{0,16},{16,32},{32,48},{48,64},{64,80},{80,96},{96,112},{112,0},{1... | collective-permute-start | bytes 393224 | tf_op jit(solution)/shard_map/ppermute | solution.py:191
  75.6 18.4 %copy-start.9 = (bf16[4,128,128]{2,1,0:T(8,128)(2,1)S(1)}, bf16[4,128,128]{2,1,0:T(8,128)(2,1)}, u32[]{:S(2)}) copy-start(bf16[4,128,128]{2,1,0:T(8,128)(2,1)} %get-tuple-element.59) | copy-start | bytes 393220
  75.6 19.1 %copy-start.8 = (bf16[4,128,128]{2,1,0:T(8,128)(2,1)S(1)}, bf16[4,128,128]{2,1,0:T(8,128)(2,1)}, u32[]{:S(2)}) copy-start(bf16[4,128,128]{2,1,0:T(8,128)(2,1)} %get-tuple-element.63) | copy-start | bytes 393220
  75.6 21.3 %copy-start.7 = (bf16[4,128,128]{2,1,0:T(8,128)(2,1)S(1)}, bf16[4,128,128]{2,1,0:T(8,128)(2,1)}, u32[]{:S(2)}) copy-start(bf16[4,128,128]{2,1,0:T(8,128)(2,1)} %get-tuple-element.51) | copy-start | bytes 393220
  75.6 21.5 %copy-start.6 = (bf16[4,128,128]{2,1,0:T(8,128)(2,1)S(1)}, bf16[4,128,128]{2,1,0:T(8,128)(2,1)}, u32[]{:S(2)}) copy-start(bf16[4,128,128]{2,1,0:T(8,128)(2,1)} %get-tuple-element.54) | copy-start | bytes 393220
  75.6 39.1 %all-to-all-start.1 = ((bf16[32,128,256]{2,1,0:T(8,128)(2,1)}), bf16[32,128,256]{2,1,0:T(8,128)(2,1)S(1)}, u32[]{:S(2)}, u32[]{:S(2)}) async-start(bf16[32,128,256]{2,1,0:T(8,128)(2,1)} %get-tuple-element.48), calls=%async_computation.1 | async-start | bytes 4194304 | tf_op jit(solution)/shard_map/all_to_all | solution.py:228
  86.3 19.5 %copy-start.2 = (bf16[4,128,128]{2,1,0:T(8,128)(2,1)S(1)}, bf16[4,128,128]{2,1,0:T(8,128)(2,1)}, u32[]{:S(2)}) copy-start(bf16[4,128,128]{2,1,0:T(8,128)(2,1)} %get-tuple-element.61) | copy-start | bytes 393220
  86.4 23.3 %copy-start.15 = (bf16[4,128,128]{2,1,0:T(8,128)(2,1)S(1)}, bf16[4,128,128]{2,1,0:T(8,128)(2,1)}, u32[]{:S(2)}) copy-start(bf16[4,128,128]{2,1,0:T(8,128)(2,1)} %get-tuple-element.49) | copy-start | bytes 393220
  86.4 5.5 %collective-permute-start.21 = (bf16[4,128,128]{2,1,0:T(8,128)(2,1)S(1)}, bf16[4,128,128]{2,1,0:T(8,128)(2,1)S(1)}, u32[]{:S(2)}, u32[]{:S(2)}) collective-permute-start(bf16[4,128,128]{2,1,0:T(8,128)(2,1)S(1)} %copy-done.30), channel_id=1, source_target_pairs={{0,112},{16,0},{32,16},{48,32},{64,48},{80,64},{96,80},{112,96},{1... | collective-permute-start | bytes 393224 | tf_op jit(solution)/shard_map/ppermute | solution.py:195
  87.8 6.2 %collective-permute-start.24 = (bf16[4,128,128]{2,1,0:T(8,128)(2,1)S(1)}, bf16[4,128,128]{2,1,0:T(8,128)(2,1)S(1)}, u32[]{:S(2)}, u32[]{:S(2)}) collective-permute-start(bf16[4,128,128]{2,1,0:T(8,128)(2,1)S(1)} %copy-done.28), channel_id=1, source_target_pairs={{0,16},{16,32},{32,48},{48,64},{64,80},{80,96},{96,112},{112,0},{1... | collective-permute-start | bytes 393224 | tf_op jit(solution)/shard_map/ppermute | solution.py:191
  88.3 6.4 %collective-permute-start.27 = (bf16[4,128,128]{2,1,0:T(8,128)(2,1)S(1)}, bf16[4,128,128]{2,1,0:T(8,128)(2,1)S(1)}, u32[]{:S(2)}, u32[]{:S(2)}) collective-permute-start(bf16[4,128,128]{2,1,0:T(8,128)(2,1)S(1)} %copy-done.25), channel_id=1, source_target_pairs={{0,112},{16,0},{32,16},{48,32},{64,48},{80,64},{96,80},{112,96},{1... | collective-permute-start | bytes 393224 | tf_op jit(solution)/shard_map/ppermute | solution.py:195
  90.5 20.8 %copy-start.14 = (bf16[4,128,128]{2,1,0:T(8,128)(2,1)S(1)}, bf16[4,128,128]{2,1,0:T(8,128)(2,1)}, u32[]{:S(2)}) copy-start(bf16[4,128,128]{2,1,0:T(8,128)(2,1)} %get-tuple-element.57) | copy-start | bytes 393220
  90.5 6.4 %collective-permute-start.18 = (bf16[4,128,128]{2,1,0:T(8,128)(2,1)S(1)}, bf16[4,128,128]{2,1,0:T(8,128)(2,1)S(1)}, u32[]{:S(2)}, u32[]{:S(2)}) collective-permute-start(bf16[4,128,128]{2,1,0:T(8,128)(2,1)S(1)} %add_convert_fusion.9), channel_id=1, source_target_pairs={{0,16},{16,32},{32,48},{48,64},{64,80},{80,96},{96,112},{112,0},{1... | collective-permute-start | bytes 393224 | tf_op jit(solution)/shard_map/ppermute | solution.py:191
  92.0 5.1 %collective-permute-start.22 = (bf16[4,128,128]{2,1,0:T(8,128)(2,1)S(1)}, bf16[4,128,128]{2,1,0:T(8,128)(2,1)S(1)}, u32[]{:S(2)}, u32[]{:S(2)}) collective-permute-start(bf16[4,128,128]{2,1,0:T(8,128)(2,1)S(1)} %add_convert_fusion.6), channel_id=1, source_target_pairs={{0,112},{16,0},{32,16},{48,32},{64,48},{80,64},{96,80},{112,96},{1... | collective-permute-start | bytes 393224 | tf_op jit(solution)/shard_map/ppermute | solution.py:195
  94.0 5.8 %collective-permute-start.25 = (bf16[4,128,128]{2,1,0:T(8,128)(2,1)S(1)}, bf16[4,128,128]{2,1,0:T(8,128)(2,1)S(1)}, u32[]{:S(2)}, u32[]{:S(2)}) collective-permute-start(bf16[4,128,128]{2,1,0:T(8,128)(2,1)S(1)} %add_convert_fusion.4), channel_id=1, source_target_pairs={{0,16},{16,32},{32,48},{48,64},{64,80},{80,96},{96,112},{112,0},{1... | collective-permute-start | bytes 393224 | tf_op jit(solution)/shard_map/ppermute | solution.py:191
  94.8 5.2 %collective-permute-start.28 = (bf16[4,128,128]{2,1,0:T(8,128)(2,1)S(1)}, bf16[4,128,128]{2,1,0:T(8,128)(2,1)S(1)}, u32[]{:S(2)}, u32[]{:S(2)}) collective-permute-start(bf16[4,128,128]{2,1,0:T(8,128)(2,1)S(1)} %add_convert_fusion.2), channel_id=1, source_target_pairs={{0,112},{16,0},{32,16},{48,32},{64,48},{80,64},{96,80},{112,96},{1... | collective-permute-start | bytes 393224 | tf_op jit(solution)/shard_map/ppermute | solution.py:195
  97.0 5.8 %collective-permute-start.19 = (bf16[4,128,128]{2,1,0:T(8,128)(2,1)S(1)}, bf16[4,128,128]{2,1,0:T(8,128)(2,1)S(1)}, u32[]{:S(2)}, u32[]{:S(2)}) collective-permute-start(bf16[4,128,128]{2,1,0:T(8,128)(2,1)S(1)} %add_convert_fusion.8), channel_id=1, source_target_pairs={{0,16},{16,32},{32,48},{48,64},{64,80},{80,96},{96,112},{112,0},{1... | collective-permute-start | bytes 393224 | tf_op jit(solution)/shard_map/ppermute | solution.py:191
  97.1 12.3 %collective-permute-start.23 = (bf16[4,128,128]{2,1,0:T(8,128)(2,1)S(1)}, bf16[4,128,128]{2,1,0:T(8,128)(2,1)S(1)}, u32[]{:S(2)}, u32[]{:S(2)}) collective-permute-start(bf16[4,128,128]{2,1,0:T(8,128)(2,1)S(1)} %add_convert_fusion.5), channel_id=1, source_target_pairs={{0,112},{16,0},{32,16},{48,32},{64,48},{80,64},{96,80},{112,96},{1... | collective-permute-start | bytes 393224 | tf_op jit(solution)/shard_map/ppermute | solution.py:195
  99.9 9.8 %collective-permute-start.26 = (bf16[4,128,128]{2,1,0:T(8,128)(2,1)S(1)}, bf16[4,128,128]{2,1,0:T(8,128)(2,1)S(1)}, u32[]{:S(2)}, u32[]{:S(2)}) collective-permute-start(bf16[4,128,128]{2,1,0:T(8,128)(2,1)S(1)} %add_convert_fusion.3), channel_id=1, source_target_pairs={{0,16},{16,32},{32,48},{48,64},{64,80},{80,96},{96,112},{112,0},{1... | collective-permute-start | bytes 393224 | tf_op jit(solution)/shard_map/ppermute | solution.py:191
  100.1 5.8 %collective-permute-start.29 = (bf16[4,128,128]{2,1,0:T(8,128)(2,1)S(1)}, bf16[4,128,128]{2,1,0:T(8,128)(2,1)S(1)}, u32[]{:S(2)}, u32[]{:S(2)}) collective-permute-start(bf16[4,128,128]{2,1,0:T(8,128)(2,1)S(1)} %add_convert_fusion.1), channel_id=1, source_target_pairs={{0,112},{16,0},{32,16},{48,32},{64,48},{80,64},{96,80},{112,96},{1... | collective-permute-start | bytes 393224 | tf_op jit(solution)/shard_map/ppermute | solution.py:195
  102.8 20.7 %copy-start = (s32[2]{0:T(128)S(1)}, s32[2]{0:T(128)}, u32[]{:S(2)}) copy-start(s32[2]{0:T(128)} %pad_add_fusion.me_ref) | copy-start | bytes 28
  102.8 6.8 %collective-permute-start.20 = (bf16[4,128,128]{2,1,0:T(8,128)(2,1)S(1)}, bf16[4,128,128]{2,1,0:T(8,128)(2,1)S(1)}, u32[]{:S(2)}, u32[]{:S(2)}) collective-permute-start(bf16[4,128,128]{2,1,0:T(8,128)(2,1)S(1)} %add_convert_fusion.7), channel_id=1, source_target_pairs={{0,16},{16,32},{32,48},{48,64},{64,80},{80,96},{96,112},{112,0},{1... | collective-permute-start | bytes 393224 | tf_op jit(solution)/shard_map/ppermute | solution.py:191
  105.9 5.4 %collective-permute-start.30 = (bf16[4,128,128]{2,1,0:T(8,128)(2,1)S(1)}, bf16[4,128,128]{2,1,0:T(8,128)(2,1)S(1)}, u32[]{:S(2)}, u32[]{:S(2)}) collective-permute-start(bf16[4,128,128]{2,1,0:T(8,128)(2,1)S(1)} %add_convert_fusion), channel_id=1, source_target_pairs={{0,112},{16,0},{32,16},{48,32},{64,48},{80,64},{96,80},{112,96},{1... | collective-permute-start | bytes 393224 | tf_op jit(solution)/shard_map/ppermute | solution.py:195
  114.7 5.5 %collective-permute-start.31 = (bf16[128,256]{1,0:T(8,128)(2,1)S(1)}, bf16[128,256]{1,0:T(8,128)(2,1)S(1)}, u32[]{:S(2)}, u32[]{:S(2)}) collective-permute-start(bf16[128,256]{1,0:T(8,128)(2,1)S(1)} %pad_maximum_fusion.3), channel_id=1, source_target_pairs={{0,8},{8,0},{128,136},{136,128},{1,9},{9,1},{129,137},{137,129},{2... | collective-permute-start | bytes 196616 | tf_op jit(solution)/shard_map/ppermute | solution.py:200
  114.9 5.3 %collective-permute-start.32 = (bf16[128,256]{1,0:T(8,128)(2,1)S(1)}, bf16[128,256]{1,0:T(8,128)(2,1)S(1)}, u32[]{:S(2)}, u32[]{:S(2)}) collective-permute-start(bf16[128,256]{1,0:T(8,128)(2,1)S(1)} %pad_maximum_fusion.4), channel_id=1, source_target_pairs={{0,128},{8,136},{128,0},{136,8},{1,129},{9,137},{129,1},{137,9},{2... | collective-permute-start | bytes 196616 | tf_op jit(solution)/shard_map/ppermute | solution.py:200
  118.0 5.6 %collective-permute-start.33 = (bf16[128,256]{1,0:T(8,128)(2,1)S(1)}, bf16[128,256]{1,0:T(8,128)(2,1)S(1)}, u32[]{:S(2)}, u32[]{:S(2)}) collective-permute-start(bf16[128,256]{1,0:T(8,128)(2,1)S(1)} %pad_maximum_fusion.5), channel_id=1, source_target_pairs={{0,136},{8,128},{128,8},{136,0},{1,137},{9,129},{129,9},{137,1},{2... | collective-permute-start | bytes 196616 | tf_op jit(solution)/shard_map/ppermute | solution.py:200
  (21 other events, 213.5 us)

commit v5 on v4

--- a/solution.py
+++ b/solution.py
@@ -48,23 +48,25 @@
     )
 
 
-def split_kv(me, key, value):
-    def kernel(me_ref, key_ref, value_ref, *tiles):
+def split_kv(key, value):
+    def kernel(key_ref, value_ref, *tiles):
+        quad = lax.axis_index(QUAD)
         for t, tile in enumerate(tiles):
-            tile[:, :HEAD_DIM] = key_ref[:, columns(me_ref[0] ^ t)]
-            tile[:, HEAD_DIM:] = value_ref[:, columns(me_ref[0] ^ t)]
-
-    return call(kernel, "split_kv", [SMEM, VMEM, VMEM], [(BLOCK, WIDE)] * 4)(me, key, value)
-
-
-def join_kv(me, tiles):
-    def kernel(me_ref, *refs):
+            tile[:, :HEAD_DIM] = key_ref[:, columns(quad ^ t)]
+            tile[:, HEAD_DIM:] = value_ref[:, columns(quad ^ t)]
+
+    return call(kernel, "split_kv", [VMEM, VMEM], [(BLOCK, WIDE)] * 4)(key, value)
+
+
+def join_kv(tiles):
+    def kernel(*refs):
+        quad = lax.axis_index(QUAD)
         *tiles, key_ref, value_ref = refs
         for t, tile in enumerate(tiles):
-            key_ref[:, columns(me_ref[0] ^ t)] = tile[:, :HEAD_DIM]
-            value_ref[:, columns(me_ref[0] ^ t)] = tile[:, HEAD_DIM:]
-
-    return call(kernel, "join_kv", [SMEM] + [VMEM] * 4, [(BLOCK, 4 * HEAD_DIM)] * 2)(me, *tiles)
+            key_ref[:, columns(quad ^ t)] = tile[:, :HEAD_DIM]
+            value_ref[:, columns(quad ^ t)] = tile[:, HEAD_DIM:]
+
+    return call(kernel, "join_kv", [VMEM] * 4, [(BLOCK, 4 * HEAD_DIM)] * 2)(*tiles)
 
 
 def split_heads(query, d_out):
@@ -93,11 +95,11 @@
     return sum(term.astype(F32) for term in terms).astype(BF16)
 
 
-def attention_kernel(me_ref, seg_ref, spans_ref, qd_ref, *refs):
+def attention_kernel(seg_ref, spans_ref, qd_ref, *refs):
     keys_in, values_in, od_ref = refs[:PLANES], refs[PLANES : 2 * PLANES], refs[2 * PLANES]
     key_parts, value_parts = refs[2 * PLANES + 1 : 3 * PLANES + 1], refs[3 * PLANES + 1 : 4 * PLANES + 1]
     k_ref, v_ref, kt_ref, vt_ref, dk_ref, dv_ref = refs[4 * PLANES + 1 :]
-    quad, z = me_ref[0], me_ref[1]
+    quad, z = lax.axis_index(QUAD), lax.axis_index("z")
 
     @pl.when(pl.program_id(0) == 0)
     def _():
@@ -128,7 +130,6 @@
         scores = nt(keys, q)
         values = jnp.concatenate([v_ref[loc] for loc in locs], axis=0)
         yield
-        dprob = nt(values, do)
         top = jnp.max(scores, axis=0, keepdims=True)
         expo = jnp.exp2((scores - top) * (FACTOR * LOG2E))
         prob = expo * (1.0 / jnp.sum(expo, axis=0, keepdims=True))
@@ -136,8 +137,11 @@
         value_t = jnp.concatenate([vt_ref[loc] for loc in locs], axis=1)
         yield
         attn_t = nn(value_t, prob_b)
-        yield
+        dprob = nt(values, do)
         value_slots = nn(prob_b, do)
+        for j in range(SPANS):
+            dv_ref[locs[j]] += value_slots[j * BLOCK : (j + 1) * BLOCK]
+        yield
         od_ref[u, :, :HEAD_DIM] = attn_t.T.astype(BF16)
         delta = jnp.sum(do.astype(F32).T * attn_t, axis=0, keepdims=True)
         dscore_b = (prob * (dprob - delta)).astype(BF16)
@@ -150,7 +154,6 @@
         for j in range(SPANS):
             rows = slice(j * BLOCK, (j + 1) * BLOCK)
             dk_ref[locs[j]] += key_slots[rows]
-            dv_ref[locs[j]] += value_slots[rows]
 
     live = [one_block(u) for u in range(UNROLL)]
     while live:
@@ -166,14 +169,14 @@
                 value_parts[o][t] = dv_ref[4 * o + t].astype(BF16)
 
 
-def attention(me, seg_map, spans_t, qd, keys, values):
+def attention(seg_map, spans_t, qd, keys, values):
     cad_blocks, doc_blocks = qd.shape[0], 4 * PLANES
     step = pl.BlockSpec((UNROLL, BLOCK, WIDE), lambda i: (i, 0, 0))
     square = (doc_blocks, BLOCK, HEAD_DIM)
     od, *parts = call(
         attention_kernel,
         "attention",
-        [SMEM] * 3 + [step] + [VMEM] * 2 * PLANES,
+        [SMEM] * 2 + [step] + [VMEM] * 2 * PLANES,
         [qd.shape] + [(4, BLOCK, HEAD_DIM)] * 2 * PLANES,
         [pltpu.VMEM(square, BF16)] * 4 + [pltpu.VMEM(square, F32)] * 2,
         [step] + [VMEM] * 2 * PLANES,
@@ -183,7 +186,7 @@
             bytes_accessed=2 * (2 * qd.size + 4 * doc_blocks * BLOCK * HEAD_DIM),
             transcendentals=cad_blocks * SPANS * BLOCK * BLOCK,
         ),
-    )(me, seg_map, spans_t, qd, *keys, *values)
+    )(seg_map, spans_t, qd, *keys, *values)
     return od, parts[:PLANES], parts[PLANES:]
 
 
@@ -229,19 +232,18 @@
 
 
 def body(query, key, value, d_out, seg_map, spans):
-    me = jnp.stack([lax.axis_index(QUAD), lax.axis_index("z")]).astype(jnp.int32)
-    tiles = exchange(split_kv(me, key, value))
+    tiles = exchange(split_kv(key, value))
     qd, tiles = lax.optimization_barrier((split_heads(query, d_out), tiles))
     own_keys = jnp.stack([tile[:, :HEAD_DIM] for tile in tiles])
     own_values = jnp.stack([tile[:, HEAD_DIM:] for tile in tiles])
     qd, keys, values = swap(qd), gather_z(own_keys, 4), gather_z(own_values, 3)
-    od, key_parts, value_parts = attention(me, seg_map, spans.T, qd, keys, values)
+    od, key_parts, value_parts = attention(seg_map, spans.T, qd, keys, values)
     od = swap(od)
     sums = scatter_z(key_parts, 4), scatter_z(value_parts, 3)
     tiles = [jnp.concatenate([plus(*(x[t] for x in s)) for s in sums], axis=1) for t in range(4)]
     od, tiles = lax.optimization_barrier((od, tiles))
     attn_out, d_query = join_heads(od)
-    d_key, d_value = join_kv(me, exchange(tiles))
+    d_key, d_value = join_kv(exchange(tiles))
     return attn_out, d_query, d_key, d_value
 
 

time: 126 us -> 124 us (0.984)
  Pallas kernels: 33.4 us -> 32.1 us
    pallas_call x3, Pallas kernels: 28.3 us -> 27 us  [the longest x1 24.5 us: attention(): call(attention_kernel, 'attention', [SMEM] * 2 + [step] + [VMEM] * 2 * PL...]
where the time goes in v5:
time: 124 us; the launch traced here: 123 us
  starting transfers between devices  65.7 us (53%)
  Pallas kernels  32.1 us (26%)
  waiting for transfers between devices  21.6 us (17%)
  local copies, waits for them, and re-layouts  2.02 us (2%)
    ppermute x14, starting transfers between devices, down(): lax.ppermute(array, 'z', [(i, (i - 1) % PLANES) for i in range(PLANES)])  35.8 us
    pallas_call x1, Pallas kernels, attention(): call(attention_kernel, 'attention', [SMEM] * 2 + [step] + [VMEM] * 2 * PL...  24.5 us
    all_to_all x2, starting transfers between devices, swap(): return lax.all_to_all(array, PLANE, split_axis=0, concat_axis=0, tiled=True)  16.4 us
    ppermute x6, starting transfers between devices, exchange(): lax.ppermute(tiles[t], QUAD, [(i, i ^ t) for i in range(4)])  10 us
    ppermute x14, waiting for transfers between devices, up(): lax.ppermute(array, 'z', [(i, (i + 1) % PLANES) for i in range(PLANES)])  8.17 us
    ppermute x14, waiting for transfers between devices, down(): lax.ppermute(array, 'z', [(i, (i - 1) % PLANES) for i in range(PLANES)])  6.32 us
    ppermute x6, waiting for transfers between devices, exchange(): lax.ppermute(tiles[t], QUAD, [(i, i ^ t) for i in range(4)])  4.06 us
    ppermute x14, starting transfers between devices, up(): lax.ppermute(array, 'z', [(i, (i + 1) % PLANES) for i in range(PLANES)])  3.45 us
  transfers between devices with their start and end apart: 36, of which 13 were waited for; matrix products, arithmetic and copies ran while one was open for 1% of the time, Pallas kernels for 4%

profile of v5, /device:TPU:1, one launch (start us, length us, event | category | flops | bytes accessed | tf_op | source)
XLA Modules:
  0.0 123.1 jit_solution(3014517558539687478)
XLA Ops:
  0.6 1.7 %split_kv.1 = (bf16[128,256]{1,0:T(8,128)(2,1)}, bf16[128,256]{1,0:T(8,128)(2,1)}, bf16[128,256]{1,0:T(8,128)(2,1)}, bf16[128,256]{1,0:T(8,128)(2,1)}) custom-call(bf16[128,512]{1,0:T(8,128)(2,1)} %key_ref.1, bf16[128,512]{1,0:T(8,128)(2,1)} %value_ref.1), custom_call_target="tpu_custom_call" | custom-call | tf_op jit(solution)/shard_map/split_kv/pallas_call | solution.py:58
  2.3 3.2 %collective-permute-start = (bf16[128,256]{1,0:T(8,128)(2,1)}, bf16[128,256]{1,0:T(8,128)(2,1)S(1)}, u32[]{:S(2)}, u32[]{:S(2)}) collective-permute-start(bf16[128,256]{1,0:T(8,128)(2,1)} %get-tuple-element.40), channel_id=1, source_target_pairs={{0,8},{8,0},{128,136},{136,128},{1,9},{9,1},{129,137},{137,129},{2... | collective-permute-start | bytes 196616 | tf_op jit(solution)/shard_map/ppermute | solution.py:203
  5.6 1.0 collective-permute-start.1
  6.6 2.1 %collective-permute-start.2 = (bf16[128,256]{1,0:T(8,128)(2,1)}, bf16[128,256]{1,0:T(8,128)(2,1)S(1)}, u32[]{:S(2)}, u32[]{:S(2)}) collective-permute-start(bf16[128,256]{1,0:T(8,128)(2,1)} %get-tuple-element.42), channel_id=1, source_target_pairs={{0,136},{8,128},{128,8},{136,0},{1,137},{9,129},{129,9},{137,1},{2... | collective-permute-start | bytes 196616 | tf_op jit(solution)/shard_map/ppermute | solution.py:203
  8.7 3.2 %split_heads.1 = bf16[32,128,256]{2,1,0:T(8,128)(2,1)} custom-call(bf16[128,4096]{1,0:T(8,128)(2,1)} %query_ref.1, bf16[128,4096]{1,0:T(8,128)(2,1)} %d_out_ref.1), custom_call_target="tpu_custom_call" | custom-call | tf_op jit(solution)/shard_map/split_heads/pallas_call | solution.py:80
  11.9 0.6 collective-permute-done.2
  12.5 5.8 %all-to-all-start = ((bf16[32,128,256]{2,1,0:T(8,128)(2,1)}), bf16[32,128,256]{2,1,0:T(8,128)(2,1)S(1)}, u32[]{:S(2)}, u32[]{:S(2)}) async-start(bf16[32,128,256]{2,1,0:T(8,128)(2,1)} %split_heads.1), calls=%async_computation | async-start | bytes 4194304 | tf_op jit(solution)/shard_map/all_to_all | solution.py:231
  18.4 1.7 %collective-permute-start.6 = (bf16[4,128,128]{2,1,0:T(8,128)(2,1)S(1)}, bf16[4,128,128]{2,1,0:T(8,128)(2,1)S(1)}, u32[]{:S(2)}, u32[]{:S(2)}) collective-permute-start(bf16[4,128,128]{2,1,0:T(8,128)(2,1)S(1)} %pad_maximum_fusion.refs_0_), channel_id=1, source_target_pairs={{0,16},{16,32},{32,48},{48,64},{64,80},{80,96},{96,112},{112,0},{1... | collective-permute-start | bytes 393224 | tf_op jit(solution)/shard_map/ppermute | solution.py:194
  20.2 4.0 %collective-permute-start.10 = (bf16[4,128,128]{2,1,0:T(8,128)(2,1)S(1)}, bf16[4,128,128]{2,1,0:T(8,128)(2,1)S(1)}, u32[]{:S(2)}, u32[]{:S(2)}) collective-permute-start(bf16[4,128,128]{2,1,0:T(8,128)(2,1)S(1)} %pad_maximum_fusion.1.refs_8_), channel_id=1, source_target_pairs={{0,112},{16,0},{32,16},{48,32},{64,48},{80,64},{96,80},{112,96},{1... | collective-permute-start | bytes 393224 | tf_op jit(solution)/shard_map/ppermute | solution.py:198
  24.2 1.4 %collective-permute-start.3 = (bf16[4,128,128]{2,1,0:T(8,128)(2,1)S(1)}, bf16[4,128,128]{2,1,0:T(8,128)(2,1)S(1)}, u32[]{:S(2)}, u32[]{:S(2)}) collective-permute-start(bf16[4,128,128]{2,1,0:T(8,128)(2,1)S(1)} %pad_maximum_fusion.refs_0_), channel_id=1, source_target_pairs={{0,112},{16,0},{32,16},{48,32},{64,48},{80,64},{96,80},{112,96},{1... | collective-permute-start | bytes 393224 | tf_op jit(solution)/shard_map/ppermute | solution.py:198
  25.7 2.1 %collective-permute-done.6.refs_7_ = bf16[4,128,128]{2,1,0:T(8,128)(2,1)S(1)} collective-permute-done((bf16[4,128,128]{2,1,0:T(8,128)(2,1)S(1)}, bf16[4,128,128]{2,1,0:T(8,128)(2,1)S(1)}, u32[]{:S(2)}, u32[]{:S(2)}) %collective-permute-start.6) | collective-permute-done | bytes 131104 | tf_op jit(solution)/shard_map/ppermute | solution.py:194
  27.8 2.7 %collective-permute-start.11 = (bf16[4,128,128]{2,1,0:T(8,128)(2,1)S(1)}, bf16[4,128,128]{2,1,0:T(8,128)(2,1)S(1)}, u32[]{:S(2)}, u32[]{:S(2)}) collective-permute-start(bf16[4,128,128]{2,1,0:T(8,128)(2,1)S(1)} %collective-permute-done.10.refs_9_), channel_id=1, source_target_pairs={{0,112},{16,0},{32,16},{48,32},{64,48},{80,64},{96,80},{112,96},{1... | collective-permute-start | bytes 393224 | tf_op jit(solution)/shard_map/ppermute | solution.py:198
  30.5 2.6 %collective-permute-start.4 = (bf16[4,128,128]{2,1,0:T(8,128)(2,1)S(1)}, bf16[4,128,128]{2,1,0:T(8,128)(2,1)S(1)}, u32[]{:S(2)}, u32[]{:S(2)}) collective-permute-start(bf16[4,128,128]{2,1,0:T(8,128)(2,1)S(1)} %collective-permute-done.3.refs_1_), channel_id=1, source_target_pairs={{0,112},{16,0},{32,16},{48,32},{64,48},{80,64},{96,80},{112,96},{1... | collective-permute-start | bytes 393224 | tf_op jit(solution)/shard_map/ppermute | solution.py:198
  33.1 1.4 %collective-permute-done.7.refs_6_ = bf16[4,128,128]{2,1,0:T(8,128)(2,1)S(1)} collective-permute-done((bf16[4,128,128]{2,1,0:T(8,128)(2,1)S(1)}, bf16[4,128,128]{2,1,0:T(8,128)(2,1)S(1)}, u32[]{:S(2)}, u32[]{:S(2)}) %collective-permute-start.7) | collective-permute-done | bytes 131104 | tf_op jit(solution)/shard_map/ppermute | solution.py:194
  34.5 2.7 %collective-permute-start.12 = (bf16[4,128,128]{2,1,0:T(8,128)(2,1)S(1)}, bf16[4,128,128]{2,1,0:T(8,128)(2,1)S(1)}, u32[]{:S(2)}, u32[]{:S(2)}) collective-permute-start(bf16[4,128,128]{2,1,0:T(8,128)(2,1)S(1)} %collective-permute-done.11.refs_10_), channel_id=1, source_target_pairs={{0,112},{16,0},{32,16},{48,32},{64,48},{80,64},{96,80},{112,96},{1... | collective-permute-start | bytes 393224 | tf_op jit(solution)/shard_map/ppermute | solution.py:198
  37.2 2.6 %collective-permute-start.5 = (bf16[4,128,128]{2,1,0:T(8,128)(2,1)S(1)}, bf16[4,128,128]{2,1,0:T(8,128)(2,1)S(1)}, u32[]{:S(2)}, u32[]{:S(2)}) collective-permute-start(bf16[4,128,128]{2,1,0:T(8,128)(2,1)S(1)} %collective-permute-done.4.refs_2_), channel_id=1, source_target_pairs={{0,112},{16,0},{32,16},{48,32},{64,48},{80,64},{96,80},{112,96},{1... | collective-permute-start | bytes 393224 | tf_op jit(solution)/shard_map/ppermute | solution.py:198
  39.8 1.0 collective-permute-done.8.refs_5_
  40.8 2.7 %collective-permute-start.13 = (bf16[4,128,128]{2,1,0:T(8,128)(2,1)S(1)}, bf16[4,128,128]{2,1,0:T(8,128)(2,1)}, u32[]{:S(2)}, u32[]{:S(2)}) collective-permute-start(bf16[4,128,128]{2,1,0:T(8,128)(2,1)S(1)} %collective-permute-done.12.refs_11_), channel_id=1, source_target_pairs={{0,112},{16,0},{32,16},{48,32},{64,48},{80,64},{96,80},{112,96},{1... | collective-permute-start | bytes 393224 | tf_op jit(solution)/shard_map/ppermute | solution.py:198
  43.5 1.6 %collective-permute-done.16.refs_13_ = bf16[4,128,128]{2,1,0:T(8,128)(2,1)S(1)} collective-permute-done((bf16[4,128,128]{2,1,0:T(8,128)(2,1)S(1)}, bf16[4,128,128]{2,1,0:T(8,128)(2,1)S(1)}, u32[]{:S(2)}, u32[]{:S(2)}) %collective-permute-start.16) | collective-permute-done | bytes 131104 | tf_op jit(solution)/shard_map/ppermute | solution.py:194
  45.1 1.8 %collective-permute-done.9.refs_4_ = bf16[4,128,128]{2,1,0:T(8,128)(2,1)S(1)} collective-permute-done((bf16[4,128,128]{2,1,0:T(8,128)(2,1)S(1)}, bf16[4,128,128]{2,1,0:T(8,128)(2,1)S(1)}, u32[]{:S(2)}, u32[]{:S(2)}) %collective-permute-start.9) | collective-permute-done | bytes 131104 | tf_op jit(solution)/shard_map/ppermute | solution.py:194
  47.0 0.6 copy-done.31
  47.7 1.2 copy-done
  48.9 24.5 %attention.1 = (bf16[32,128,256]{2,1,0:T(8,128)(2,1)}, bf16[4,128,128]{2,1,0:T(8,128)(2,1)}, bf16[4,128,128]{2,1,0:T(8,128)(2,1)}, bf16[4,128,128]{2,1,0:T(8,128...) custom-call(s32[256]{0:T(256)} %seg_ref.1, ...), custom_call_target="tpu_custom_call" | custom-call | flops 6442450944 | bytes 8388608 | tf_op jit(solution)/shard_map/attention/pallas_call | solution.py:176
  73.5 0.8 collective-permute-start.17
  74.3 10.7 %all-to-all-start.1 = ((bf16[32,128,256]{2,1,0:T(8,128)(2,1)}), bf16[32,128,256]{2,1,0:T(8,128)(2,1)S(1)}, u32[]{:S(2)}, u32[]{:S(2)}) async-start(bf16[32,128,256]{2,1,0:T(8,128)(2,1)} %get-tuple-element.48), calls=%async_computation.1 | async-start | bytes 4194304 | tf_op jit(solution)/shard_map/all_to_all | solution.py:231
  85.0 1.4 %collective-permute-start.21 = (bf16[4,128,128]{2,1,0:T(8,128)(2,1)S(1)}, bf16[4,128,128]{2,1,0:T(8,128)(2,1)S(1)}, u32[]{:S(2)}, u32[]{:S(2)}) collective-permute-start(bf16[4,128,128]{2,1,0:T(8,128)(2,1)S(1)} %copy-done.29), channel_id=1, source_target_pairs={{0,112},{16,0},{32,16},{48,32},{64,48},{80,64},{96,80},{112,96},{1... | collective-permute-start | bytes 393224 | tf_op jit(solution)/shard_map/ppermute | solution.py:198
  86.4 0.5 collective-permute-start.24
  87.0 2.2 %collective-permute-start.27 = (bf16[4,128,128]{2,1,0:T(8,128)(2,1)S(1)}, bf16[4,128,128]{2,1,0:T(8,128)(2,1)S(1)}, u32[]{:S(2)}, u32[]{:S(2)}) collective-permute-start(bf16[4,128,128]{2,1,0:T(8,128)(2,1)S(1)} %copy-done.24), channel_id=1, source_target_pairs={{0,112},{16,0},{32,16},{48,32},{64,48},{80,64},{96,80},{112,96},{1... | collective-permute-start | bytes 393224 | tf_op jit(solution)/shard_map/ppermute | solution.py:198
  89.3 1.3 %collective-permute-done.21 = bf16[4,128,128]{2,1,0:T(8,128)(2,1)S(1)} collective-permute-done((bf16[4,128,128]{2,1,0:T(8,128)(2,1)S(1)}, bf16[4,128,128]{2,1,0:T(8,128)(2,1)S(1)}, u32[]{:S(2)}, u32[]{:S(2)}) %collective-permute-start.21) | collective-permute-done | bytes 131104 | tf_op jit(solution)/shard_map/ppermute | solution.py:198
  90.6 2.2 %collective-permute-start.22 = (bf16[4,128,128]{2,1,0:T(8,128)(2,1)S(1)}, bf16[4,128,128]{2,1,0:T(8,128)(2,1)S(1)}, u32[]{:S(2)}, u32[]{:S(2)}) collective-permute-start(bf16[4,128,128]{2,1,0:T(8,128)(2,1)S(1)} %add_convert_fusion.6), channel_id=1, source_target_pairs={{0,112},{16,0},{32,16},{48,32},{64,48},{80,64},{96,80},{112,96},{1... | collective-permute-start | bytes 393224 | tf_op jit(solution)/shard_map/ppermute | solution.py:198
  92.9 0.1 collective-permute-start.25
  93.0 0.4 collective-permute-done.27
  93.4 2.4 %collective-permute-start.28 = (bf16[4,128,128]{2,1,0:T(8,128)(2,1)S(1)}, bf16[4,128,128]{2,1,0:T(8,128)(2,1)S(1)}, u32[]{:S(2)}, u32[]{:S(2)}) collective-permute-start(bf16[4,128,128]{2,1,0:T(8,128)(2,1)S(1)} %add_convert_fusion.2), channel_id=1, source_target_pairs={{0,112},{16,0},{32,16},{48,32},{64,48},{80,64},{96,80},{112,96},{1... | collective-permute-start | bytes 393224 | tf_op jit(solution)/shard_map/ppermute | solution.py:198
  95.8 0.1 collective-permute-start.19
  96.0 2.7 %collective-permute-start.23 = (bf16[4,128,128]{2,1,0:T(8,128)(2,1)S(1)}, bf16[4,128,128]{2,1,0:T(8,128)(2,1)S(1)}, u32[]{:S(2)}, u32[]{:S(2)}) collective-permute-start(bf16[4,128,128]{2,1,0:T(8,128)(2,1)S(1)} %add_convert_fusion.5), channel_id=1, source_target_pairs={{0,112},{16,0},{32,16},{48,32},{64,48},{80,64},{96,80},{112,96},{1... | collective-permute-start | bytes 393224 | tf_op jit(solution)/shard_map/ppermute | solution.py:198
  98.8 0.1 collective-permute-start.26
  98.9 2.7 %collective-permute-start.29 = (bf16[4,128,128]{2,1,0:T(8,128)(2,1)S(1)}, bf16[4,128,128]{2,1,0:T(8,128)(2,1)S(1)}, u32[]{:S(2)}, u32[]{:S(2)}) collective-permute-start(bf16[4,128,128]{2,1,0:T(8,128)(2,1)S(1)} %add_convert_fusion.1), channel_id=1, source_target_pairs={{0,112},{16,0},{32,16},{48,32},{64,48},{80,64},{96,80},{112,96},{1... | collective-permute-start | bytes 393224 | tf_op jit(solution)/shard_map/ppermute | solution.py:198
  101.8 2.9 %collective-permute-done.29 = bf16[4,128,128]{2,1,0:T(8,128)(2,1)S(1)} collective-permute-done((bf16[4,128,128]{2,1,0:T(8,128)(2,1)S(1)}, bf16[4,128,128]{2,1,0:T(8,128)(2,1)S(1)}, u32[]{:S(2)}, u32[]{:S(2)}) %collective-permute-start.29) | collective-permute-done | bytes 131104 | tf_op jit(solution)/shard_map/ppermute | solution.py:198
  104.8 3.5 %collective-permute-start.30 = (bf16[4,128,128]{2,1,0:T(8,128)(2,1)S(1)}, bf16[4,128,128]{2,1,0:T(8,128)(2,1)S(1)}, u32[]{:S(2)}, u32[]{:S(2)}) collective-permute-start(bf16[4,128,128]{2,1,0:T(8,128)(2,1)S(1)} %add_convert_fusion), channel_id=1, source_target_pairs={{0,112},{16,0},{32,16},{48,32},{64,48},{80,64},{96,80},{112,96},{1... | collective-permute-start | bytes 393224 | tf_op jit(solution)/shard_map/ppermute | solution.py:198
  108.3 0.2 collective-permute-done.20
  108.5 1.7 %collective-permute-done.30 = bf16[4,128,128]{2,1,0:T(8,128)(2,1)S(1)} collective-permute-done((bf16[4,128,128]{2,1,0:T(8,128)(2,1)S(1)}, bf16[4,128,128]{2,1,0:T(8,128)(2,1)S(1)}, u32[]{:S(2)}, u32[]{:S(2)}) %collective-permute-start.30) | collective-permute-done | bytes 131104 | tf_op jit(solution)/shard_map/ppermute | solution.py:198
  110.3 3.0 %all-to-all-done.1.tiles = bf16[32,128,256]{2,1,0:T(8,128)(2,1)S(1)} async-done(((bf16[32,128,256]{2,1,0:T(8,128)(2,1)}), bf16[32,128,256]{2,1,0:T(8,128)(2,1)S(1)}, u32[]{:S(2)}, u32[]{:S(2)}) %all-to-all-start.1) | async-done | bytes 2097184 | tf_op jit(solution)/shard_map/all_to_all | solution.py:231
  113.3 0.4 collective-permute-start.31
  113.8 3.0 %collective-permute-start.32 = (bf16[128,256]{1,0:T(8,128)(2,1)S(1)}, bf16[128,256]{1,0:T(8,128)(2,1)S(1)}, u32[]{:S(2)}, u32[]{:S(2)}) collective-permute-start(bf16[128,256]{1,0:T(8,128)(2,1)S(1)} %pad_maximum_fusion.4), channel_id=1, source_target_pairs={{0,128},{8,136},{128,0},{136,8},{1,129},{9,137},{129,1},{137,9},{2... | collective-permute-start | bytes 196616 | tf_op jit(solution)/shard_map/ppermute | solution.py:203
  116.8 0.2 collective-permute-start.33
  117.0 1.9 %join_heads.1 = (bf16[128,4096]{1,0:T(8,128)(2,1)}, bf16[128,4096]{1,0:T(8,128)(2,1)}) custom-call(bf16[32,128,256]{2,1,0:T(8,128)(2,1)S(1)} %all-to-all-done.1.tiles), custom_call_target="tpu_custom_call" | custom-call | tf_op jit(solution)/shard_map/join_heads/pallas_call | solution.py:91
  119.0 3.4 %collective-permute-done.33.refs_3_ = bf16[128,256]{1,0:T(8,128)(2,1)S(1)} collective-permute-done((bf16[128,256]{1,0:T(8,128)(2,1)S(1)}, bf16[128,256]{1,0:T(8,128)(2,1)S(1)}, u32[]{:S(2)}, u32[]{:S(2)}) %collective-permute-start.33) | collective-permute-done | bytes 65568 | tf_op jit(solution)/shard_map/ppermute | solution.py:203
  122.4 0.7 join_kv.1
  (113 shorter events, 1.1 us)
Async XLA Ops:
  2.3 9.6 %collective-permute-start = (bf16[128,256]{1,0:T(8,128)(2,1)}, bf16[128,256]{1,0:T(8,128)(2,1)S(1)}, u32[]{:S(2)}, u32[]{:S(2)}) collective-permute-start(bf16[128,256]{1,0:T(8,128)(2,1)} %get-tuple-element.40), channel_id=1, source_target_pairs={{0,8},{8,0},{128,136},{136,128},{1,9},{9,1},{129,137},{137,129},{2... | collective-permute-start | bytes 196616 | tf_op jit(solution)/shard_map/ppermute | solution.py:203
  5.6 6.4 %collective-permute-start.1 = (bf16[128,256]{1,0:T(8,128)(2,1)}, bf16[128,256]{1,0:T(8,128)(2,1)S(1)}, u32[]{:S(2)}, u32[]{:S(2)}) collective-permute-start(bf16[128,256]{1,0:T(8,128)(2,1)} %get-tuple-element.41), channel_id=1, source_target_pairs={{0,128},{8,136},{128,0},{136,8},{1,129},{9,137},{129,1},{137,9},{2... | collective-permute-start | bytes 196616 | tf_op jit(solution)/shard_map/ppermute | solution.py:203
  6.6 5.9 %collective-permute-start.2 = (bf16[128,256]{1,0:T(8,128)(2,1)}, bf16[128,256]{1,0:T(8,128)(2,1)S(1)}, u32[]{:S(2)}, u32[]{:S(2)}) collective-permute-start(bf16[128,256]{1,0:T(8,128)(2,1)} %get-tuple-element.42), channel_id=1, source_target_pairs={{0,136},{8,128},{128,8},{136,0},{1,137},{9,129},{129,9},{137,1},{2... | collective-permute-start | bytes 196616 | tf_op jit(solution)/shard_map/ppermute | solution.py:203
  12.5 35.1 %all-to-all-start = ((bf16[32,128,256]{2,1,0:T(8,128)(2,1)}), bf16[32,128,256]{2,1,0:T(8,128)(2,1)S(1)}, u32[]{:S(2)}, u32[]{:S(2)}) async-start(bf16[32,128,256]{2,1,0:T(8,128)(2,1)} %split_heads.1), calls=%async_computation | async-start | bytes 4194304 | tf_op jit(solution)/shard_map/all_to_all | solution.py:231
  18.4 29.2 %copy-start.11 = (bf16[4,128,128]{2,1,0:T(8,128)(2,1)}, bf16[4,128,128]{2,1,0:T(8,128)(2,1)S(1)}, u32[]{:S(2)}) copy-start(bf16[4,128,128]{2,1,0:T(8,128)(2,1)S(1)} %pad_maximum_fusion.refs_0_) | copy-start | bytes 393220
  18.4 9.4 %collective-permute-start.6 = (bf16[4,128,128]{2,1,0:T(8,128)(2,1)S(1)}, bf16[4,128,128]{2,1,0:T(8,128)(2,1)S(1)}, u32[]{:S(2)}, u32[]{:S(2)}) collective-permute-start(bf16[4,128,128]{2,1,0:T(8,128)(2,1)S(1)} %pad_maximum_fusion.refs_0_), channel_id=1, source_target_pairs={{0,16},{16,32},{32,48},{48,64},{64,80},{80,96},{96,112},{112,0},{1... | collective-permute-start | bytes 393224 | tf_op jit(solution)/shard_map/ppermute | solution.py:194
  20.2 27.5 %copy-start.12 = (bf16[4,128,128]{2,1,0:T(8,128)(2,1)}, bf16[4,128,128]{2,1,0:T(8,128)(2,1)S(1)}, u32[]{:S(2)}) copy-start(bf16[4,128,128]{2,1,0:T(8,128)(2,1)S(1)} %pad_maximum_fusion.1.refs_8_) | copy-start | bytes 393220
  20.2 7.6 %collective-permute-start.10 = (bf16[4,128,128]{2,1,0:T(8,128)(2,1)S(1)}, bf16[4,128,128]{2,1,0:T(8,128)(2,1)S(1)}, u32[]{:S(2)}, u32[]{:S(2)}) collective-permute-start(bf16[4,128,128]{2,1,0:T(8,128)(2,1)S(1)} %pad_maximum_fusion.1.refs_8_), channel_id=1, source_target_pairs={{0,112},{16,0},{32,16},{48,32},{64,48},{80,64},{96,80},{112,96},{1... | collective-permute-start | bytes 393224 | tf_op jit(solution)/shard_map/ppermute | solution.py:198
  24.2 6.3 %collective-permute-start.3 = (bf16[4,128,128]{2,1,0:T(8,128)(2,1)S(1)}, bf16[4,128,128]{2,1,0:T(8,128)(2,1)S(1)}, u32[]{:S(2)}, u32[]{:S(2)}) collective-permute-start(bf16[4,128,128]{2,1,0:T(8,128)(2,1)S(1)} %pad_maximum_fusion.refs_0_), channel_id=1, source_target_pairs={{0,112},{16,0},{32,16},{48,32},{64,48},{80,64},{96,80},{112,96},{1... | collective-permute-start | bytes 393224 | tf_op jit(solution)/shard_map/ppermute | solution.py:198
  25.7 7.4 %collective-permute-start.14 = (bf16[4,128,128]{2,1,0:T(8,128)(2,1)S(1)}, bf16[4,128,128]{2,1,0:T(8,128)(2,1)S(1)}, u32[]{:S(2)}, u32[]{:S(2)}) collective-permute-start(bf16[4,128,128]{2,1,0:T(8,128)(2,1)S(1)} %pad_maximum_fusion.1.refs_8_), channel_id=1, source_target_pairs={{0,16},{16,32},{32,48},{48,64},{64,80},{80,96},{96,112},{112,0},{1... | collective-permute-start | bytes 393224 | tf_op jit(solution)/shard_map/ppermute | solution.py:194
  27.8 19.8 %copy-start.16 = (bf16[4,128,128]{2,1,0:T(8,128)(2,1)}, bf16[4,128,128]{2,1,0:T(8,128)(2,1)S(1)}, u32[]{:S(2)}) copy-start(bf16[4,128,128]{2,1,0:T(8,128)(2,1)S(1)} %collective-permute-done.6.refs_7_) | copy-start | bytes 393220
  27.8 6.7 %collective-permute-start.7 = (bf16[4,128,128]{2,1,0:T(8,128)(2,1)S(1)}, bf16[4,128,128]{2,1,0:T(8,128)(2,1)S(1)}, u32[]{:S(2)}, u32[]{:S(2)}) collective-permute-start(bf16[4,128,128]{2,1,0:T(8,128)(2,1)S(1)} %collective-permute-done.6.refs_7_), channel_id=1, source_target_pairs={{0,16},{16,32},{32,48},{48,64},{64,80},{80,96},{96,112},{112,0},{1... | collective-permute-start | bytes 393224 | tf_op jit(solution)/shard_map/ppermute | solution.py:194
  27.8 19.8 %copy-start.17 = (bf16[4,128,128]{2,1,0:T(8,128)(2,1)}, bf16[4,128,128]{2,1,0:T(8,128)(2,1)S(1)}, u32[]{:S(2)}) copy-start(bf16[4,128,128]{2,1,0:T(8,128)(2,1)S(1)} %collective-permute-done.10.refs_9_) | copy-start | bytes 393220
  27.8 6.7 %collective-permute-start.11 = (bf16[4,128,128]{2,1,0:T(8,128)(2,1)S(1)}, bf16[4,128,128]{2,1,0:T(8,128)(2,1)S(1)}, u32[]{:S(2)}, u32[]{:S(2)}) collective-permute-start(bf16[4,128,128]{2,1,0:T(8,128)(2,1)S(1)} %collective-permute-done.10.refs_9_), channel_id=1, source_target_pairs={{0,112},{16,0},{32,16},{48,32},{64,48},{80,64},{96,80},{112,96},{1... | collective-permute-start | bytes 393224 | tf_op jit(solution)/shard_map/ppermute | solution.py:198
  30.5 17.2 %copy-start.18 = (bf16[4,128,128]{2,1,0:T(8,128)(2,1)}, bf16[4,128,128]{2,1,0:T(8,128)(2,1)S(1)}, u32[]{:S(2)}) copy-start(bf16[4,128,128]{2,1,0:T(8,128)(2,1)S(1)} %collective-permute-done.3.refs_1_) | copy-start | bytes 393220
  30.5 6.7 %collective-permute-start.4 = (bf16[4,128,128]{2,1,0:T(8,128)(2,1)S(1)}, bf16[4,128,128]{2,1,0:T(8,128)(2,1)S(1)}, u32[]{:S(2)}, u32[]{:S(2)}) collective-permute-start(bf16[4,128,128]{2,1,0:T(8,128)(2,1)S(1)} %collective-permute-done.3.refs_1_), channel_id=1, source_target_pairs={{0,112},{16,0},{32,16},{48,32},{64,48},{80,64},{96,80},{112,96},{1... | collective-permute-start | bytes 393224 | tf_op jit(solution)/shard_map/ppermute | solution.py:198
  33.1 6.7 %collective-permute-start.15 = (bf16[4,128,128]{2,1,0:T(8,128)(2,1)S(1)}, bf16[4,128,128]{2,1,0:T(8,128)(2,1)S(1)}, u32[]{:S(2)}, u32[]{:S(2)}) collective-permute-start(bf16[4,128,128]{2,1,0:T(8,128)(2,1)S(1)} %collective-permute-done.14.refs_15_), channel_id=1, source_target_pairs={{0,16},{16,32},{32,48},{48,64},{64,80},{80,96},{96,112},{112,0},{1... | collective-permute-start | bytes 393224 | tf_op jit(solution)/shard_map/ppermute | solution.py:194
  34.5 6.3 %collective-permute-start.8 = (bf16[4,128,128]{2,1,0:T(8,128)(2,1)S(1)}, bf16[4,128,128]{2,1,0:T(8,128)(2,1)S(1)}, u32[]{:S(2)}, u32[]{:S(2)}) collective-permute-start(bf16[4,128,128]{2,1,0:T(8,128)(2,1)S(1)} %collective-permute-done.7.refs_6_), channel_id=1, source_target_pairs={{0,16},{16,32},{32,48},{48,64},{64,80},{80,96},{96,112},{112,0},{1... | collective-permute-start | bytes 393224 | tf_op jit(solution)/shard_map/ppermute | solution.py:194
  34.5 6.3 %collective-permute-start.12 = (bf16[4,128,128]{2,1,0:T(8,128)(2,1)S(1)}, bf16[4,128,128]{2,1,0:T(8,128)(2,1)S(1)}, u32[]{:S(2)}, u32[]{:S(2)}) collective-permute-start(bf16[4,128,128]{2,1,0:T(8,128)(2,1)S(1)} %collective-permute-done.11.refs_10_), channel_id=1, source_target_pairs={{0,112},{16,0},{32,16},{48,32},{64,48},{80,64},{96,80},{112,96},{1... | collective-permute-start | bytes 393224 | tf_op jit(solution)/shard_map/ppermute | solution.py:198
  37.2 6.3 %collective-permute-start.5 = (bf16[4,128,128]{2,1,0:T(8,128)(2,1)S(1)}, bf16[4,128,128]{2,1,0:T(8,128)(2,1)S(1)}, u32[]{:S(2)}, u32[]{:S(2)}) collective-permute-start(bf16[4,128,128]{2,1,0:T(8,128)(2,1)S(1)} %collective-permute-done.4.refs_2_), channel_id=1, source_target_pairs={{0,112},{16,0},{32,16},{48,32},{64,48},{80,64},{96,80},{112,96},{1... | collective-permute-start | bytes 393224 | tf_op jit(solution)/shard_map/ppermute | solution.py:198
  39.8 5.3 %collective-permute-start.16 = (bf16[4,128,128]{2,1,0:T(8,128)(2,1)S(1)}, bf16[4,128,128]{2,1,0:T(8,128)(2,1)S(1)}, u32[]{:S(2)}, u32[]{:S(2)}) collective-permute-start(bf16[4,128,128]{2,1,0:T(8,128)(2,1)S(1)} %collective-permute-done.15.refs_14_), channel_id=1, source_target_pairs={{0,16},{16,32},{32,48},{48,64},{64,80},{80,96},{96,112},{112,0},{1... | collective-permute-start | bytes 393224 | tf_op jit(solution)/shard_map/ppermute | solution.py:194
  40.8 6.2 %collective-permute-start.9 = (bf16[4,128,128]{2,1,0:T(8,128)(2,1)S(1)}, bf16[4,128,128]{2,1,0:T(8,128)(2,1)S(1)}, u32[]{:S(2)}, u32[]{:S(2)}) collective-permute-start(bf16[4,128,128]{2,1,0:T(8,128)(2,1)S(1)} %collective-permute-done.8.refs_5_), channel_id=1, source_target_pairs={{0,16},{16,32},{32,48},{48,64},{64,80},{80,96},{96,112},{112,0},{1... | collective-permute-start | bytes 393224 | tf_op jit(solution)/shard_map/ppermute | solution.py:194
  40.8 6.8 %collective-permute-start.13 = (bf16[4,128,128]{2,1,0:T(8,128)(2,1)S(1)}, bf16[4,128,128]{2,1,0:T(8,128)(2,1)}, u32[]{:S(2)}, u32[]{:S(2)}) collective-permute-start(bf16[4,128,128]{2,1,0:T(8,128)(2,1)S(1)} %collective-permute-done.12.refs_11_), channel_id=1, source_target_pairs={{0,112},{16,0},{32,16},{48,32},{64,48},{80,64},{96,80},{112,96},{1... | collective-permute-start | bytes 393224 | tf_op jit(solution)/shard_map/ppermute | solution.py:198
  73.5 15.7 %collective-permute-start.17 = (bf16[4,128,128]{2,1,0:T(8,128)(2,1)}, bf16[4,128,128]{2,1,0:T(8,128)(2,1)S(1)}, u32[]{:S(2)}, u32[]{:S(2)}) collective-permute-start(bf16[4,128,128]{2,1,0:T(8,128)(2,1)} %get-tuple-element.53), channel_id=1, source_target_pairs={{0,16},{16,32},{32,48},{48,64},{64,80},{80,96},{96,112},{112,0},{1... | collective-permute-start | bytes 393224 | tf_op jit(solution)/shard_map/ppermute | solution.py:194
  74.2 18.6 %copy-start.8 = (bf16[4,128,128]{2,1,0:T(8,128)(2,1)S(1)}, bf16[4,128,128]{2,1,0:T(8,128)(2,1)}, u32[]{:S(2)}) copy-start(bf16[4,128,128]{2,1,0:T(8,128)(2,1)} %get-tuple-element.59) | copy-start | bytes 393220
  74.3 19.1 %copy-start.7 = (bf16[4,128,128]{2,1,0:T(8,128)(2,1)S(1)}, bf16[4,128,128]{2,1,0:T(8,128)(2,1)}, u32[]{:S(2)}) copy-start(bf16[4,128,128]{2,1,0:T(8,128)(2,1)} %get-tuple-element.63) | copy-start | bytes 393220
  74.3 21.5 %copy-start.6 = (bf16[4,128,128]{2,1,0:T(8,128)(2,1)S(1)}, bf16[4,128,128]{2,1,0:T(8,128)(2,1)}, u32[]{:S(2)}) copy-start(bf16[4,128,128]{2,1,0:T(8,128)(2,1)} %get-tuple-element.51) | copy-start | bytes 393220
  74.3 21.7 %copy-start.5 = (bf16[4,128,128]{2,1,0:T(8,128)(2,1)S(1)}, bf16[4,128,128]{2,1,0:T(8,128)(2,1)}, u32[]{:S(2)}) copy-start(bf16[4,128,128]{2,1,0:T(8,128)(2,1)} %get-tuple-element.54) | copy-start | bytes 393220
  74.3 39.0 %all-to-all-start.1 = ((bf16[32,128,256]{2,1,0:T(8,128)(2,1)}), bf16[32,128,256]{2,1,0:T(8,128)(2,1)S(1)}, u32[]{:S(2)}, u32[]{:S(2)}) async-start(bf16[32,128,256]{2,1,0:T(8,128)(2,1)} %get-tuple-element.48), calls=%async_computation.1 | async-start | bytes 4194304 | tf_op jit(solution)/shard_map/all_to_all | solution.py:231
  85.0 19.7 %copy-start.1 = (bf16[4,128,128]{2,1,0:T(8,128)(2,1)S(1)}, bf16[4,128,128]{2,1,0:T(8,128)(2,1)}, u32[]{:S(2)}) copy-start(bf16[4,128,128]{2,1,0:T(8,128)(2,1)} %get-tuple-element.61) | copy-start | bytes 393220
  85.0 23.4 %copy-start.14 = (bf16[4,128,128]{2,1,0:T(8,128)(2,1)S(1)}, bf16[4,128,128]{2,1,0:T(8,128)(2,1)}, u32[]{:S(2)}) copy-start(bf16[4,128,128]{2,1,0:T(8,128)(2,1)} %get-tuple-element.49) | copy-start | bytes 393220
  85.0 5.5 %collective-permute-start.21 = (bf16[4,128,128]{2,1,0:T(8,128)(2,1)S(1)}, bf16[4,128,128]{2,1,0:T(8,128)(2,1)S(1)}, u32[]{:S(2)}, u32[]{:S(2)}) collective-permute-start(bf16[4,128,128]{2,1,0:T(8,128)(2,1)S(1)} %copy-done.29), channel_id=1, source_target_pairs={{0,112},{16,0},{32,16},{48,32},{64,48},{80,64},{96,80},{112,96},{1... | collective-permute-start | bytes 393224 | tf_op jit(solution)/shard_map/ppermute | solution.py:198
  86.4 6.4 %collective-permute-start.24 = (bf16[4,128,128]{2,1,0:T(8,128)(2,1)S(1)}, bf16[4,128,128]{2,1,0:T(8,128)(2,1)S(1)}, u32[]{:S(2)}, u32[]{:S(2)}) collective-permute-start(bf16[4,128,128]{2,1,0:T(8,128)(2,1)S(1)} %copy-done.27), channel_id=1, source_target_pairs={{0,16},{16,32},{32,48},{48,64},{64,80},{80,96},{96,112},{112,0},{1... | collective-permute-start | bytes 393224 | tf_op jit(solution)/shard_map/ppermute | solution.py:194
  87.0 6.4 %collective-permute-start.27 = (bf16[4,128,128]{2,1,0:T(8,128)(2,1)S(1)}, bf16[4,128,128]{2,1,0:T(8,128)(2,1)S(1)}, u32[]{:S(2)}, u32[]{:S(2)}) collective-permute-start(bf16[4,128,128]{2,1,0:T(8,128)(2,1)S(1)} %copy-done.24), channel_id=1, source_target_pairs={{0,112},{16,0},{32,16},{48,32},{64,48},{80,64},{96,80},{112,96},{1... | collective-permute-start | bytes 393224 | tf_op jit(solution)/shard_map/ppermute | solution.py:198
  89.2 21.0 %copy-start.13 = (bf16[4,128,128]{2,1,0:T(8,128)(2,1)S(1)}, bf16[4,128,128]{2,1,0:T(8,128)(2,1)}, u32[]{:S(2)}) copy-start(bf16[4,128,128]{2,1,0:T(8,128)(2,1)} %get-tuple-element.57) | copy-start | bytes 393220
  89.2 6.6 %collective-permute-start.18 = (bf16[4,128,128]{2,1,0:T(8,128)(2,1)S(1)}, bf16[4,128,128]{2,1,0:T(8,128)(2,1)S(1)}, u32[]{:S(2)}, u32[]{:S(2)}) collective-permute-start(bf16[4,128,128]{2,1,0:T(8,128)(2,1)S(1)} %add_convert_fusion.9), channel_id=1, source_target_pairs={{0,16},{16,32},{32,48},{48,64},{64,80},{80,96},{96,112},{112,0},{1... | collective-permute-start | bytes 393224 | tf_op jit(solution)/shard_map/ppermute | solution.py:194
  90.6 5.3 %collective-permute-start.22 = (bf16[4,128,128]{2,1,0:T(8,128)(2,1)S(1)}, bf16[4,128,128]{2,1,0:T(8,128)(2,1)S(1)}, u32[]{:S(2)}, u32[]{:S(2)}) collective-permute-start(bf16[4,128,128]{2,1,0:T(8,128)(2,1)S(1)} %add_convert_fusion.6), channel_id=1, source_target_pairs={{0,112},{16,0},{32,16},{48,32},{64,48},{80,64},{96,80},{112,96},{1... | collective-permute-start | bytes 393224 | tf_op jit(solution)/shard_map/ppermute | solution.py:198
  92.9 5.8 %collective-permute-start.25 = (bf16[4,128,128]{2,1,0:T(8,128)(2,1)S(1)}, bf16[4,128,128]{2,1,0:T(8,128)(2,1)S(1)}, u32[]{:S(2)}, u32[]{:S(2)}) collective-permute-start(bf16[4,128,128]{2,1,0:T(8,128)(2,1)S(1)} %add_convert_fusion.4), channel_id=1, source_target_pairs={{0,16},{16,32},{32,48},{48,64},{64,80},{80,96},{96,112},{112,0},{1... | collective-permute-start | bytes 393224 | tf_op jit(solution)/shard_map/ppermute | solution.py:194
  93.4 5.4 %collective-permute-start.28 = (bf16[4,128,128]{2,1,0:T(8,128)(2,1)S(1)}, bf16[4,128,128]{2,1,0:T(8,128)(2,1)S(1)}, u32[]{:S(2)}, u32[]{:S(2)}) collective-permute-start(bf16[4,128,128]{2,1,0:T(8,128)(2,1)S(1)} %add_convert_fusion.2), channel_id=1, source_target_pairs={{0,112},{16,0},{32,16},{48,32},{64,48},{80,64},{96,80},{112,96},{1... | collective-permute-start | bytes 393224 | tf_op jit(solution)/shard_map/ppermute | solution.py:198
  95.8 5.8 %collective-permute-start.19 = (bf16[4,128,128]{2,1,0:T(8,128)(2,1)S(1)}, bf16[4,128,128]{2,1,0:T(8,128)(2,1)S(1)}, u32[]{:S(2)}, u32[]{:S(2)}) collective-permute-start(bf16[4,128,128]{2,1,0:T(8,128)(2,1)S(1)} %add_convert_fusion.8), channel_id=1, source_target_pairs={{0,16},{16,32},{32,48},{48,64},{64,80},{80,96},{96,112},{112,0},{1... | collective-permute-start | bytes 393224 | tf_op jit(solution)/shard_map/ppermute | solution.py:194
  96.0 12.3 %collective-permute-start.23 = (bf16[4,128,128]{2,1,0:T(8,128)(2,1)S(1)}, bf16[4,128,128]{2,1,0:T(8,128)(2,1)S(1)}, u32[]{:S(2)}, u32[]{:S(2)}) collective-permute-start(bf16[4,128,128]{2,1,0:T(8,128)(2,1)S(1)} %add_convert_fusion.5), channel_id=1, source_target_pairs={{0,112},{16,0},{32,16},{48,32},{64,48},{80,64},{96,80},{112,96},{1... | collective-permute-start | bytes 393224 | tf_op jit(solution)/shard_map/ppermute | solution.py:198
  98.8 9.8 %collective-permute-start.26 = (bf16[4,128,128]{2,1,0:T(8,128)(2,1)S(1)}, bf16[4,128,128]{2,1,0:T(8,128)(2,1)S(1)}, u32[]{:S(2)}, u32[]{:S(2)}) collective-permute-start(bf16[4,128,128]{2,1,0:T(8,128)(2,1)S(1)} %add_convert_fusion.3), channel_id=1, source_target_pairs={{0,16},{16,32},{32,48},{48,64},{64,80},{80,96},{96,112},{112,0},{1... | collective-permute-start | bytes 393224 | tf_op jit(solution)/shard_map/ppermute | solution.py:194
  98.9 5.8 %collective-permute-start.29 = (bf16[4,128,128]{2,1,0:T(8,128)(2,1)S(1)}, bf16[4,128,128]{2,1,0:T(8,128)(2,1)S(1)}, u32[]{:S(2)}, u32[]{:S(2)}) collective-permute-start(bf16[4,128,128]{2,1,0:T(8,128)(2,1)S(1)} %add_convert_fusion.1), channel_id=1, source_target_pairs={{0,112},{16,0},{32,16},{48,32},{64,48},{80,64},{96,80},{112,96},{1... | collective-permute-start | bytes 393224 | tf_op jit(solution)/shard_map/ppermute | solution.py:198
  101.7 6.8 %collective-permute-start.20 = (bf16[4,128,128]{2,1,0:T(8,128)(2,1)S(1)}, bf16[4,128,128]{2,1,0:T(8,128)(2,1)S(1)}, u32[]{:S(2)}, u32[]{:S(2)}) collective-permute-start(bf16[4,128,128]{2,1,0:T(8,128)(2,1)S(1)} %add_convert_fusion.7), channel_id=1, source_target_pairs={{0,16},{16,32},{32,48},{48,64},{64,80},{80,96},{96,112},{112,0},{1... | collective-permute-start | bytes 393224 | tf_op jit(solution)/shard_map/ppermute | solution.py:194
  104.8 5.4 %collective-permute-start.30 = (bf16[4,128,128]{2,1,0:T(8,128)(2,1)S(1)}, bf16[4,128,128]{2,1,0:T(8,128)(2,1)S(1)}, u32[]{:S(2)}, u32[]{:S(2)}) collective-permute-start(bf16[4,128,128]{2,1,0:T(8,128)(2,1)S(1)} %add_convert_fusion), channel_id=1, source_target_pairs={{0,112},{16,0},{32,16},{48,32},{64,48},{80,64},{96,80},{112,96},{1... | collective-permute-start | bytes 393224 | tf_op jit(solution)/shard_map/ppermute | solution.py:198
  113.3 5.6 %collective-permute-start.31 = (bf16[128,256]{1,0:T(8,128)(2,1)S(1)}, bf16[128,256]{1,0:T(8,128)(2,1)S(1)}, u32[]{:S(2)}, u32[]{:S(2)}) collective-permute-start(bf16[128,256]{1,0:T(8,128)(2,1)S(1)} %pad_maximum_fusion.3), channel_id=1, source_target_pairs={{0,8},{8,0},{128,136},{136,128},{1,9},{9,1},{129,137},{137,129},{2... | collective-permute-start | bytes 196616 | tf_op jit(solution)/shard_map/ppermute | solution.py:203
  113.8 5.2 %collective-permute-start.32 = (bf16[128,256]{1,0:T(8,128)(2,1)S(1)}, bf16[128,256]{1,0:T(8,128)(2,1)S(1)}, u32[]{:S(2)}, u32[]{:S(2)}) collective-permute-start(bf16[128,256]{1,0:T(8,128)(2,1)S(1)} %pad_maximum_fusion.4), channel_id=1, source_target_pairs={{0,128},{8,136},{128,0},{136,8},{1,129},{9,137},{129,1},{137,9},{2... | collective-permute-start | bytes 196616 | tf_op jit(solution)/shard_map/ppermute | solution.py:203
  116.8 5.6 %collective-permute-start.33 = (bf16[128,256]{1,0:T(8,128)(2,1)S(1)}, bf16[128,256]{1,0:T(8,128)(2,1)S(1)}, u32[]{:S(2)}, u32[]{:S(2)}) collective-permute-start(bf16[128,256]{1,0:T(8,128)(2,1)S(1)} %pad_maximum_fusion.5), channel_id=1, source_target_pairs={{0,136},{8,128},{128,8},{136,0},{1,137},{9,129},{129,9},{137,1},{2... | collective-permute-start | bytes 196616 | tf_op jit(solution)/shard_map/ppermute | solution.py:203
  (20 other events, 196.8 us)

commit v6 on v5

--- a/solution.py
+++ b/solution.py
@@ -147,8 +147,8 @@
         dscore_b = (prob * (dprob - delta)).astype(BF16)
         key_t = jnp.concatenate([kt_ref[loc] for loc in locs], axis=1)
         yield
+        key_slots = nn(dscore_b, q)
         dq_t = nn(key_t, dscore_b) * FACTOR
-        key_slots = nn(dscore_b, q)
         yield
         od_ref[u, :, HEAD_DIM:] = dq_t.T.astype(BF16)
         for j in range(SPANS):

time: 124 us -> 122 us (0.984)
  Pallas kernels: 32.1 us -> 30 us
    pallas_call x1, Pallas kernels: 24.5 us -> 22.4 us  [attention(): call(attention_kernel, 'attention', [SMEM] * 2 + [step] + [VMEM] * 2 * PL...]
where the time goes in v6:
time: 122 us; the launch traced here: 121 us
  starting transfers between devices  65.7 us (54%)
  Pallas kernels  30 us (25%)
  waiting for transfers between devices  21.6 us (18%)
  local copies, waits for them, and re-layouts  2.02 us (2%)
    ppermute x14, starting transfers between devices, down(): lax.ppermute(array, 'z', [(i, (i - 1) % PLANES) for i in range(PLANES)])  35.7 us
    pallas_call x1, Pallas kernels, attention(): call(attention_kernel, 'attention', [SMEM] * 2 + [step] + [VMEM] * 2 * PL...  22.4 us
    all_to_all x2, starting transfers between devices, swap(): return lax.all_to_all(array, PLANE, split_axis=0, concat_axis=0, tiled=True)  16.4 us
    ppermute x6, starting transfers between devices, exchange(): lax.ppermute(tiles[t], QUAD, [(i, i ^ t) for i in range(4)])  10.1 us
    ppermute x14, waiting for transfers between devices, up(): lax.ppermute(array, 'z', [(i, (i + 1) % PLANES) for i in range(PLANES)])  8.17 us
    ppermute x14, waiting for transfers between devices, down(): lax.ppermute(array, 'z', [(i, (i - 1) % PLANES) for i in range(PLANES)])  6.34 us
    ppermute x6, waiting for transfers between devices, exchange(): lax.ppermute(tiles[t], QUAD, [(i, i ^ t) for i in range(4)])  4.06 us
    ppermute x14, starting transfers between devices, up(): lax.ppermute(array, 'z', [(i, (i + 1) % PLANES) for i in range(PLANES)])  3.45 us
  transfers between devices with their start and end apart: 36, of which 13 were waited for; matrix products, arithmetic and copies ran while one was open for 1% of the time, Pallas kernels for 4%

profile of v6, /device:TPU:1, one launch (start us, length us, event | category | flops | bytes accessed | tf_op | source)
XLA Modules:
  0.0 121.0 jit_solution(10813887138350210720)
XLA Ops:
  0.6 1.7 %split_kv.1 = (bf16[128,256]{1,0:T(8,128)(2,1)}, bf16[128,256]{1,0:T(8,128)(2,1)}, bf16[128,256]{1,0:T(8,128)(2,1)}, bf16[128,256]{1,0:T(8,128)(2,1)}) custom-call(bf16[128,512]{1,0:T(8,128)(2,1)} %key_ref.1, bf16[128,512]{1,0:T(8,128)(2,1)} %value_ref.1), custom_call_target="tpu_custom_call" | custom-call | tf_op jit(solution)/shard_map/split_kv/pallas_call | solution.py:58
  2.3 3.2 %collective-permute-start = (bf16[128,256]{1,0:T(8,128)(2,1)}, bf16[128,256]{1,0:T(8,128)(2,1)S(1)}, u32[]{:S(2)}, u32[]{:S(2)}) collective-permute-start(bf16[128,256]{1,0:T(8,128)(2,1)} %get-tuple-element.40), channel_id=1, source_target_pairs={{0,8},{8,0},{128,136},{136,128},{1,9},{9,1},{129,137},{137,129},{2... | collective-permute-start | bytes 196616 | tf_op jit(solution)/shard_map/ppermute | solution.py:203
  5.6 1.0 collective-permute-start.1
  6.6 2.1 %collective-permute-start.2 = (bf16[128,256]{1,0:T(8,128)(2,1)}, bf16[128,256]{1,0:T(8,128)(2,1)S(1)}, u32[]{:S(2)}, u32[]{:S(2)}) collective-permute-start(bf16[128,256]{1,0:T(8,128)(2,1)} %get-tuple-element.42), channel_id=1, source_target_pairs={{0,136},{8,128},{128,8},{136,0},{1,137},{9,129},{129,9},{137,1},{2... | collective-permute-start | bytes 196616 | tf_op jit(solution)/shard_map/ppermute | solution.py:203
  8.7 3.2 %split_heads.1 = bf16[32,128,256]{2,1,0:T(8,128)(2,1)} custom-call(bf16[128,4096]{1,0:T(8,128)(2,1)} %query_ref.1, bf16[128,4096]{1,0:T(8,128)(2,1)} %d_out_ref.1), custom_call_target="tpu_custom_call" | custom-call | tf_op jit(solution)/shard_map/split_heads/pallas_call | solution.py:80
  11.9 0.6 collective-permute-done.2
  12.5 5.8 %all-to-all-start = ((bf16[32,128,256]{2,1,0:T(8,128)(2,1)}), bf16[32,128,256]{2,1,0:T(8,128)(2,1)S(1)}, u32[]{:S(2)}, u32[]{:S(2)}) async-start(bf16[32,128,256]{2,1,0:T(8,128)(2,1)} %split_heads.1), calls=%async_computation | async-start | bytes 4194304 | tf_op jit(solution)/shard_map/all_to_all | solution.py:231
  18.4 1.7 %collective-permute-start.6 = (bf16[4,128,128]{2,1,0:T(8,128)(2,1)S(1)}, bf16[4,128,128]{2,1,0:T(8,128)(2,1)S(1)}, u32[]{:S(2)}, u32[]{:S(2)}) collective-permute-start(bf16[4,128,128]{2,1,0:T(8,128)(2,1)S(1)} %pad_maximum_fusion.refs_0_), channel_id=1, source_target_pairs={{0,16},{16,32},{32,48},{48,64},{64,80},{80,96},{96,112},{112,0},{1... | collective-permute-start | bytes 393224 | tf_op jit(solution)/shard_map/ppermute | solution.py:194
  20.2 4.0 %collective-permute-start.10 = (bf16[4,128,128]{2,1,0:T(8,128)(2,1)S(1)}, bf16[4,128,128]{2,1,0:T(8,128)(2,1)S(1)}, u32[]{:S(2)}, u32[]{:S(2)}) collective-permute-start(bf16[4,128,128]{2,1,0:T(8,128)(2,1)S(1)} %pad_maximum_fusion.1.refs_8_), channel_id=1, source_target_pairs={{0,112},{16,0},{32,16},{48,32},{64,48},{80,64},{96,80},{112,96},{1... | collective-permute-start | bytes 393224 | tf_op jit(solution)/shard_map/ppermute | solution.py:198
  24.2 1.4 %collective-permute-start.3 = (bf16[4,128,128]{2,1,0:T(8,128)(2,1)S(1)}, bf16[4,128,128]{2,1,0:T(8,128)(2,1)S(1)}, u32[]{:S(2)}, u32[]{:S(2)}) collective-permute-start(bf16[4,128,128]{2,1,0:T(8,128)(2,1)S(1)} %pad_maximum_fusion.refs_0_), channel_id=1, source_target_pairs={{0,112},{16,0},{32,16},{48,32},{64,48},{80,64},{96,80},{112,96},{1... | collective-permute-start | bytes 393224 | tf_op jit(solution)/shard_map/ppermute | solution.py:198
  25.7 2.1 %collective-permute-done.6.refs_7_ = bf16[4,128,128]{2,1,0:T(8,128)(2,1)S(1)} collective-permute-done((bf16[4,128,128]{2,1,0:T(8,128)(2,1)S(1)}, bf16[4,128,128]{2,1,0:T(8,128)(2,1)S(1)}, u32[]{:S(2)}, u32[]{:S(2)}) %collective-permute-start.6) | collective-permute-done | bytes 131104 | tf_op jit(solution)/shard_map/ppermute | solution.py:194
  27.8 2.7 %collective-permute-start.11 = (bf16[4,128,128]{2,1,0:T(8,128)(2,1)S(1)}, bf16[4,128,128]{2,1,0:T(8,128)(2,1)S(1)}, u32[]{:S(2)}, u32[]{:S(2)}) collective-permute-start(bf16[4,128,128]{2,1,0:T(8,128)(2,1)S(1)} %collective-permute-done.10.refs_9_), channel_id=1, source_target_pairs={{0,112},{16,0},{32,16},{48,32},{64,48},{80,64},{96,80},{112,96},{1... | collective-permute-start | bytes 393224 | tf_op jit(solution)/shard_map/ppermute | solution.py:198
  30.5 2.6 %collective-permute-start.4 = (bf16[4,128,128]{2,1,0:T(8,128)(2,1)S(1)}, bf16[4,128,128]{2,1,0:T(8,128)(2,1)S(1)}, u32[]{:S(2)}, u32[]{:S(2)}) collective-permute-start(bf16[4,128,128]{2,1,0:T(8,128)(2,1)S(1)} %collective-permute-done.3.refs_1_), channel_id=1, source_target_pairs={{0,112},{16,0},{32,16},{48,32},{64,48},{80,64},{96,80},{112,96},{1... | collective-permute-start | bytes 393224 | tf_op jit(solution)/shard_map/ppermute | solution.py:198
  33.1 1.4 %collective-permute-done.7.refs_6_ = bf16[4,128,128]{2,1,0:T(8,128)(2,1)S(1)} collective-permute-done((bf16[4,128,128]{2,1,0:T(8,128)(2,1)S(1)}, bf16[4,128,128]{2,1,0:T(8,128)(2,1)S(1)}, u32[]{:S(2)}, u32[]{:S(2)}) %collective-permute-start.7) | collective-permute-done | bytes 131104 | tf_op jit(solution)/shard_map/ppermute | solution.py:194
  34.5 2.7 %collective-permute-start.12 = (bf16[4,128,128]{2,1,0:T(8,128)(2,1)S(1)}, bf16[4,128,128]{2,1,0:T(8,128)(2,1)S(1)}, u32[]{:S(2)}, u32[]{:S(2)}) collective-permute-start(bf16[4,128,128]{2,1,0:T(8,128)(2,1)S(1)} %collective-permute-done.11.refs_10_), channel_id=1, source_target_pairs={{0,112},{16,0},{32,16},{48,32},{64,48},{80,64},{96,80},{112,96},{1... | collective-permute-start | bytes 393224 | tf_op jit(solution)/shard_map/ppermute | solution.py:198
  37.2 2.6 %collective-permute-start.5 = (bf16[4,128,128]{2,1,0:T(8,128)(2,1)S(1)}, bf16[4,128,128]{2,1,0:T(8,128)(2,1)S(1)}, u32[]{:S(2)}, u32[]{:S(2)}) collective-permute-start(bf16[4,128,128]{2,1,0:T(8,128)(2,1)S(1)} %collective-permute-done.4.refs_2_), channel_id=1, source_target_pairs={{0,112},{16,0},{32,16},{48,32},{64,48},{80,64},{96,80},{112,96},{1... | collective-permute-start | bytes 393224 | tf_op jit(solution)/shard_map/ppermute | solution.py:198
  39.8 1.0 collective-permute-done.8.refs_5_
  40.8 2.7 %collective-permute-start.13 = (bf16[4,128,128]{2,1,0:T(8,128)(2,1)S(1)}, bf16[4,128,128]{2,1,0:T(8,128)(2,1)}, u32[]{:S(2)}, u32[]{:S(2)}) collective-permute-start(bf16[4,128,128]{2,1,0:T(8,128)(2,1)S(1)} %collective-permute-done.12.refs_11_), channel_id=1, source_target_pairs={{0,112},{16,0},{32,16},{48,32},{64,48},{80,64},{96,80},{112,96},{1... | collective-permute-start | bytes 393224 | tf_op jit(solution)/shard_map/ppermute | solution.py:198
  43.5 1.6 %collective-permute-done.16.refs_13_ = bf16[4,128,128]{2,1,0:T(8,128)(2,1)S(1)} collective-permute-done((bf16[4,128,128]{2,1,0:T(8,128)(2,1)S(1)}, bf16[4,128,128]{2,1,0:T(8,128)(2,1)S(1)}, u32[]{:S(2)}, u32[]{:S(2)}) %collective-permute-start.16) | collective-permute-done | bytes 131104 | tf_op jit(solution)/shard_map/ppermute | solution.py:194
  45.1 1.8 %collective-permute-done.9.refs_4_ = bf16[4,128,128]{2,1,0:T(8,128)(2,1)S(1)} collective-permute-done((bf16[4,128,128]{2,1,0:T(8,128)(2,1)S(1)}, bf16[4,128,128]{2,1,0:T(8,128)(2,1)S(1)}, u32[]{:S(2)}, u32[]{:S(2)}) %collective-permute-start.9) | collective-permute-done | bytes 131104 | tf_op jit(solution)/shard_map/ppermute | solution.py:194
  47.0 0.6 copy-done.31
  47.7 1.2 copy-done
  48.9 22.4 %attention.1 = (bf16[32,128,256]{2,1,0:T(8,128)(2,1)}, bf16[4,128,128]{2,1,0:T(8,128)(2,1)}, bf16[4,128,128]{2,1,0:T(8,128)(2,1)}, bf16[4,128,128]{2,1,0:T(8,128...) custom-call(s32[256]{0:T(256)} %seg_ref.1, ...), custom_call_target="tpu_custom_call" | custom-call | flops 6442450944 | bytes 8388608 | tf_op jit(solution)/shard_map/attention/pallas_call | solution.py:176
  71.4 0.8 collective-permute-start.17
  72.2 10.7 %all-to-all-start.1 = ((bf16[32,128,256]{2,1,0:T(8,128)(2,1)}), bf16[32,128,256]{2,1,0:T(8,128)(2,1)S(1)}, u32[]{:S(2)}, u32[]{:S(2)}) async-start(bf16[32,128,256]{2,1,0:T(8,128)(2,1)} %get-tuple-element.48), calls=%async_computation.1 | async-start | bytes 4194304 | tf_op jit(solution)/shard_map/all_to_all | solution.py:231
  83.0 1.4 %collective-permute-start.21 = (bf16[4,128,128]{2,1,0:T(8,128)(2,1)S(1)}, bf16[4,128,128]{2,1,0:T(8,128)(2,1)S(1)}, u32[]{:S(2)}, u32[]{:S(2)}) collective-permute-start(bf16[4,128,128]{2,1,0:T(8,128)(2,1)S(1)} %copy-done.29), channel_id=1, source_target_pairs={{0,112},{16,0},{32,16},{48,32},{64,48},{80,64},{96,80},{112,96},{1... | collective-permute-start | bytes 393224 | tf_op jit(solution)/shard_map/ppermute | solution.py:198
  84.4 0.5 collective-permute-start.24
  84.9 2.2 %collective-permute-start.27 = (bf16[4,128,128]{2,1,0:T(8,128)(2,1)S(1)}, bf16[4,128,128]{2,1,0:T(8,128)(2,1)S(1)}, u32[]{:S(2)}, u32[]{:S(2)}) collective-permute-start(bf16[4,128,128]{2,1,0:T(8,128)(2,1)S(1)} %copy-done.24), channel_id=1, source_target_pairs={{0,112},{16,0},{32,16},{48,32},{64,48},{80,64},{96,80},{112,96},{1... | collective-permute-start | bytes 393224 | tf_op jit(solution)/shard_map/ppermute | solution.py:198
  87.1 0.1 collective-permute-start.18
  87.2 1.3 %collective-permute-done.21 = bf16[4,128,128]{2,1,0:T(8,128)(2,1)S(1)} collective-permute-done((bf16[4,128,128]{2,1,0:T(8,128)(2,1)S(1)}, bf16[4,128,128]{2,1,0:T(8,128)(2,1)S(1)}, u32[]{:S(2)}, u32[]{:S(2)}) %collective-permute-start.21) | collective-permute-done | bytes 131104 | tf_op jit(solution)/shard_map/ppermute | solution.py:198
  88.6 2.2 %collective-permute-start.22 = (bf16[4,128,128]{2,1,0:T(8,128)(2,1)S(1)}, bf16[4,128,128]{2,1,0:T(8,128)(2,1)S(1)}, u32[]{:S(2)}, u32[]{:S(2)}) collective-permute-start(bf16[4,128,128]{2,1,0:T(8,128)(2,1)S(1)} %add_convert_fusion.6), channel_id=1, source_target_pairs={{0,112},{16,0},{32,16},{48,32},{64,48},{80,64},{96,80},{112,96},{1... | collective-permute-start | bytes 393224 | tf_op jit(solution)/shard_map/ppermute | solution.py:198
  90.9 0.4 collective-permute-done.27
  91.4 2.4 %collective-permute-start.28 = (bf16[4,128,128]{2,1,0:T(8,128)(2,1)S(1)}, bf16[4,128,128]{2,1,0:T(8,128)(2,1)S(1)}, u32[]{:S(2)}, u32[]{:S(2)}) collective-permute-start(bf16[4,128,128]{2,1,0:T(8,128)(2,1)S(1)} %add_convert_fusion.2), channel_id=1, source_target_pairs={{0,112},{16,0},{32,16},{48,32},{64,48},{80,64},{96,80},{112,96},{1... | collective-permute-start | bytes 393224 | tf_op jit(solution)/shard_map/ppermute | solution.py:198
  93.8 0.1 collective-permute-start.19
  93.9 2.7 %collective-permute-start.23 = (bf16[4,128,128]{2,1,0:T(8,128)(2,1)S(1)}, bf16[4,128,128]{2,1,0:T(8,128)(2,1)S(1)}, u32[]{:S(2)}, u32[]{:S(2)}) collective-permute-start(bf16[4,128,128]{2,1,0:T(8,128)(2,1)S(1)} %add_convert_fusion.5), channel_id=1, source_target_pairs={{0,112},{16,0},{32,16},{48,32},{64,48},{80,64},{96,80},{112,96},{1... | collective-permute-start | bytes 393224 | tf_op jit(solution)/shard_map/ppermute | solution.py:198
  96.7 0.1 collective-permute-start.26
  96.9 2.7 %collective-permute-start.29 = (bf16[4,128,128]{2,1,0:T(8,128)(2,1)S(1)}, bf16[4,128,128]{2,1,0:T(8,128)(2,1)S(1)}, u32[]{:S(2)}, u32[]{:S(2)}) collective-permute-start(bf16[4,128,128]{2,1,0:T(8,128)(2,1)S(1)} %add_convert_fusion.1), channel_id=1, source_target_pairs={{0,112},{16,0},{32,16},{48,32},{64,48},{80,64},{96,80},{112,96},{1... | collective-permute-start | bytes 393224 | tf_op jit(solution)/shard_map/ppermute | solution.py:198
  99.7 2.9 %collective-permute-done.29 = bf16[4,128,128]{2,1,0:T(8,128)(2,1)S(1)} collective-permute-done((bf16[4,128,128]{2,1,0:T(8,128)(2,1)S(1)}, bf16[4,128,128]{2,1,0:T(8,128)(2,1)S(1)}, u32[]{:S(2)}, u32[]{:S(2)}) %collective-permute-start.29) | collective-permute-done | bytes 131104 | tf_op jit(solution)/shard_map/ppermute | solution.py:198
  102.7 3.5 %collective-permute-start.30 = (bf16[4,128,128]{2,1,0:T(8,128)(2,1)S(1)}, bf16[4,128,128]{2,1,0:T(8,128)(2,1)S(1)}, u32[]{:S(2)}, u32[]{:S(2)}) collective-permute-start(bf16[4,128,128]{2,1,0:T(8,128)(2,1)S(1)} %add_convert_fusion), channel_id=1, source_target_pairs={{0,112},{16,0},{32,16},{48,32},{64,48},{80,64},{96,80},{112,96},{1... | collective-permute-start | bytes 393224 | tf_op jit(solution)/shard_map/ppermute | solution.py:198
  106.2 0.2 collective-permute-done.20
  106.5 1.7 %collective-permute-done.30 = bf16[4,128,128]{2,1,0:T(8,128)(2,1)S(1)} collective-permute-done((bf16[4,128,128]{2,1,0:T(8,128)(2,1)S(1)}, bf16[4,128,128]{2,1,0:T(8,128)(2,1)S(1)}, u32[]{:S(2)}, u32[]{:S(2)}) %collective-permute-start.30) | collective-permute-done | bytes 131104 | tf_op jit(solution)/shard_map/ppermute | solution.py:198
  108.3 3.0 %all-to-all-done.1.tiles = bf16[32,128,256]{2,1,0:T(8,128)(2,1)S(1)} async-done(((bf16[32,128,256]{2,1,0:T(8,128)(2,1)}), bf16[32,128,256]{2,1,0:T(8,128)(2,1)S(1)}, u32[]{:S(2)}, u32[]{:S(2)}) %all-to-all-start.1) | async-done | bytes 2097184 | tf_op jit(solution)/shard_map/all_to_all | solution.py:231
  111.3 0.4 collective-permute-start.31
  111.7 3.0 %collective-permute-start.32 = (bf16[128,256]{1,0:T(8,128)(2,1)S(1)}, bf16[128,256]{1,0:T(8,128)(2,1)S(1)}, u32[]{:S(2)}, u32[]{:S(2)}) collective-permute-start(bf16[128,256]{1,0:T(8,128)(2,1)S(1)} %pad_maximum_fusion.4), channel_id=1, source_target_pairs={{0,128},{8,136},{128,0},{136,8},{1,129},{9,137},{129,1},{137,9},{2... | collective-permute-start | bytes 196616 | tf_op jit(solution)/shard_map/ppermute | solution.py:203
  114.7 0.2 collective-permute-start.33
  114.9 1.9 %join_heads.1 = (bf16[128,4096]{1,0:T(8,128)(2,1)}, bf16[128,4096]{1,0:T(8,128)(2,1)}) custom-call(bf16[32,128,256]{2,1,0:T(8,128)(2,1)S(1)} %all-to-all-done.1.tiles), custom_call_target="tpu_custom_call" | custom-call | tf_op jit(solution)/shard_map/join_heads/pallas_call | solution.py:91
  116.9 3.4 %collective-permute-done.33.refs_3_ = bf16[128,256]{1,0:T(8,128)(2,1)S(1)} collective-permute-done((bf16[128,256]{1,0:T(8,128)(2,1)S(1)}, bf16[128,256]{1,0:T(8,128)(2,1)S(1)}, u32[]{:S(2)}, u32[]{:S(2)}) %collective-permute-start.33) | collective-permute-done | bytes 65568 | tf_op jit(solution)/shard_map/ppermute | solution.py:203
  120.3 0.7 join_kv.1
  (113 shorter events, 1.1 us)
Async XLA Ops:
  2.3 9.6 %collective-permute-start = (bf16[128,256]{1,0:T(8,128)(2,1)}, bf16[128,256]{1,0:T(8,128)(2,1)S(1)}, u32[]{:S(2)}, u32[]{:S(2)}) collective-permute-start(bf16[128,256]{1,0:T(8,128)(2,1)} %get-tuple-element.40), channel_id=1, source_target_pairs={{0,8},{8,0},{128,136},{136,128},{1,9},{9,1},{129,137},{137,129},{2... | collective-permute-start | bytes 196616 | tf_op jit(solution)/shard_map/ppermute | solution.py:203
  5.6 6.4 %collective-permute-start.1 = (bf16[128,256]{1,0:T(8,128)(2,1)}, bf16[128,256]{1,0:T(8,128)(2,1)S(1)}, u32[]{:S(2)}, u32[]{:S(2)}) collective-permute-start(bf16[128,256]{1,0:T(8,128)(2,1)} %get-tuple-element.41), channel_id=1, source_target_pairs={{0,128},{8,136},{128,0},{136,8},{1,129},{9,137},{129,1},{137,9},{2... | collective-permute-start | bytes 196616 | tf_op jit(solution)/shard_map/ppermute | solution.py:203
  6.6 5.9 %collective-permute-start.2 = (bf16[128,256]{1,0:T(8,128)(2,1)}, bf16[128,256]{1,0:T(8,128)(2,1)S(1)}, u32[]{:S(2)}, u32[]{:S(2)}) collective-permute-start(bf16[128,256]{1,0:T(8,128)(2,1)} %get-tuple-element.42), channel_id=1, source_target_pairs={{0,136},{8,128},{128,8},{136,0},{1,137},{9,129},{129,9},{137,1},{2... | collective-permute-start | bytes 196616 | tf_op jit(solution)/shard_map/ppermute | solution.py:203
  12.5 35.1 %all-to-all-start = ((bf16[32,128,256]{2,1,0:T(8,128)(2,1)}), bf16[32,128,256]{2,1,0:T(8,128)(2,1)S(1)}, u32[]{:S(2)}, u32[]{:S(2)}) async-start(bf16[32,128,256]{2,1,0:T(8,128)(2,1)} %split_heads.1), calls=%async_computation | async-start | bytes 4194304 | tf_op jit(solution)/shard_map/all_to_all | solution.py:231
  18.4 29.2 %copy-start.11 = (bf16[4,128,128]{2,1,0:T(8,128)(2,1)}, bf16[4,128,128]{2,1,0:T(8,128)(2,1)S(1)}, u32[]{:S(2)}) copy-start(bf16[4,128,128]{2,1,0:T(8,128)(2,1)S(1)} %pad_maximum_fusion.refs_0_) | copy-start | bytes 393220
  18.4 9.4 %collective-permute-start.6 = (bf16[4,128,128]{2,1,0:T(8,128)(2,1)S(1)}, bf16[4,128,128]{2,1,0:T(8,128)(2,1)S(1)}, u32[]{:S(2)}, u32[]{:S(2)}) collective-permute-start(bf16[4,128,128]{2,1,0:T(8,128)(2,1)S(1)} %pad_maximum_fusion.refs_0_), channel_id=1, source_target_pairs={{0,16},{16,32},{32,48},{48,64},{64,80},{80,96},{96,112},{112,0},{1... | collective-permute-start | bytes 393224 | tf_op jit(solution)/shard_map/ppermute | solution.py:194
  20.2 27.5 %copy-start.12 = (bf16[4,128,128]{2,1,0:T(8,128)(2,1)}, bf16[4,128,128]{2,1,0:T(8,128)(2,1)S(1)}, u32[]{:S(2)}) copy-start(bf16[4,128,128]{2,1,0:T(8,128)(2,1)S(1)} %pad_maximum_fusion.1.refs_8_) | copy-start | bytes 393220
  20.2 7.6 %collective-permute-start.10 = (bf16[4,128,128]{2,1,0:T(8,128)(2,1)S(1)}, bf16[4,128,128]{2,1,0:T(8,128)(2,1)S(1)}, u32[]{:S(2)}, u32[]{:S(2)}) collective-permute-start(bf16[4,128,128]{2,1,0:T(8,128)(2,1)S(1)} %pad_maximum_fusion.1.refs_8_), channel_id=1, source_target_pairs={{0,112},{16,0},{32,16},{48,32},{64,48},{80,64},{96,80},{112,96},{1... | collective-permute-start | bytes 393224 | tf_op jit(solution)/shard_map/ppermute | solution.py:198
  24.2 6.3 %collective-permute-start.3 = (bf16[4,128,128]{2,1,0:T(8,128)(2,1)S(1)}, bf16[4,128,128]{2,1,0:T(8,128)(2,1)S(1)}, u32[]{:S(2)}, u32[]{:S(2)}) collective-permute-start(bf16[4,128,128]{2,1,0:T(8,128)(2,1)S(1)} %pad_maximum_fusion.refs_0_), channel_id=1, source_target_pairs={{0,112},{16,0},{32,16},{48,32},{64,48},{80,64},{96,80},{112,96},{1... | collective-permute-start | bytes 393224 | tf_op jit(solution)/shard_map/ppermute | solution.py:198
  25.7 7.4 %collective-permute-start.14 = (bf16[4,128,128]{2,1,0:T(8,128)(2,1)S(1)}, bf16[4,128,128]{2,1,0:T(8,128)(2,1)S(1)}, u32[]{:S(2)}, u32[]{:S(2)}) collective-permute-start(bf16[4,128,128]{2,1,0:T(8,128)(2,1)S(1)} %pad_maximum_fusion.1.refs_8_), channel_id=1, source_target_pairs={{0,16},{16,32},{32,48},{48,64},{64,80},{80,96},{96,112},{112,0},{1... | collective-permute-start | bytes 393224 | tf_op jit(solution)/shard_map/ppermute | solution.py:194
  27.8 19.8 %copy-start.16 = (bf16[4,128,128]{2,1,0:T(8,128)(2,1)}, bf16[4,128,128]{2,1,0:T(8,128)(2,1)S(1)}, u32[]{:S(2)}) copy-start(bf16[4,128,128]{2,1,0:T(8,128)(2,1)S(1)} %collective-permute-done.6.refs_7_) | copy-start | bytes 393220
  27.8 6.7 %collective-permute-start.7 = (bf16[4,128,128]{2,1,0:T(8,128)(2,1)S(1)}, bf16[4,128,128]{2,1,0:T(8,128)(2,1)S(1)}, u32[]{:S(2)}, u32[]{:S(2)}) collective-permute-start(bf16[4,128,128]{2,1,0:T(8,128)(2,1)S(1)} %collective-permute-done.6.refs_7_), channel_id=1, source_target_pairs={{0,16},{16,32},{32,48},{48,64},{64,80},{80,96},{96,112},{112,0},{1... | collective-permute-start | bytes 393224 | tf_op jit(solution)/shard_map/ppermute | solution.py:194
  27.8 19.8 %copy-start.17 = (bf16[4,128,128]{2,1,0:T(8,128)(2,1)}, bf16[4,128,128]{2,1,0:T(8,128)(2,1)S(1)}, u32[]{:S(2)}) copy-start(bf16[4,128,128]{2,1,0:T(8,128)(2,1)S(1)} %collective-permute-done.10.refs_9_) | copy-start | bytes 393220
  27.8 6.7 %collective-permute-start.11 = (bf16[4,128,128]{2,1,0:T(8,128)(2,1)S(1)}, bf16[4,128,128]{2,1,0:T(8,128)(2,1)S(1)}, u32[]{:S(2)}, u32[]{:S(2)}) collective-permute-start(bf16[4,128,128]{2,1,0:T(8,128)(2,1)S(1)} %collective-permute-done.10.refs_9_), channel_id=1, source_target_pairs={{0,112},{16,0},{32,16},{48,32},{64,48},{80,64},{96,80},{112,96},{1... | collective-permute-start | bytes 393224 | tf_op jit(solution)/shard_map/ppermute | solution.py:198
  30.5 17.2 %copy-start.18 = (bf16[4,128,128]{2,1,0:T(8,128)(2,1)}, bf16[4,128,128]{2,1,0:T(8,128)(2,1)S(1)}, u32[]{:S(2)}) copy-start(bf16[4,128,128]{2,1,0:T(8,128)(2,1)S(1)} %collective-permute-done.3.refs_1_) | copy-start | bytes 393220
  30.5 6.7 %collective-permute-start.4 = (bf16[4,128,128]{2,1,0:T(8,128)(2,1)S(1)}, bf16[4,128,128]{2,1,0:T(8,128)(2,1)S(1)}, u32[]{:S(2)}, u32[]{:S(2)}) collective-permute-start(bf16[4,128,128]{2,1,0:T(8,128)(2,1)S(1)} %collective-permute-done.3.refs_1_), channel_id=1, source_target_pairs={{0,112},{16,0},{32,16},{48,32},{64,48},{80,64},{96,80},{112,96},{1... | collective-permute-start | bytes 393224 | tf_op jit(solution)/shard_map/ppermute | solution.py:198
  33.1 6.7 %collective-permute-start.15 = (bf16[4,128,128]{2,1,0:T(8,128)(2,1)S(1)}, bf16[4,128,128]{2,1,0:T(8,128)(2,1)S(1)}, u32[]{:S(2)}, u32[]{:S(2)}) collective-permute-start(bf16[4,128,128]{2,1,0:T(8,128)(2,1)S(1)} %collective-permute-done.14.refs_15_), channel_id=1, source_target_pairs={{0,16},{16,32},{32,48},{48,64},{64,80},{80,96},{96,112},{112,0},{1... | collective-permute-start | bytes 393224 | tf_op jit(solution)/shard_map/ppermute | solution.py:194
  34.5 6.3 %collective-permute-start.8 = (bf16[4,128,128]{2,1,0:T(8,128)(2,1)S(1)}, bf16[4,128,128]{2,1,0:T(8,128)(2,1)S(1)}, u32[]{:S(2)}, u32[]{:S(2)}) collective-permute-start(bf16[4,128,128]{2,1,0:T(8,128)(2,1)S(1)} %collective-permute-done.7.refs_6_), channel_id=1, source_target_pairs={{0,16},{16,32},{32,48},{48,64},{64,80},{80,96},{96,112},{112,0},{1... | collective-permute-start | bytes 393224 | tf_op jit(solution)/shard_map/ppermute | solution.py:194
  34.5 6.3 %collective-permute-start.12 = (bf16[4,128,128]{2,1,0:T(8,128)(2,1)S(1)}, bf16[4,128,128]{2,1,0:T(8,128)(2,1)S(1)}, u32[]{:S(2)}, u32[]{:S(2)}) collective-permute-start(bf16[4,128,128]{2,1,0:T(8,128)(2,1)S(1)} %collective-permute-done.11.refs_10_), channel_id=1, source_target_pairs={{0,112},{16,0},{32,16},{48,32},{64,48},{80,64},{96,80},{112,96},{1... | collective-permute-start | bytes 393224 | tf_op jit(solution)/shard_map/ppermute | solution.py:198
  37.2 6.3 %collective-permute-start.5 = (bf16[4,128,128]{2,1,0:T(8,128)(2,1)S(1)}, bf16[4,128,128]{2,1,0:T(8,128)(2,1)S(1)}, u32[]{:S(2)}, u32[]{:S(2)}) collective-permute-start(bf16[4,128,128]{2,1,0:T(8,128)(2,1)S(1)} %collective-permute-done.4.refs_2_), channel_id=1, source_target_pairs={{0,112},{16,0},{32,16},{48,32},{64,48},{80,64},{96,80},{112,96},{1... | collective-permute-start | bytes 393224 | tf_op jit(solution)/shard_map/ppermute | solution.py:198
  39.8 5.3 %collective-permute-start.16 = (bf16[4,128,128]{2,1,0:T(8,128)(2,1)S(1)}, bf16[4,128,128]{2,1,0:T(8,128)(2,1)S(1)}, u32[]{:S(2)}, u32[]{:S(2)}) collective-permute-start(bf16[4,128,128]{2,1,0:T(8,128)(2,1)S(1)} %collective-permute-done.15.refs_14_), channel_id=1, source_target_pairs={{0,16},{16,32},{32,48},{48,64},{64,80},{80,96},{96,112},{112,0},{1... | collective-permute-start | bytes 393224 | tf_op jit(solution)/shard_map/ppermute | solution.py:194
  40.8 6.2 %collective-permute-start.9 = (bf16[4,128,128]{2,1,0:T(8,128)(2,1)S(1)}, bf16[4,128,128]{2,1,0:T(8,128)(2,1)S(1)}, u32[]{:S(2)}, u32[]{:S(2)}) collective-permute-start(bf16[4,128,128]{2,1,0:T(8,128)(2,1)S(1)} %collective-permute-done.8.refs_5_), channel_id=1, source_target_pairs={{0,16},{16,32},{32,48},{48,64},{64,80},{80,96},{96,112},{112,0},{1... | collective-permute-start | bytes 393224 | tf_op jit(solution)/shard_map/ppermute | solution.py:194
  40.8 6.8 %collective-permute-start.13 = (bf16[4,128,128]{2,1,0:T(8,128)(2,1)S(1)}, bf16[4,128,128]{2,1,0:T(8,128)(2,1)}, u32[]{:S(2)}, u32[]{:S(2)}) collective-permute-start(bf16[4,128,128]{2,1,0:T(8,128)(2,1)S(1)} %collective-permute-done.12.refs_11_), channel_id=1, source_target_pairs={{0,112},{16,0},{32,16},{48,32},{64,48},{80,64},{96,80},{112,96},{1... | collective-permute-start | bytes 393224 | tf_op jit(solution)/shard_map/ppermute | solution.py:198
  71.4 15.7 %collective-permute-start.17 = (bf16[4,128,128]{2,1,0:T(8,128)(2,1)}, bf16[4,128,128]{2,1,0:T(8,128)(2,1)S(1)}, u32[]{:S(2)}, u32[]{:S(2)}) collective-permute-start(bf16[4,128,128]{2,1,0:T(8,128)(2,1)} %get-tuple-element.53), channel_id=1, source_target_pairs={{0,16},{16,32},{32,48},{48,64},{64,80},{80,96},{96,112},{112,0},{1... | collective-permute-start | bytes 393224 | tf_op jit(solution)/shard_map/ppermute | solution.py:194
  72.2 18.6 %copy-start.8 = (bf16[4,128,128]{2,1,0:T(8,128)(2,1)S(1)}, bf16[4,128,128]{2,1,0:T(8,128)(2,1)}, u32[]{:S(2)}) copy-start(bf16[4,128,128]{2,1,0:T(8,128)(2,1)} %get-tuple-element.59) | copy-start | bytes 393220
  72.2 19.1 %copy-start.7 = (bf16[4,128,128]{2,1,0:T(8,128)(2,1)S(1)}, bf16[4,128,128]{2,1,0:T(8,128)(2,1)}, u32[]{:S(2)}) copy-start(bf16[4,128,128]{2,1,0:T(8,128)(2,1)} %get-tuple-element.63) | copy-start | bytes 393220
  72.2 21.5 %copy-start.6 = (bf16[4,128,128]{2,1,0:T(8,128)(2,1)S(1)}, bf16[4,128,128]{2,1,0:T(8,128)(2,1)}, u32[]{:S(2)}) copy-start(bf16[4,128,128]{2,1,0:T(8,128)(2,1)} %get-tuple-element.51) | copy-start | bytes 393220
  72.2 21.7 %copy-start.5 = (bf16[4,128,128]{2,1,0:T(8,128)(2,1)S(1)}, bf16[4,128,128]{2,1,0:T(8,128)(2,1)}, u32[]{:S(2)}) copy-start(bf16[4,128,128]{2,1,0:T(8,128)(2,1)} %get-tuple-element.54) | copy-start | bytes 393220
  72.2 39.1 %all-to-all-start.1 = ((bf16[32,128,256]{2,1,0:T(8,128)(2,1)}), bf16[32,128,256]{2,1,0:T(8,128)(2,1)S(1)}, u32[]{:S(2)}, u32[]{:S(2)}) async-start(bf16[32,128,256]{2,1,0:T(8,128)(2,1)} %get-tuple-element.48), calls=%async_computation.1 | async-start | bytes 4194304 | tf_op jit(solution)/shard_map/all_to_all | solution.py:231
  82.9 19.7 %copy-start.1 = (bf16[4,128,128]{2,1,0:T(8,128)(2,1)S(1)}, bf16[4,128,128]{2,1,0:T(8,128)(2,1)}, u32[]{:S(2)}) copy-start(bf16[4,128,128]{2,1,0:T(8,128)(2,1)} %get-tuple-element.61) | copy-start | bytes 393220
  82.9 23.4 %copy-start.14 = (bf16[4,128,128]{2,1,0:T(8,128)(2,1)S(1)}, bf16[4,128,128]{2,1,0:T(8,128)(2,1)}, u32[]{:S(2)}) copy-start(bf16[4,128,128]{2,1,0:T(8,128)(2,1)} %get-tuple-element.49) | copy-start | bytes 393220
  83.0 5.5 %collective-permute-start.21 = (bf16[4,128,128]{2,1,0:T(8,128)(2,1)S(1)}, bf16[4,128,128]{2,1,0:T(8,128)(2,1)S(1)}, u32[]{:S(2)}, u32[]{:S(2)}) collective-permute-start(bf16[4,128,128]{2,1,0:T(8,128)(2,1)S(1)} %copy-done.29), channel_id=1, source_target_pairs={{0,112},{16,0},{32,16},{48,32},{64,48},{80,64},{96,80},{112,96},{1... | collective-permute-start | bytes 393224 | tf_op jit(solution)/shard_map/ppermute | solution.py:198
  84.4 6.4 %collective-permute-start.24 = (bf16[4,128,128]{2,1,0:T(8,128)(2,1)S(1)}, bf16[4,128,128]{2,1,0:T(8,128)(2,1)S(1)}, u32[]{:S(2)}, u32[]{:S(2)}) collective-permute-start(bf16[4,128,128]{2,1,0:T(8,128)(2,1)S(1)} %copy-done.27), channel_id=1, source_target_pairs={{0,16},{16,32},{32,48},{48,64},{64,80},{80,96},{96,112},{112,0},{1... | collective-permute-start | bytes 393224 | tf_op jit(solution)/shard_map/ppermute | solution.py:194
  84.9 6.4 %collective-permute-start.27 = (bf16[4,128,128]{2,1,0:T(8,128)(2,1)S(1)}, bf16[4,128,128]{2,1,0:T(8,128)(2,1)S(1)}, u32[]{:S(2)}, u32[]{:S(2)}) collective-permute-start(bf16[4,128,128]{2,1,0:T(8,128)(2,1)S(1)} %copy-done.24), channel_id=1, source_target_pairs={{0,112},{16,0},{32,16},{48,32},{64,48},{80,64},{96,80},{112,96},{1... | collective-permute-start | bytes 393224 | tf_op jit(solution)/shard_map/ppermute | solution.py:198
  87.1 21.0 %copy-start.13 = (bf16[4,128,128]{2,1,0:T(8,128)(2,1)S(1)}, bf16[4,128,128]{2,1,0:T(8,128)(2,1)}, u32[]{:S(2)}) copy-start(bf16[4,128,128]{2,1,0:T(8,128)(2,1)} %get-tuple-element.57) | copy-start | bytes 393220
  87.1 6.6 %collective-permute-start.18 = (bf16[4,128,128]{2,1,0:T(8,128)(2,1)S(1)}, bf16[4,128,128]{2,1,0:T(8,128)(2,1)S(1)}, u32[]{:S(2)}, u32[]{:S(2)}) collective-permute-start(bf16[4,128,128]{2,1,0:T(8,128)(2,1)S(1)} %add_convert_fusion.9), channel_id=1, source_target_pairs={{0,16},{16,32},{32,48},{48,64},{64,80},{80,96},{96,112},{112,0},{1... | collective-permute-start | bytes 393224 | tf_op jit(solution)/shard_map/ppermute | solution.py:194
  88.6 5.3 %collective-permute-start.22 = (bf16[4,128,128]{2,1,0:T(8,128)(2,1)S(1)}, bf16[4,128,128]{2,1,0:T(8,128)(2,1)S(1)}, u32[]{:S(2)}, u32[]{:S(2)}) collective-permute-start(bf16[4,128,128]{2,1,0:T(8,128)(2,1)S(1)} %add_convert_fusion.6), channel_id=1, source_target_pairs={{0,112},{16,0},{32,16},{48,32},{64,48},{80,64},{96,80},{112,96},{1... | collective-permute-start | bytes 393224 | tf_op jit(solution)/shard_map/ppermute | solution.py:198
  90.8 5.8 %collective-permute-start.25 = (bf16[4,128,128]{2,1,0:T(8,128)(2,1)S(1)}, bf16[4,128,128]{2,1,0:T(8,128)(2,1)S(1)}, u32[]{:S(2)}, u32[]{:S(2)}) collective-permute-start(bf16[4,128,128]{2,1,0:T(8,128)(2,1)S(1)} %add_convert_fusion.4), channel_id=1, source_target_pairs={{0,16},{16,32},{32,48},{48,64},{64,80},{80,96},{96,112},{112,0},{1... | collective-permute-start | bytes 393224 | tf_op jit(solution)/shard_map/ppermute | solution.py:194
  91.4 5.4 %collective-permute-start.28 = (bf16[4,128,128]{2,1,0:T(8,128)(2,1)S(1)}, bf16[4,128,128]{2,1,0:T(8,128)(2,1)S(1)}, u32[]{:S(2)}, u32[]{:S(2)}) collective-permute-start(bf16[4,128,128]{2,1,0:T(8,128)(2,1)S(1)} %add_convert_fusion.2), channel_id=1, source_target_pairs={{0,112},{16,0},{32,16},{48,32},{64,48},{80,64},{96,80},{112,96},{1... | collective-permute-start | bytes 393224 | tf_op jit(solution)/shard_map/ppermute | solution.py:198
  93.8 5.8 %collective-permute-start.19 = (bf16[4,128,128]{2,1,0:T(8,128)(2,1)S(1)}, bf16[4,128,128]{2,1,0:T(8,128)(2,1)S(1)}, u32[]{:S(2)}, u32[]{:S(2)}) collective-permute-start(bf16[4,128,128]{2,1,0:T(8,128)(2,1)S(1)} %add_convert_fusion.8), channel_id=1, source_target_pairs={{0,16},{16,32},{32,48},{48,64},{64,80},{80,96},{96,112},{112,0},{1... | collective-permute-start | bytes 393224 | tf_op jit(solution)/shard_map/ppermute | solution.py:194
  93.9 12.3 %collective-permute-start.23 = (bf16[4,128,128]{2,1,0:T(8,128)(2,1)S(1)}, bf16[4,128,128]{2,1,0:T(8,128)(2,1)S(1)}, u32[]{:S(2)}, u32[]{:S(2)}) collective-permute-start(bf16[4,128,128]{2,1,0:T(8,128)(2,1)S(1)} %add_convert_fusion.5), channel_id=1, source_target_pairs={{0,112},{16,0},{32,16},{48,32},{64,48},{80,64},{96,80},{112,96},{1... | collective-permute-start | bytes 393224 | tf_op jit(solution)/shard_map/ppermute | solution.py:198
  96.7 9.8 %collective-permute-start.26 = (bf16[4,128,128]{2,1,0:T(8,128)(2,1)S(1)}, bf16[4,128,128]{2,1,0:T(8,128)(2,1)S(1)}, u32[]{:S(2)}, u32[]{:S(2)}) collective-permute-start(bf16[4,128,128]{2,1,0:T(8,128)(2,1)S(1)} %add_convert_fusion.3), channel_id=1, source_target_pairs={{0,16},{16,32},{32,48},{48,64},{64,80},{80,96},{96,112},{112,0},{1... | collective-permute-start | bytes 393224 | tf_op jit(solution)/shard_map/ppermute | solution.py:194
  96.9 5.8 %collective-permute-start.29 = (bf16[4,128,128]{2,1,0:T(8,128)(2,1)S(1)}, bf16[4,128,128]{2,1,0:T(8,128)(2,1)S(1)}, u32[]{:S(2)}, u32[]{:S(2)}) collective-permute-start(bf16[4,128,128]{2,1,0:T(8,128)(2,1)S(1)} %add_convert_fusion.1), channel_id=1, source_target_pairs={{0,112},{16,0},{32,16},{48,32},{64,48},{80,64},{96,80},{112,96},{1... | collective-permute-start | bytes 393224 | tf_op jit(solution)/shard_map/ppermute | solution.py:198
  99.6 6.8 %collective-permute-start.20 = (bf16[4,128,128]{2,1,0:T(8,128)(2,1)S(1)}, bf16[4,128,128]{2,1,0:T(8,128)(2,1)S(1)}, u32[]{:S(2)}, u32[]{:S(2)}) collective-permute-start(bf16[4,128,128]{2,1,0:T(8,128)(2,1)S(1)} %add_convert_fusion.7), channel_id=1, source_target_pairs={{0,16},{16,32},{32,48},{48,64},{64,80},{80,96},{96,112},{112,0},{1... | collective-permute-start | bytes 393224 | tf_op jit(solution)/shard_map/ppermute | solution.py:194
  102.7 5.4 %collective-permute-start.30 = (bf16[4,128,128]{2,1,0:T(8,128)(2,1)S(1)}, bf16[4,128,128]{2,1,0:T(8,128)(2,1)S(1)}, u32[]{:S(2)}, u32[]{:S(2)}) collective-permute-start(bf16[4,128,128]{2,1,0:T(8,128)(2,1)S(1)} %add_convert_fusion), channel_id=1, source_target_pairs={{0,112},{16,0},{32,16},{48,32},{64,48},{80,64},{96,80},{112,96},{1... | collective-permute-start | bytes 393224 | tf_op jit(solution)/shard_map/ppermute | solution.py:198
  111.3 5.6 %collective-permute-start.31 = (bf16[128,256]{1,0:T(8,128)(2,1)S(1)}, bf16[128,256]{1,0:T(8,128)(2,1)S(1)}, u32[]{:S(2)}, u32[]{:S(2)}) collective-permute-start(bf16[128,256]{1,0:T(8,128)(2,1)S(1)} %pad_maximum_fusion.3), channel_id=1, source_target_pairs={{0,8},{8,0},{128,136},{136,128},{1,9},{9,1},{129,137},{137,129},{2... | collective-permute-start | bytes 196616 | tf_op jit(solution)/shard_map/ppermute | solution.py:203
  111.7 5.2 %collective-permute-start.32 = (bf16[128,256]{1,0:T(8,128)(2,1)S(1)}, bf16[128,256]{1,0:T(8,128)(2,1)S(1)}, u32[]{:S(2)}, u32[]{:S(2)}) collective-permute-start(bf16[128,256]{1,0:T(8,128)(2,1)S(1)} %pad_maximum_fusion.4), channel_id=1, source_target_pairs={{0,128},{8,136},{128,0},{136,8},{1,129},{9,137},{129,1},{137,9},{2... | collective-permute-start | bytes 196616 | tf_op jit(solution)/shard_map/ppermute | solution.py:203
  114.7 5.6 %collective-permute-start.33 = (bf16[128,256]{1,0:T(8,128)(2,1)S(1)}, bf16[128,256]{1,0:T(8,128)(2,1)S(1)}, u32[]{:S(2)}, u32[]{:S(2)}) collective-permute-start(bf16[128,256]{1,0:T(8,128)(2,1)S(1)} %pad_maximum_fusion.5), channel_id=1, source_target_pairs={{0,136},{8,128},{128,8},{136,0},{1,137},{9,129},{129,9},{137,1},{2... | collective-permute-start | bytes 196616 | tf_op jit(solution)/shard_map/ppermute | solution.py:203
  (20 other events, 196.9 us)
